TPU v7x, 32 devices: a whole 2x2x4 slice. The times are simulated.
32 devices in a mesh: dp: 8 (over z, y), tensor: 4 (over x, core).
Axes of the slice: x: 2, y: 2, z: 4, core: 2. Of those that a mesh axis runs over, the one named last changes fastest.
Arguments:
- tokens: bfloat16 [1024, 768], P(('dp', 'tensor')), may hold values from -6 to 6
- cotangent: bfloat16 [1024, 768], P(('dp', 'tensor')), may hold values from -6 to 6
- segments: int32 [1024], replicated, may hold values from 0 to 4, never falling along the last dimension, each value on 1 to 384 neighbouring positions
- w_qkv: bfloat16 [2, 768, 3, 768], P(None, None, None, 'tensor'), may hold values from -0.21875 to 0.21875
- qv_bias: float32 [2, 2, 768], P(None, None, 'tensor'), may hold values from -3 to 3
- w_out: bfloat16 [2, 768, 768], P(None, 'tensor'), may hold values from -0.875 to 0.875
- w_up: bfloat16 [2, 768, 3072], P(None, None, 'tensor'), may hold values from -0.21875 to 0.21875
- w_down: bfloat16 [2, 3072, 768], P(None, 'tensor'), may hold values from -0.109375 to 0.109375
- ff_bias: float32 [2, 3072], P(None, 'tensor'), may hold values from -3 to 3
- gains: float32 [2, 2, 768], replicated, may hold values from 0.25 to 1.75
- biases: float32 [2, 4, 768], replicated, may hold values from -2 to 2
Outputs:
- result: bfloat16 [1024, 768], P(('dp', 'tensor'))
- input_grad: bfloat16 [1024, 768], P(('dp', 'tensor'))
- w_qkv_grad: float32 [2, 768, 3, 768], P(None, 'dp', None, 'tensor')
- w_out_grad: float32 [2, 768, 768], P(None, 'tensor', 'dp')
- w_up_grad: float32 [2, 768, 3072], P(None, 'dp', 'tensor')
- w_down_grad: float32 [2, 3072, 768], P(None, 'tensor', 'dp')
- gains_grad: float32 [2, 2, 768], replicated
- biases_grad: float32 [2, 4, 768], replicated
- qv_bias_grad: float32 [2, 2, 768], replicated
- ff_bias_grad: float32 [2, 3072], replicated
Inputs may be any that keep to these rules, and one draw needn't show every extreme that they name: `segments`: the document numbers never fall along the stream; each document has 1 to 384 tokens and some document has exactly 384.
All inputs are finite; a program needn't handle non-finite values.
Results may differ from a plain program's by a relative error of at most 0.025.
Values may be sent and summed in bfloat16 or wider, within the bound.
No kernel may reach another device: no remote copies, remote signals or barrier semaphores. Data moves between devices by JAX's collectives and lax.ppermute only.
A program may use at most 128 MiB of HBM per device.

v0:
```python
import jax
import jax.numpy as jnp
from jax import lax
from jax.sharding import PartitionSpec as P

D = 768
HD = 64
FF = 3072
LAYERS = 2
SPAN = 4


epsilon = 1e-05
gelu_c = 0.7978845608028654


def shifted(array, axis, by):
    length = lax.axis_size(axis)
    pairs = [(i, i + by) for i in range(length) if 0 <= i + by < length]
    return lax.ppermute(array, axis, pairs)


def norm_fwd(values_in, gain, shift_bias):
    mean_v = jnp.mean(values_in, axis=-1, keepdims=True)
    centred = values_in - mean_v
    var_v = jnp.mean(centred * centred, axis=-1, keepdims=True)
    rstd = lax.rsqrt(var_v + epsilon)
    normed = centred * rstd
    return (normed * gain + shift_bias, normed, rstd)


def norm_bwd(grad_in, normed, rstd, gain):
    scaled = grad_in * gain
    inner = jnp.mean(scaled, axis=-1, keepdims=True)
    along = jnp.mean(scaled * normed, axis=-1, keepdims=True)
    return rstd * (scaled - inner - normed * along)


def gelu_pair(pre_act):
    inner = gelu_c * (pre_act + 0.044715 * pre_act * pre_act * pre_act)
    tanh_v = jnp.tanh(inner)
    value_out = 0.5 * pre_act * (1.0 + tanh_v)
    slope = 0.5 * (1.0 + tanh_v) + 0.5 * pre_act * (1.0 - tanh_v * tanh_v) * gelu_c * (
        1.0 + 3.0 * 0.044715 * pre_act * pre_act
    )
    return (value_out, slope)


def build_mask(segments, tok_rows):
    dev_index = lax.axis_index("dp")
    row_ids = jnp.arange(tok_rows, dtype=jnp.int32)
    query_pos = dev_index * tok_rows + row_ids
    query_seg = lax.dynamic_slice_in_dim(segments, dev_index * tok_rows, tok_rows)
    key_pos = []
    key_seg = []
    for offset in range(SPAN):
        key_start = (dev_index - (SPAN - 1 - offset)) * tok_rows
        key_pos.append(key_start + row_ids)
        key_seg.append(lax.dynamic_slice_in_dim(segments, jnp.maximum(key_start, 0), tok_rows))
    key_pos = jnp.concatenate(key_pos)
    key_seg = jnp.concatenate(key_seg)
    return (
        (key_pos[None, :] <= query_pos[:, None])
        & (key_pos[None, :] >= 0)
        & (key_seg[None, :] == query_seg[:, None])
    )


def fetch_keys(packed):
    pieces = []
    for distance in range(1, SPAN):
        pieces.append(shifted(packed, "dp", distance))
    ordered = pieces[::-1] + [packed]
    return jnp.concatenate(ordered, axis=1)


def return_keys(grads_all, tok_rows):
    blocks = [grads_all[:, offset * tok_rows : (offset + 1) * tok_rows] for offset in range(SPAN)]
    summed = blocks[SPAN - 1]
    for distance in range(1, SPAN):
        summed = summed + shifted(blocks[SPAN - 1 - distance], "dp", -distance)
    return summed


def score_block(queries, keys_all, key_mask):
    scaled = jnp.einsum(
        "qhd,khd->hqk", queries, keys_all, preferred_element_type=jnp.float32
    ) * HD ** (-0.5)
    return jnp.where(key_mask[None], scaled, -1e30)


def layer_forward(hidden, layer_no, params, key_mask):
    w_qkv, qv_bias, w_out, w_up, w_down, ff_bias, gains, biases = params
    f32 = jnp.float32
    bf16 = jnp.bfloat16
    local_width = w_out.shape[1]
    head_count = local_width // HD
    normed1, hat1, rstd1 = norm_fwd(hidden, gains[layer_no, 0], biases[layer_no, 0])
    act1 = lax.all_gather(normed1.astype(bf16), "tensor", axis=0, tiled=True)
    tok_rows = act1.shape[0]
    projected = jnp.einsum("td,djc->tjc", act1, w_qkv[layer_no], preferred_element_type=f32)
    queries = (
        (projected[:, 0] + qv_bias[layer_no, 0]).astype(bf16).reshape(tok_rows, head_count, HD)
    )
    keys_own = projected[:, 1].astype(bf16)
    values_own = (projected[:, 2] + qv_bias[layer_no, 1]).astype(bf16)
    key_values = fetch_keys(jnp.stack([keys_own, values_own]))
    keys_all = key_values[0].reshape(-1, head_count, HD)
    values_all = key_values[1].reshape(-1, head_count, HD)
    scores = score_block(queries, keys_all, key_mask)
    row_max = jnp.max(scores, axis=-1, keepdims=True)
    row_total = jnp.sum(jnp.exp(scores - row_max), axis=-1, keepdims=True)
    log_total = row_max + jnp.log(row_total)
    weights_b = jnp.exp(scores - log_total).astype(bf16)
    attended = (
        jnp.einsum("hqk,khd->qhd", weights_b, values_all, preferred_element_type=f32)
        .astype(bf16)
        .reshape(tok_rows, local_width)
    )
    branch_sum = lax.psum_scatter(
        jnp.dot(attended, w_out[layer_no], preferred_element_type=f32),
        "tensor",
        scatter_dimension=0,
        tiled=True,
    )
    mid = hidden + branch_sum + biases[layer_no, 1]
    normed2, hat2, rstd2 = norm_fwd(mid, gains[layer_no, 1], biases[layer_no, 2])
    act2 = lax.all_gather(normed2.astype(bf16), "tensor", axis=0, tiled=True)
    pre_act = jnp.dot(act2, w_up[layer_no], preferred_element_type=f32) + ff_bias[layer_no]
    gelu_v, slope = gelu_pair(pre_act)
    act3 = gelu_v.astype(bf16)
    ffn_total = lax.psum_scatter(
        jnp.dot(act3, w_down[layer_no], preferred_element_type=f32),
        "tensor",
        scatter_dimension=0,
        tiled=True,
    )
    final = mid + ffn_total + biases[layer_no, 3]
    cache = (
        hat1,
        rstd1,
        act1,
        queries,
        keys_all,
        values_all,
        attended,
        log_total,
        hat2,
        rstd2,
        act2,
        slope,
        act3,
    )
    return (final, cache)


def layer_backward(grad_now, layer_no, params, cache, key_mask):
    w_qkv, qv_bias, w_out, w_up, w_down, ff_bias, gains, biases = params
    (
        hat1,
        rstd1,
        act1,
        queries,
        keys_all,
        values_all,
        attended,
        log_total,
        hat2,
        rstd2,
        act2,
        slope,
        act3,
    ) = cache
    f32 = jnp.float32
    bf16 = jnp.bfloat16
    tok_rows = act1.shape[0]
    local_width = w_out.shape[1]
    head_count = local_width // HD
    g_bdown = jnp.sum(grad_now, axis=0)
    out_b = lax.all_gather(grad_now.astype(bf16), "tensor", axis=0, tiled=True)
    g_wdown = jnp.dot(act3.T, out_b, preferred_element_type=f32)
    d_pre = jnp.dot(out_b, w_down[layer_no].T, preferred_element_type=f32) * slope
    g_ffb = jnp.sum(d_pre, axis=0)
    pre_b = d_pre.astype(bf16)
    g_wup = jnp.dot(act2.T, pre_b, preferred_element_type=f32)
    d_norm2 = lax.psum_scatter(
        jnp.dot(pre_b, w_up[layer_no].T, preferred_element_type=f32),
        "tensor",
        scatter_dimension=0,
        tiled=True,
    )
    g_gain2 = jnp.sum(d_norm2 * hat2, axis=0)
    g_bias2 = jnp.sum(d_norm2, axis=0)
    grad_mid = grad_now + norm_bwd(d_norm2, hat2, rstd2, gains[layer_no, 1])
    g_bout = jnp.sum(grad_mid, axis=0)
    mid_b = lax.all_gather(grad_mid.astype(bf16), "tensor", axis=0, tiled=True)
    g_wout = jnp.dot(attended.T, mid_b, preferred_element_type=f32)
    d_att = (
        jnp.dot(mid_b, w_out[layer_no].T, preferred_element_type=f32)
        .astype(bf16)
        .reshape(tok_rows, head_count, HD)
    )
    att_heads = attended.reshape(tok_rows, head_count, HD)
    delta = jnp.sum(d_att.astype(f32) * att_heads.astype(f32), axis=-1).T[:, :, None]
    scores = score_block(queries, keys_all, key_mask)
    probs = jnp.exp(scores - log_total)
    d_prob = jnp.einsum("qhd,khd->hqk", d_att, values_all, preferred_element_type=f32)
    d_score = (probs * (d_prob - delta) * HD ** (-0.5)).astype(bf16)
    d_query = jnp.einsum("hqk,khd->qhd", d_score, keys_all, preferred_element_type=f32).reshape(
        tok_rows, local_width
    )
    d_keys = jnp.einsum("hqk,qhd->khd", d_score, queries, preferred_element_type=f32).reshape(
        -1, local_width
    )
    d_values = jnp.einsum(
        "hqk,qhd->khd", probs.astype(bf16), d_att, preferred_element_type=f32
    ).reshape(-1, local_width)
    kv_grads = return_keys(jnp.stack([d_keys, d_values]), tok_rows)
    g_qb = jnp.sum(d_query, axis=0)
    g_vb = jnp.sum(kv_grads[1], axis=0)
    d_proj = jnp.stack([d_query, kv_grads[0], kv_grads[1]], axis=1).astype(bf16)
    g_wqkv = jnp.einsum("td,tjc->djc", act1, d_proj, preferred_element_type=f32)
    d_norm1 = lax.psum_scatter(
        jnp.einsum("tjc,djc->td", d_proj, w_qkv[layer_no], preferred_element_type=f32),
        "tensor",
        scatter_dimension=0,
        tiled=True,
    )
    g_gain1 = jnp.sum(d_norm1 * hat1, axis=0)
    g_bias1 = jnp.sum(d_norm1, axis=0)
    grad_in = grad_mid + norm_bwd(d_norm1, hat1, rstd1, gains[layer_no, 0])
    tensor_index = lax.axis_index("tensor")
    qv_wide = lax.dynamic_update_slice_in_dim(
        jnp.zeros((2, D), f32), jnp.stack([g_qb, g_vb]), tensor_index * local_width, 1
    )
    ff_wide = lax.dynamic_update_slice_in_dim(
        jnp.zeros((FF,), f32), g_ffb, tensor_index * g_ffb.shape[0], 0
    )
    weight_grads = (g_wqkv[None], g_wout[None], g_wup[None], g_wdown[None])
    small_grads = (
        jnp.stack([g_gain1, g_gain2])[None],
        jnp.stack([g_bias1, g_bout, g_bias2, g_bdown])[None],
        qv_wide[None],
        ff_wide[None],
    )
    return (grad_in, weight_grads, small_grads)


def shards(
    tokens, cotangent, segments, w_qkv, qv_bias, w_out, w_up, w_down, ff_bias, gains, biases
):
    params = (w_qkv, qv_bias, w_out, w_up, w_down, ff_bias, gains, biases)
    tok_rows = tokens.shape[0] * lax.axis_size("tensor")
    key_mask = build_mask(segments, tok_rows)
    hidden = tokens.astype(jnp.float32)
    caches = []
    for layer_no in range(LAYERS):
        hidden, cache = layer_forward(hidden, layer_no, params, key_mask)
        caches.append(cache)
    result = hidden.astype(jnp.bfloat16)
    grad_now = cotangent.astype(jnp.float32)
    weight_parts = [None] * LAYERS
    small_parts = [None] * LAYERS
    for layer_no in range(LAYERS - 1, -1, -1):
        grad_now, weight_grads, small_grads = layer_backward(
            grad_now, layer_no, params, caches[layer_no], key_mask
        )
        weight_parts[layer_no] = weight_grads
        small_parts[layer_no] = small_grads
    stacked = [
        jnp.concatenate([per_layer[member] for per_layer in weight_parts], axis=0)
        for member in range(4)
    ]
    small_stack = [
        jnp.concatenate([per_layer[member] for per_layer in small_parts], axis=0)
        for member in range(4)
    ]
    stacked = (
        lax.psum_scatter(stacked[0], "dp", scatter_dimension=1, tiled=True),
        lax.psum_scatter(stacked[1], "dp", scatter_dimension=2, tiled=True),
        lax.psum_scatter(stacked[2], "dp", scatter_dimension=1, tiled=True),
        lax.psum_scatter(stacked[3], "dp", scatter_dimension=2, tiled=True),
    )
    small_stack = lax.psum(
        (small_stack[0], small_stack[1], small_stack[2], small_stack[3]), ("dp", "tensor")
    )
    return (
        result,
        grad_now.astype(jnp.bfloat16),
        stacked[0],
        stacked[1],
        stacked[2],
        stacked[3],
        small_stack[0],
        small_stack[1],
        small_stack[2],
        small_stack[3],
    )


def solution(mesh):
    return jax.shard_map(
        shards,
        mesh=mesh,
        in_specs=(
            P(("dp", "tensor"), None),
            P(("dp", "tensor"), None),
            P(),
            P(None, None, None, "tensor"),
            P(None, None, "tensor"),
            P(None, "tensor", None),
            P(None, None, "tensor"),
            P(None, "tensor", None),
            P(None, "tensor"),
            P(),
            P(),
        ),
        out_specs=(
            P(("dp", "tensor"), None),
            P(("dp", "tensor"), None),
            P(None, "dp", None, "tensor"),
            P(None, "tensor", "dp"),
            P(None, "dp", "tensor"),
            P(None, "tensor", "dp"),
            P(),
            P(),
            P(),
            P(),
        ),
        check_vma=False,
    )
```

profile of v0, /device:TPU:0, one launch (start us, length us, event | category | flops | bytes accessed | tf_op | source)
XLA Modules:
  0.0 898.1 jit_solution(10383623494256973941)
XLA Ops:
  11.1 6.8 all_gather.24
  38.4 21.1 %reduce-scatter.16.cloned.1.call-done = f32[32,768]{1,0:T(8,128)} async-done(((f32[128,768]{1,0:T(8,128)}), f32[32,768]{1,0:T(8,128)}) %reduce-scatter.16.cloned.1.call-update) | async-done | bytes 98320 | tf_op jit(solution)/shard_map/reduce_scatter | solution.py:120
  60.9 5.6 all_gather.25
  69.5 21.0 %reduce-scatter.18.cloned.1.call-done = f32[32,768]{1,0:T(8,128)} async-done(((f32[128,768]{1,0:T(8,128)}), f32[32,768]{1,0:T(8,128)}) %reduce-scatter.18.cloned.1.call-update) | async-done | bytes 98320 | tf_op jit(solution)/shard_map/reduce_scatter | solution.py:132
  91.8 5.6 all_gather.26
  113.6 5.6 all_gather.28
  119.2 15.3 %reduce-scatter.20.cloned.1.call-done = f32[32,768]{1,0:T(8,128)} async-done(((f32[128,768]{1,0:T(8,128)}), f32[32,768]{1,0:T(8,128)}) %reduce-scatter.20.cloned.1.call-update) | async-done | bytes 98320 | tf_op jit(solution)/shard_map/reduce_scatter | solution.py:120
  135.9 5.6 all_gather.27
  149.1 18.3 %reduce-scatter.24.cloned.1.call-done = f32[32,768]{1,0:T(8,128)} async-done(((f32[128,768]{1,0:T(8,128)}), f32[32,768]{1,0:T(8,128)}) %reduce-scatter.24.cloned.1.call-update) | async-done | bytes 98320 | tf_op jit(solution)/shard_map/reduce_scatter | solution.py:186
  169.1 22.2 %reduce-scatter.22.cloned.1.call-done = f32[32,768]{1,0:T(8,128)} async-done(((f32[128,768]{1,0:T(8,128)}), f32[32,768]{1,0:T(8,128)}) %reduce-scatter.22.cloned.1.call-update) | async-done | bytes 98320 | tf_op jit(solution)/shard_map/reduce_scatter | solution.py:132
  193.5 5.6 all_gather.29
  211.5 5.1 collective-permute-done.7
  220.7 25.3 %reduce-scatter.26.cloned.1.call-done = f32[32,768]{1,0:T(8,128)} async-done(((f32[128,768]{1,0:T(8,128)}), f32[32,768]{1,0:T(8,128)}) %reduce-scatter.26.cloned.1.call-update) | async-done | bytes 98320 | tf_op jit(solution)/shard_map/reduce_scatter | solution.py:223
  249.5 5.6 all_gather.30
  259.7 21.0 %reduce-scatter.28.cloned.1.call-done = f32[32,768]{1,0:T(8,128)} async-done(((f32[128,768]{1,0:T(8,128)}), f32[32,768]{1,0:T(8,128)}) %reduce-scatter.28.cloned.1.call-update) | async-done | bytes 98320 | tf_op jit(solution)/shard_map/reduce_scatter | solution.py:186
  284.0 5.8 all_gather.31
  297.3 5.5 collective-permute-done.10
  318.7 8.2 copy.23
  333.6 8.0 reshape.387
  357.5 45.7 %reduce-scatter.36.cloned.1.call-done = f32[96,384]{1,0:T(8,128)} async-done(((f32[768,384]{1,0:T(8,128)}), f32[96,384]{1,0:T(8,128)}) %reduce-scatter.36.cloned.1.call-update) | async-done | bytes 147472
  405.2 170.2 %all-reduce.5.cloned.1.call-done = f32[2,768,768]{1,0,2:T(2,128)} async-done(((f32[2,768,768]{1,0,2:T(2,128)}), f32[2,768,768]{1,0,2:T(2,128)}) %all-reduce.5.cloned.1.call-update) | async-done | bytes 4718608
  577.3 79.9 %reduce-scatter.34.cloned.1.call-done = f32[96,1152]{1,0:T(8,128)} async-done(((f32[768,1152]{1,0:T(8,128)}), f32[96,1152]{1,0:T(8,128)}) %reduce-scatter.34.cloned.1.call-update) | async-done | bytes 442384
  659.8 123.8 %all-reduce.7.cloned.1.call-done = (f32[2,2,768]{2,1,0:T(2,128)}, f32[2,4,768]{2,1,0:T(4,128)}, f32[2,2,768]{2,1,0:T(2,128)}, f32[2,3072]{1,0:T(2,128)}) async-done(((f32[2,2,768]{2,1,0:T(2,128)}, f32[2,4,768]{2,1,0:T(4,128)}, f32[2,2,768]{2,1,0:T(2,128)}, f32[2,3072]{1,0:T(2,128)}), (f32[2,2,768]{2,1,0:T(2,128)}, f32[2,4,768]{2,1,0:T(4,128)}, f32[2,2,768]{2,1,0:T(2,128)}, ...) | async-done | bytes 73744 | tf_op jit(solution)/shard_map/psum | solution.py:284
  783.6 102.7 %reduce-scatter.32.cloned.1.call-done = f32[2,96,768]{2,1,0:T(8,128)} async-done(((f32[2,768,768]{2,1,0:T(8,128)}), f32[2,96,768]{2,1,0:T(8,128)}) %reduce-scatter.32.cloned.1.call-update) | async-done | bytes 589840 | tf_op jit(solution)/shard_map/reduce_scatter | solution.py:281
  (376 shorter events, 142.5 us)
Async XLA Ops:
  7.2 52.3 %reduce-scatter.16.cloned.1.call-start = ((), (), s32[]{:S(2)}) async-start(), calls=%async_computation.11 | async-start | bytes 491520 | tf_op jit(solution)/shard_map/reduce_scatter | solution.py:120
  20.6 12.0 %collective-permute-start = (bf16[2,128,192]{1,2,0:T(8,128)(2,1)S(1)}, bf16[2,128,192]{1,2,0:T(8,128)(2,1)S(1)}, u32[]{:S(2)}, u32[]{:S(2)}) collective-permute-start(bf16[2,128,192]{1,2,0:T(8,128)(2,1)S(1)} %pad_maximum_fusion.8), channel_id=1, source_target_pairs={{0,12},{4,16},{8,20},{12,24},{16,28},{1,13},{5,17},{9,21},{13,25},... | collective-permute-start | bytes 294920 | tf_op jit(solution)/shard_map/ppermute | solution.py:20
  25.3 7.4 collective-permute-start.1
  28.8 5.6 collective-permute-start.2
  37.7 52.7 %reduce-scatter.18.cloned.1.call-start = ((), (), s32[]{:S(2)}) async-start(), calls=%async_computation.12 | async-start | bytes 491520 | tf_op jit(solution)/shard_map/reduce_scatter | solution.py:132
  69.4 65.0 %reduce-scatter.20.cloned.1.call-start = ((), (), s32[]{:S(2)}) async-start(), calls=%async_computation.13 | async-start | bytes 491520 | tf_op jit(solution)/shard_map/reduce_scatter | solution.py:120
  97.9 11.9 %collective-permute-start.3 = (bf16[2,128,192]{1,2,0:T(8,128)(2,1)S(1)}, bf16[2,128,192]{1,2,0:T(8,128)(2,1)S(1)}, u32[]{:S(2)}, u32[]{:S(2)}) collective-permute-start(bf16[2,128,192]{1,2,0:T(8,128)(2,1)S(1)} %pad_maximum_fusion.9), channel_id=1, source_target_pairs={{0,12},{4,16},{8,20},{12,24},{16,28},{1,13},{5,17},{9,21},{13,25},... | collective-permute-start | bytes 294920 | tf_op jit(solution)/shard_map/ppermute | solution.py:20
  102.2 7.6 collective-permute-start.4
  113.5 54.0 %reduce-scatter.24.cloned.1.call-start = ((), (), s32[]{:S(2)}) async-start(), calls=%async_computation.15 | async-start | bytes 491520 | tf_op jit(solution)/shard_map/reduce_scatter | solution.py:186
  146.5 44.8 %reduce-scatter.22.cloned.1.call-start = ((), (), s32[]{:S(2)}) async-start(), calls=%async_computation.14 | async-start | bytes 491520 | tf_op jit(solution)/shard_map/reduce_scatter | solution.py:132
  149.1 97.0 %reduce-scatter.26.cloned.1.call-start = ((), (), s32[]{:S(2)}) async-start(), calls=%async_computation.16 | async-start | bytes 491520 | tf_op jit(solution)/shard_map/reduce_scatter | solution.py:223
  202.4 9.0 %collective-permute-start.6 = (f32[2,128,192]{1,2,0:T(8,128)S(1)}, f32[2,128,192]{1,2,0:T(8,128)S(1)}, u32[]{:S(2)}, u32[]{:S(2)}) collective-permute-start(f32[2,128,192]{1,2,0:T(8,128)S(1)} %get-tuple-element.85), channel_id=1, source_target_pairs={{4,0},{8,4},{12,8},{16,12},{20,16},{24,20},{28,24},{5,1},{9,5},{13... | collective-permute-start | bytes 589832 | tf_op jit(solution)/shard_map/ppermute | solution.py:20
  203.7 12.9 %collective-permute-start.7 = (f32[2,128,192]{1,2,0:T(8,128)S(1)}, f32[2,128,192]{1,2,0:T(8,128)S(1)}, u32[]{:S(2)}, u32[]{:S(2)}) collective-permute-start(f32[2,128,192]{1,2,0:T(8,128)S(1)} %get-tuple-element.87), channel_id=1, source_target_pairs={{8,0},{12,4},{16,8},{20,12},{24,16},{28,20},{9,1},{13,5},{17,9},{2... | collective-permute-start | bytes 589832 | tf_op jit(solution)/shard_map/ppermute | solution.py:20
  205.0 13.8 %collective-permute-start.8 = (f32[2,128,192]{1,2,0:T(8,128)S(1)}, f32[2,128,192]{1,2,0:T(8,128)S(1)}, u32[]{:S(2)}, u32[]{:S(2)}) collective-permute-start(f32[2,128,192]{1,2,0:T(8,128)S(1)} %get-tuple-element.86), channel_id=1, source_target_pairs={{12,0},{16,4},{20,8},{24,12},{28,16},{13,1},{17,5},{21,9},{25,13},... | collective-permute-start | bytes 589832 | tf_op jit(solution)/shard_map/ppermute | solution.py:20
  220.7 60.0 %reduce-scatter.28.cloned.1.call-start = ((), (), s32[]{:S(2)}) async-start(), calls=%async_computation.17 | async-start | bytes 491520 | tf_op jit(solution)/shard_map/reduce_scatter | solution.py:186
  259.7 88.6 %reduce-scatter.30.cloned.1.call-start = ((), (), s32[]{:S(2)}) async-start(), calls=%async_computation.18 | async-start | bytes 491520 | tf_op jit(solution)/shard_map/reduce_scatter | solution.py:223
  292.9 9.9 %collective-permute-start.10 = (f32[2,128,192]{1,2,0:T(8,128)S(1)}, f32[2,128,192]{1,2,0:T(8,128)S(1)}, u32[]{:S(2)}, u32[]{:S(2)}) collective-permute-start(f32[2,128,192]{1,2,0:T(8,128)S(1)} %get-tuple-element.84), channel_id=1, source_target_pairs={{8,0},{12,4},{16,8},{20,12},{24,16},{28,20},{9,1},{13,5},{17,9},{2... | collective-permute-start | bytes 589832 | tf_op jit(solution)/shard_map/ppermute | solution.py:20
  294.4 13.0 %collective-permute-start.11 = (f32[2,128,192]{1,2,0:T(8,128)S(1)}, f32[2,128,192]{1,2,0:T(8,128)S(1)}, u32[]{:S(2)}, u32[]{:S(2)}) collective-permute-start(f32[2,128,192]{1,2,0:T(8,128)S(1)} %get-tuple-element.83), channel_id=1, source_target_pairs={{12,0},{16,4},{20,8},{24,12},{28,16},{13,1},{17,5},{21,9},{25,13},... | collective-permute-start | bytes 589832 | tf_op jit(solution)/shard_map/ppermute | solution.py:20
  295.7 13.3 %collective-permute-start.9 = (f32[2,128,192]{1,2,0:T(8,128)S(1)}, f32[2,128,192]{1,2,0:T(8,128)S(1)}, u32[]{:S(2)}, u32[]{:S(2)}) collective-permute-start(f32[2,128,192]{1,2,0:T(8,128)S(1)} %get-tuple-element.82), channel_id=1, source_target_pairs={{4,0},{8,4},{12,8},{16,12},{20,16},{24,20},{28,24},{5,1},{9,5},{13... | collective-permute-start | bytes 589832 | tf_op jit(solution)/shard_map/ppermute | solution.py:20
  310.8 92.5 %reduce-scatter.36.cloned.1.call-start = ((), (), s32[]{:S(2)}) async-start(), calls=%async_computation.21 | async-start | bytes 1327104
  314.6 260.7 %all-reduce.5.cloned.1.call-start = ((), (), s32[]{:S(2)}) async-start(), calls=%async_computation.22 | async-start | bytes 9437184
  327.0 330.3 %reduce-scatter.34.cloned.1.call-start = ((), (), s32[]{:S(2)}) async-start(), calls=%async_computation.20 | async-start | bytes 3981312
  341.8 441.9 %all-reduce.7.cloned.1.call-start = ((), (), s32[]{:S(2)}) async-start(), calls=%async_computation.23 | async-start | bytes 147456 | tf_op jit(solution)/shard_map/psum | solution.py:284
  350.7 535.5 %reduce-scatter.32.cloned.1.call-start = ((), (), s32[]{:S(2)}) async-start(), calls=%async_computation.19 | async-start | bytes 5308416 | tf_op jit(solution)/shard_map/reduce_scatter | solution.py:281
  (82 other events, 800.5 us)
Sparse Core Ops, SparseCore 0:
  37.8 21.6 reduce-scatter.15
  69.5 20.8 reduce-scatter.17
  113.6 20.7 reduce-scatter.19
  146.6 20.8 reduce-scatter.23
  170.4 20.8 reduce-scatter.21
  220.8 25.1 reduce-scatter.25
  259.8 20.8 reduce-scatter.27
  310.9 24.7 reduce-scatter.29
  339.2 64.0 reduce-scatter.35
  406.7 168.5 all-reduce.4
  579.0 78.2 reduce-scatter.33
  664.4 119.1 all-reduce.6
  787.8 98.3 reduce-scatter.31
where the time goes:
time: 900 us; the launch traced here: 898 us
  waiting for transfers between devices  693 us (77%)
  local copies, waits for them, and re-layouts  47.5 us (5%)
  blocking collectives  46.3 us (5%)
  matrix products  33.3 us (4%)
  starting transfers between devices  31.1 us (3%)
  other arithmetic  31 us (3%)
  between operations  16 us (2%)
    unnamed x16, waiting for transfers between devices  296 us
    psum x1, waiting for transfers between devices, shards(): lax.psum((small_stack[0], small_stack[1], small_stack[2], small_stack[3])...  124 us
    reduce_scatter x1, waiting for transfers between devices, shards(): lax.psum_scatter(stacked[2], 'dp', scatter_dimension=1, tiled=True)  103 us
    reduce_scatter x2, waiting for transfers between devices, layer_forward(): lax.psum_scatter(jnp.dot(act3, w_down[layer_no], preferred_element_type=f...  43.2 us
    reduce_scatter x2, waiting for transfers between devices, layer_backward(): lax.psum_scatter(jnp.dot(pre_b, w_up[layer_no].T, preferred_element_type=...  39.3 us
    reduce_scatter x2, waiting for transfers between devices, layer_forward(): lax.psum_scatter(jnp.dot(attended, w_out[layer_no], preferred_element_typ...  36.4 us
    unnamed x177, local copies, waits for them, and re-layouts  33.8 us
    ppermute x12, starting transfers between devices, shifted(): return lax.ppermute(array, axis, pairs)  30.5 us
  transfers between devices with their start and end apart: 25, of which 20 were waited for; matrix products, arithmetic and copies ran while one was open for 6% of the time, Pallas kernels for 0%

commit v1 on v0

v1 whole, which is shorter than its diff:
```python
import jax
import jax.numpy as jnp
from jax import lax
from jax.sharding import PartitionSpec as P

D = 768
HD = 64
FF = 3072
LAYERS = 2
SPAN = 4


epsilon = 1e-05
gelu_c = 0.7978845608028654
f32 = jnp.float32
bf16 = jnp.bfloat16


def shifted(array, axis, by):
    length = lax.axis_size(axis)
    pairs = [(i, i + by) for i in range(length) if 0 <= i + by < length]
    return lax.ppermute(array, axis, pairs)


def swapped(array, axis, bit):
    length = lax.axis_size(axis)
    return lax.ppermute(array, axis, [(i, i ^ bit) for i in range(length)])


def bits_of(axis):
    length = lax.axis_size(axis)
    found, bit = [], 1
    while bit < length:
        found.append(bit)
        bit *= 2
    assert bit == length
    return found


def norm_fwd(values_in, gain, shift_bias):
    mean_v = jnp.mean(values_in, axis=-1, keepdims=True)
    centred = values_in - mean_v
    var_v = jnp.mean(centred * centred, axis=-1, keepdims=True)
    rstd = lax.rsqrt(var_v + epsilon)
    normed = centred * rstd
    return (normed * gain + shift_bias, normed, rstd)


def norm_bwd(grad_in, normed, rstd, gain):
    scaled = grad_in * gain
    inner = jnp.mean(scaled, axis=-1, keepdims=True)
    along = jnp.mean(scaled * normed, axis=-1, keepdims=True)
    return rstd * (scaled - inner - normed * along)


def gelu_pair(pre_act):
    inner = gelu_c * (pre_act + 0.044715 * pre_act * pre_act * pre_act)
    tanh_v = jnp.tanh(inner)
    value_out = 0.5 * pre_act * (1.0 + tanh_v)
    slope = 0.5 * (1.0 + tanh_v) + 0.5 * pre_act * (1.0 - tanh_v * tanh_v) * gelu_c * (
        1.0 + 3.0 * 0.044715 * pre_act * pre_act
    )
    return (value_out, slope)


def build_mask(segments, tok_rows):
    dev_index = lax.axis_index("dp")
    row_ids = jnp.arange(tok_rows, dtype=jnp.int32)
    query_pos = dev_index * tok_rows + row_ids
    query_seg = lax.dynamic_slice_in_dim(segments, dev_index * tok_rows, tok_rows)
    key_pos = []
    key_seg = []
    for offset in range(SPAN):
        key_start = (dev_index - (SPAN - 1 - offset)) * tok_rows
        key_pos.append(key_start + row_ids)
        key_seg.append(lax.dynamic_slice_in_dim(segments, jnp.maximum(key_start, 0), tok_rows))
    key_pos = jnp.concatenate(key_pos)
    key_seg = jnp.concatenate(key_seg)
    return (
        (key_pos[None, :] <= query_pos[:, None])
        & (key_pos[None, :] >= 0)
        & (key_seg[None, :] == query_seg[:, None])
    )


def gather_rows(rows):
    bits = bits_of("tensor")
    mine = lax.axis_index("tensor")
    for place, bit in enumerate(bits[::-1]):
        other = swapped(rows, "tensor", bit)
        high = (mine & bit) != 0
        pair = [jnp.where(high, other, rows), jnp.where(high, rows, other)]
        rows = jnp.stack(pair, axis=place)
    return rows.reshape(-1, rows.shape[-1])


def tensor_sum(part):
    bits = bits_of("tensor")
    high = (lax.axis_index("tensor") & 1) != 0
    half = part.shape[0] // 2
    low_half, high_half = part[:half], part[half:]
    keep = jnp.where(high, high_half, low_half)
    give = jnp.where(high, low_half, high_half).astype(bf16)
    total = keep + swapped(give, "tensor", 1).astype(f32)
    for bit in bits[1:]:
        rounded = total.astype(bf16)
        total = rounded.astype(f32) + swapped(rounded, "tensor", bit).astype(f32)
    rounded = total.astype(bf16)
    other = swapped(rounded, "tensor", 1)
    return jnp.concatenate(
        [jnp.where(high, other, rounded), jnp.where(high, rounded, other)]
    ).astype(f32)


def dp_halving(pairs):
    bits = bits_of("dp")
    mine = lax.axis_index("dp")
    count = lax.axis_size("dp")

    def pick(array, axis, bit, own):
        at = jnp.where(((mine & bit) != 0) == own, 1, 0)
        return lax.dynamic_index_in_dim(array, at, axis, keepdims=False)

    def products(own):
        parts = []
        for left, right in pairs:
            rows, width = left.shape
            split = left.reshape(rows, count // 2, 2, width // count)
            chosen = pick(split, 2, 1, own).reshape(rows, width // 2)
            parts.append(
                lax.dot_general(
                    chosen, right, (((0,), (0,)), ((), ())), preferred_element_type=f32
                )
            )
        return jnp.concatenate(parts, axis=1)

    incoming = swapped(products(False).astype(bf16), "dp", bits[0])
    total = products(True) + incoming.astype(f32)
    wide = total.shape[1]
    block = total.shape[0] // (count // 2)
    blocks = count // 2
    for bit in bits[1:]:
        split = total.reshape(blocks // 2, 2, block, wide)
        incoming = swapped(pick(split, 1, bit, False).astype(bf16), "dp", bit)
        total = pick(split, 1, bit, True) + incoming.astype(f32)
        blocks //= 2
    return total.reshape(block, wide)


def fetch_keys(packed):
    pieces = []
    for distance in range(1, SPAN):
        pieces.append(shifted(packed, "dp", distance))
    ordered = pieces[::-1] + [packed]
    return jnp.concatenate(ordered, axis=0)


def return_keys(grads_all, tok_rows):
    blocks = [grads_all[offset * tok_rows : (offset + 1) * tok_rows] for offset in range(SPAN)]
    summed = blocks[SPAN - 1]
    for distance in range(1, SPAN):
        given = blocks[SPAN - 1 - distance].astype(bf16)
        summed = summed + shifted(given, "dp", -distance).astype(f32)
    return summed


def score_block(queries, keys_all, key_mask):
    scaled = jnp.einsum(
        "qhd,khd->hqk", queries, keys_all, preferred_element_type=f32
    ) * HD ** (-0.5)
    return jnp.where(key_mask[None], scaled, -1e30)


def layer_forward(hidden, layer_no, params, key_mask):
    w_qkv, qv_bias, w_out, w_up, w_down, ff_bias, gains, biases = params
    local_width = w_out.shape[1]
    head_count = local_width // HD
    normed1, hat1, rstd1 = norm_fwd(hidden, gains[layer_no, 0], biases[layer_no, 0])
    act1 = normed1.astype(bf16)
    tok_rows = act1.shape[0]

    def project(member):
        return jnp.dot(act1, w_qkv[layer_no, :, member], preferred_element_type=f32)

    keys_own = project(1).astype(bf16)
    values_own = (project(2) + qv_bias[layer_no, 1]).astype(bf16)
    key_values = fetch_keys(jnp.concatenate([keys_own, values_own], axis=1))
    queries = (project(0) + qv_bias[layer_no, 0]).astype(bf16)
    queries = queries.reshape(tok_rows, head_count, HD)
    keys_all = key_values[:, :local_width].reshape(-1, head_count, HD)
    values_all = key_values[:, local_width:].reshape(-1, head_count, HD)
    scores = score_block(queries, keys_all, key_mask)
    row_max = jnp.max(scores, axis=-1, keepdims=True)
    row_total = jnp.sum(jnp.exp(scores - row_max), axis=-1, keepdims=True)
    log_total = row_max + jnp.log(row_total)
    weights_b = jnp.exp(scores - log_total).astype(bf16)
    attended = (
        jnp.einsum("hqk,khd->qhd", weights_b, values_all, preferred_element_type=f32)
        .astype(bf16)
        .reshape(tok_rows, local_width)
    )
    branch_sum = tensor_sum(jnp.dot(attended, w_out[layer_no], preferred_element_type=f32))
    mid = hidden + branch_sum + biases[layer_no, 1]
    normed2, hat2, rstd2 = norm_fwd(mid, gains[layer_no, 1], biases[layer_no, 2])
    act2 = normed2.astype(bf16)
    pre_act = jnp.dot(act2, w_up[layer_no], preferred_element_type=f32) + ff_bias[layer_no]
    gelu_v, slope = gelu_pair(pre_act)
    act3 = gelu_v.astype(bf16)
    ffn_total = tensor_sum(jnp.dot(act3, w_down[layer_no], preferred_element_type=f32))
    final = mid + ffn_total + biases[layer_no, 3]
    cache = (
        hat1,
        rstd1,
        act1,
        queries,
        keys_all,
        values_all,
        attended,
        log_total,
        hat2,
        rstd2,
        act2,
        slope,
        act3,
    )
    return (final, cache)


def layer_backward(grad_now, layer_no, params, cache, key_mask):
    w_qkv, qv_bias, w_out, w_up, w_down, ff_bias, gains, biases = params
    (
        hat1,
        rstd1,
        act1,
        queries,
        keys_all,
        values_all,
        attended,
        log_total,
        hat2,
        rstd2,
        act2,
        slope,
        act3,
    ) = cache
    tok_rows = act1.shape[0]
    local_width = w_out.shape[1]
    head_count = local_width // HD
    g_bdown = jnp.sum(grad_now, axis=0)
    out_b = grad_now.astype(bf16)
    d_pre = jnp.dot(out_b, w_down[layer_no].T, preferred_element_type=f32) * slope
    g_ffb = jnp.sum(d_pre, axis=0)
    pre_b = d_pre.astype(bf16)
    d_norm2 = tensor_sum(jnp.dot(pre_b, w_up[layer_no].T, preferred_element_type=f32))
    mlp_grads = dp_halving([(act2, pre_b), (out_b, act3)])
    g_gain2 = jnp.sum(d_norm2 * hat2, axis=0)
    g_bias2 = jnp.sum(d_norm2, axis=0)
    grad_mid = grad_now + norm_bwd(d_norm2, hat2, rstd2, gains[layer_no, 1])
    g_bout = jnp.sum(grad_mid, axis=0)
    mid_b = grad_mid.astype(bf16)
    d_att = (
        jnp.dot(mid_b, w_out[layer_no].T, preferred_element_type=f32)
        .astype(bf16)
        .reshape(tok_rows, head_count, HD)
    )
    att_heads = attended.reshape(tok_rows, head_count, HD)
    delta = jnp.sum(d_att.astype(f32) * att_heads.astype(f32), axis=-1).T[:, :, None]
    scores = score_block(queries, keys_all, key_mask)
    probs = jnp.exp(scores - log_total)
    d_prob = jnp.einsum("qhd,khd->hqk", d_att, values_all, preferred_element_type=f32)
    d_score = (probs * (d_prob - delta) * HD ** (-0.5)).astype(bf16)
    d_keys = jnp.einsum("hqk,qhd->khd", d_score, queries, preferred_element_type=f32).reshape(
        -1, local_width
    )
    d_values = jnp.einsum(
        "hqk,qhd->khd", probs.astype(bf16), d_att, preferred_element_type=f32
    ).reshape(-1, local_width)
    kv_grads = return_keys(jnp.concatenate([d_keys, d_values], axis=1), tok_rows)
    d_query = jnp.einsum("hqk,khd->qhd", d_score, keys_all, preferred_element_type=f32).reshape(
        tok_rows, local_width
    )
    g_qb = jnp.sum(d_query, axis=0)
    g_vb = jnp.sum(kv_grads[:, local_width:], axis=0)
    d_proj = jnp.concatenate([d_query, kv_grads], axis=1).astype(bf16)
    d_norm1 = tensor_sum(
        sum(
            lax.dot_general(
                d_proj[:, member * local_width : (member + 1) * local_width],
                w_qkv[layer_no, :, member],
                (((1,), (1,)), ((), ())),
                preferred_element_type=f32,
            )
            for member in range(3)
        )
    )
    att_grads = dp_halving([(act1, d_proj), (mid_b, attended)])
    g_gain1 = jnp.sum(d_norm1 * hat1, axis=0)
    g_bias1 = jnp.sum(d_norm1, axis=0)
    grad_in = grad_mid + norm_bwd(d_norm1, hat1, rstd1, gains[layer_no, 0])
    small = (
        jnp.stack([g_gain1, g_gain2]),
        jnp.stack([g_bias1, g_bout, g_bias2, g_bdown]),
        jnp.stack([g_qb, g_vb]),
        g_ffb,
    )
    return (grad_in, mlp_grads, att_grads, small)


def shards(
    tokens, cotangent, segments, w_qkv, qv_bias, w_out, w_up, w_down, ff_bias, gains, biases
):
    params = (w_qkv, qv_bias, w_out, w_up, w_down, ff_bias, gains, biases)
    tensor_count = lax.axis_size("tensor")
    tensor_index = lax.axis_index("tensor")
    own_rows = tokens.shape[0]
    tok_rows = own_rows * tensor_count
    local_width = w_out.shape[1]
    local_ff = w_up.shape[2]
    key_mask = build_mask(segments, tok_rows)
    hidden = gather_rows(tokens).astype(f32)
    grad_now = gather_rows(cotangent).astype(f32)
    caches = []
    for layer_no in range(LAYERS):
        hidden, cache = layer_forward(hidden, layer_no, params, key_mask)
        caches.append(cache)

    def own(rows):
        return lax.dynamic_slice_in_dim(rows, tensor_index * own_rows, own_rows).astype(bf16)

    result = own(hidden)
    mlp_parts = [None] * LAYERS
    att_parts = [None] * LAYERS
    small_parts = [None] * LAYERS
    for layer_no in range(LAYERS - 1, -1, -1):
        grad_now, mlp_parts[layer_no], att_parts[layer_no], small_parts[layer_no] = layer_backward(
            grad_now, layer_no, params, caches[layer_no], key_mask
        )
    block = mlp_parts[0].shape[0]
    g_wqkv = jnp.stack([a[:, : 3 * local_width].reshape(block, 3, local_width) for a in att_parts])
    g_wout = jnp.stack([a[:, 3 * local_width :].T for a in att_parts])
    g_wup = jnp.stack([m[:, :local_ff] for m in mlp_parts])
    g_wdown = jnp.stack([m[:, local_ff:].T for m in mlp_parts])

    def widened(array):
        wide = jnp.zeros(array.shape[:-1] + (array.shape[-1] * tensor_count,), f32)
        start = tensor_index * array.shape[-1]
        return lax.dynamic_update_slice_in_dim(wide, array, start, array.ndim - 1)

    share = 1.0 / tensor_count
    small = [
        jnp.stack([s[0] for s in small_parts]) * share,
        jnp.stack([s[1] for s in small_parts]) * share,
        widened(jnp.stack([s[2] for s in small_parts])),
        widened(jnp.stack([s[3] for s in small_parts])),
    ]
    flat = jnp.concatenate([s.reshape(-1, D) for s in small])
    for axis in ("tensor", "dp"):
        for bit in bits_of(axis):
            flat = flat + swapped(flat, axis, bit)
    outs = []
    start = 0
    for s in small:
        rows = s.size // D
        outs.append(flat[start : start + rows].reshape(s.shape))
        start += rows
    return (result, own(grad_now), g_wqkv, g_wout, g_wup, g_wdown, *outs)


def solution(mesh):
    return jax.shard_map(
        shards,
        mesh=mesh,
        in_specs=(
            P(("dp", "tensor"), None),
            P(("dp", "tensor"), None),
            P(),
            P(None, None, None, "tensor"),
            P(None, None, "tensor"),
            P(None, "tensor", None),
            P(None, None, "tensor"),
            P(None, "tensor", None),
            P(None, "tensor"),
            P(),
            P(),
        ),
        out_specs=(
            P(("dp", "tensor"), None),
            P(("dp", "tensor"), None),
            P(None, "dp", None, "tensor"),
            P(None, "tensor", "dp"),
            P(None, "dp", "tensor"),
            P(None, "tensor", "dp"),
            P(),
            P(),
            P(),
            P(),
        ),
        check_vma=False,
    )
```

time: 900 us -> 346 us (0.38)
  waiting for transfers between devices: 693 us -> 76 us
  starting transfers between devices: 31.1 us -> 81.2 us
  blocking collectives: 46.3 us -> 0 us
  other arithmetic: 31 us -> 75 us
  local copies, waits for them, and re-layouts: 47.5 us -> 72.5 us
  between operations: 16 us -> 3.6 us
    unnamed x16 -> x0, waiting for transfers between devices: 296 us -> none
    reduce_scatter x9 -> x0, waiting for transfers between devices: 247 us -> none  [the longest x1 103 us: shards(): lax.psum_scatter(stacked[2], 'dp', scatter_dimension=1, tiled=True)]
    psum x1 -> x0, waiting for transfers between devices: 124 us -> none  [shards(): lax.psum((small_stack[0], small_stack[1], small_stack[2], small_stack[3])...]
    ppermute x0 -> x45, waiting for transfers between devices: none -> 65 us  [swapped(): return lax.ppermute(array, axis, [(i, i ^ bit) for i in range(length)])]
    ppermute x0 -> x45, starting transfers between devices: none -> 48 us  [swapped(): return lax.ppermute(array, axis, [(i, i ^ bit) for i in range(length)])]
    all_gather x8 -> x0, blocking collectives: 46.3 us -> none  [the longest x2 12.4 us: layer_forward(): act1 = lax.all_gather(normed1.astype(bf16), 'tensor', axis=0, tiled=True)]
    convert_element_type x10 -> x44, other arithmetic: 2.08 us -> 28.6 us  [the longest x16 8.35 us: tensor_sum(): rounded = total.astype(bf16)]
    unnamed x177 -> x352, local copies, waits for them, and re-layouts: 33.8 us -> 8.47 us
  transfers between devices with their start and end apart: 25 -> 57, of which waited for: 20 -> 25; matrix products, arithmetic and copies ran while one was open for 6% -> 41% of each run, Pallas kernels for 0% -> 0%
where the time goes in v1:
time: 346 us; the launch traced here: 343 us
  starting transfers between devices  81.2 us (23%)
  waiting for transfers between devices  76 us (22%)
  other arithmetic  75 us (22%)
  local copies, waits for them, and re-layouts  72.5 us (21%)
  matrix products  35.3 us (10%)
  between operations  3.6 us (1%)
    ppermute x45, waiting for transfers between devices, swapped(): return lax.ppermute(array, axis, [(i, i ^ bit) for i in range(length)])  65 us
    ppermute x45, starting transfers between devices, swapped(): return lax.ppermute(array, axis, [(i, i ^ bit) for i in range(length)])  48 us
    ppermute x12, starting transfers between devices, shifted(): return lax.ppermute(array, axis, pairs)  33.2 us
    dot_general x16, matrix products, products(): lax.dot_general(chosen, right, (((0,), (0,)), ((), ())), preferred_elemen...  12.8 us
    ppermute x12, waiting for transfers between devices, shifted(): return lax.ppermute(array, axis, pairs)  11 us
    unnamed x352, local copies, waits for them, and re-layouts  8.47 us
    convert_element_type x16, other arithmetic, tensor_sum(): rounded = total.astype(bf16)  8.35 us
    dynamic_slice x12, local copies, waits for them, and re-layouts, pick(): return lax.dynamic_index_in_dim(array, at, axis, keepdims=False)  7.68 us
  transfers between devices with their start and end apart: 57, of which 25 were waited for; matrix products, arithmetic and copies ran while one was open for 41% of the time, Pallas kernels for 0%

profile of v1, /device:TPU:0, one launch (start us, length us, event | category | flops | bytes accessed | tf_op | source)
XLA Modules:
  0.0 343.5 jit_solution(17771645283413253307)
XLA Ops:
  0.7 3.0 collective-permute-start
  20.6 3.9 %collective-permute-start.4 = (bf16[128,384]{0,1:T(8,128)(2,1)S(1)}, bf16[128,384]{0,1:T(8,128)(2,1)S(1)}, u32[]{:S(2)}, u32[]{:S(2)}) collective-permute-start(bf16[128,384]{0,1:T(8,128)(2,1)S(1)} %pad_maximum_fusion.20), channel_id=1, source_target_pairs={{0,4},{4,8},{8,12},{12,16},{16,20},{20,24},{24,28},{1,5},{5,9},{9,... | collective-permute-start | bytes 294920 | tf_op jit(solution)/shard_map/ppermute | solution.py:22
  24.5 3.5 %collective-permute-start.3 = (bf16[128,384]{0,1:T(8,128)(2,1)S(1)}, bf16[128,384]{0,1:T(8,128)(2,1)S(1)}, u32[]{:S(2)}, u32[]{:S(2)}) collective-permute-start(bf16[128,384]{0,1:T(8,128)(2,1)S(1)} %pad_maximum_fusion.20), channel_id=1, source_target_pairs={{0,8},{4,12},{8,16},{12,20},{16,24},{20,28},{1,9},{5,13},{9,17},{1... | collective-permute-start | bytes 294920 | tf_op jit(solution)/shard_map/ppermute | solution.py:22
  28.0 4.4 %collective-permute-start.2 = (bf16[128,384]{0,1:T(8,128)(2,1)S(1)}, bf16[128,384]{0,1:T(8,128)(2,1)S(1)}, u32[]{:S(2)}, u32[]{:S(2)}) collective-permute-start(bf16[128,384]{0,1:T(8,128)(2,1)S(1)} %pad_maximum_fusion.20), channel_id=1, source_target_pairs={{0,12},{4,16},{8,20},{12,24},{16,28},{1,13},{5,17},{9,21},{13,25},... | collective-permute-start | bytes 294920 | tf_op jit(solution)/shard_map/ppermute | solution.py:22
  62.0 3.4 collective-permute-start.13
  65.4 4.3 %collective-permute-start.12 = (bf16[128,384]{0,1:T(8,128)(2,1)S(1)}, bf16[128,384]{0,1:T(8,128)(2,1)S(1)}, u32[]{:S(2)}, u32[]{:S(2)}) collective-permute-start(bf16[128,384]{0,1:T(8,128)(2,1)S(1)} %pad_maximum_fusion.21), channel_id=1, source_target_pairs={{0,8},{4,12},{8,16},{12,20},{16,24},{20,28},{1,9},{5,13},{9,17},{1... | collective-permute-start | bytes 294920 | tf_op jit(solution)/shard_map/ppermute | solution.py:22
  69.7 5.4 %collective-permute-start.11 = (bf16[128,384]{0,1:T(8,128)(2,1)S(1)}, bf16[128,384]{0,1:T(8,128)(2,1)S(1)}, u32[]{:S(2)}, u32[]{:S(2)}) collective-permute-start(bf16[128,384]{0,1:T(8,128)(2,1)S(1)} %pad_maximum_fusion.21), channel_id=1, source_target_pairs={{0,12},{4,16},{8,20},{12,24},{16,28},{1,13},{5,17},{9,21},{13,25},... | collective-permute-start | bytes 294920 | tf_op jit(solution)/shard_map/ppermute | solution.py:22
  143.7 3.8 %collective-permute-done.27 = bf16[128,384]{0,1:T(8,128)(2,1)S(1)} collective-permute-done((bf16[128,384]{0,1:T(8,128)(2,1)S(1)}, bf16[128,384]{0,1:T(8,128)(2,1)S(1)}, u32[]{:S(2)}, u32[]{:S(2)}) %collective-permute-start.27) | collective-permute-done | bytes 98336 | tf_op jit(solution)/shard_map/ppermute | solution.py:22
  158.8 2.9 collective-permute-done.29
  168.1 2.8 fusion.148
  180.6 3.3 collective-permute-start.43
  203.7 2.8 fusion.144
  223.6 3.5 %collective-permute-start.46 = (bf16[384,1536]{1,0:T(8,128)(2,1)}, bf16[384,1536]{1,0:T(8,128)(2,1)}, u32[]{:S(2)}, u32[]{:S(2)}) collective-permute-start(bf16[384,1536]{1,0:T(8,128)(2,1)} %pad_maximum_fusion), channel_id=1, source_target_pairs={{0,4},{4,0},{8,12},{12,8},{16,20},{20,16},{24,28},{28,24},{1,5},{5... | collective-permute-start | bytes 3538952 | tf_op jit(solution)/shard_map/ppermute | solution.py:27
  238.1 2.6 collective-permute-done.38
  242.5 2.9 collective-permute-start.44
  254.4 12.6 %collective-permute-done.54 = f32[24,768]{1,0:T(8,128)S(1)} collective-permute-done((f32[24,768]{1,0:T(8,128)S(1)}, f32[24,768]{1,0:T(8,128)S(1)}, u32[]{:S(2)}, u32[]{:S(2)}) %collective-permute-start.54) | collective-permute-done | bytes 73760 | tf_op jit(solution)/shard_map/ppermute | solution.py:27
  267.1 2.9 collective-permute-start.55
  270.6 4.4 %collective-permute-start.45 = (bf16[1,96,768]{2,1,0:T(8,128)(2,1)}, bf16[1,96,768]{2,1,0:T(8,128)(2,1)}, u32[]{:S(2)}, u32[]{:S(2)}) collective-permute-start(bf16[1,96,768]{2,1,0:T(8,128)(2,1)} %dynamic-slice_convert_fusion.3), channel_id=1, source_target_pairs={{0,16},{4,20},{8,24},{12,28},{16,0},{20,4},{24,8},{28,12},{1,17},{... | collective-permute-start | bytes 442376 | tf_op jit(solution)/shard_map/ppermute | solution.py:27
  296.4 2.8 collective-permute-start.42
  300.7 9.3 %collective-permute-done.42 = bf16[1,96,768]{2,1,0:T(8,128)(2,1)S(1)} collective-permute-done((bf16[1,96,768]{2,1,0:T(8,128)(2,1)S(1)}, bf16[1,96,768]{2,1,0:T(8,128)(2,1)S(1)}, u32[]{:S(2)}, u32[]{:S(2)}) %collective-permute-start.42) | collective-permute-done | bytes 147488 | tf_op jit(solution)/shard_map/ppermute | solution.py:27
  315.4 3.4 %collective-permute-start.51 = (bf16[1,96,1536]{2,1,0:T(8,128)(2,1)S(1)}, bf16[1,96,1536]{2,1,0:T(8,128)(2,1)S(1)}, u32[]{:S(2)}, u32[]{:S(2)}) collective-permute-start(bf16[1,96,1536]{2,1,0:T(8,128)(2,1)S(1)} %dynamic-slice_convert_fusion), channel_id=1, source_target_pairs={{0,16},{4,20},{8,24},{12,28},{16,0},{20,4},{24,8},{28,12},{1,17},{... | collective-permute-start | bytes 884744 | tf_op jit(solution)/shard_map/ppermute | solution.py:27
  318.8 9.1 %collective-permute-done.47 = bf16[2,96,1536]{2,1,0:T(8,128)(2,1)} collective-permute-done((bf16[2,96,1536]{2,1,0:T(8,128)(2,1)}, bf16[2,96,1536]{2,1,0:T(8,128)(2,1)}, u32[]{:S(2)}, u32[]{:S(2)}) %collective-permute-start.47) | collective-permute-done | bytes 589856 | tf_op jit(solution)/shard_map/ppermute | solution.py:27
  329.2 3.2 collective-permute-done.51
  332.5 9.1 %collective-permute-done.48 = bf16[1,96,1536]{2,1,0:T(8,128)(2,1)S(1)} collective-permute-done((bf16[1,96,1536]{2,1,0:T(8,128)(2,1)S(1)}, bf16[1,96,1536]{2,1,0:T(8,128)(2,1)S(1)}, u32[]{:S(2)}, u32[]{:S(2)}) %collective-permute-start.48) | collective-permute-done | bytes 294944 | tf_op jit(solution)/shard_map/ppermute | solution.py:27
  (752 shorter events, 230.5 us)
Async XLA Ops:
  0.7 16.6 %collective-permute-start = (bf16[32,768]{1,0:T(8,128)(2,1)}, bf16[32,768]{1,0:T(8,128)(2,1)S(1)}, u32[]{:S(2)}, u32[]{:S(2)}) collective-permute-start(bf16[32,768]{1,0:T(8,128)(2,1)} %param.11), channel_id=1, source_target_pairs={{0,2},{1,3},{2,0},{3,1},{4,6},{5,7},{6,4},{7,5},{8,10},{9,11},{10,... | collective-permute-start | bytes 147464 | tf_op jit(solution)/shard_map/ppermute | solution.py:27
  3.7 14.5 %collective-permute-start.20 = (bf16[32,768]{1,0:T(8,128)(2,1)}, bf16[32,768]{1,0:T(8,128)(2,1)S(1)}, u32[]{:S(2)}, u32[]{:S(2)}) collective-permute-start(bf16[32,768]{1,0:T(8,128)(2,1)} %param.12), channel_id=1, source_target_pairs={{0,2},{1,3},{2,0},{3,1},{4,6},{5,7},{6,4},{7,5},{8,10},{9,11},{10,... | collective-permute-start | bytes 147464 | tf_op jit(solution)/shard_map/ppermute | solution.py:27
  20.6 12.1 %collective-permute-start.4 = (bf16[128,384]{0,1:T(8,128)(2,1)S(1)}, bf16[128,384]{0,1:T(8,128)(2,1)S(1)}, u32[]{:S(2)}, u32[]{:S(2)}) collective-permute-start(bf16[128,384]{0,1:T(8,128)(2,1)S(1)} %pad_maximum_fusion.20), channel_id=1, source_target_pairs={{0,4},{4,8},{8,12},{12,16},{16,20},{20,24},{24,28},{1,5},{5,9},{9,... | collective-permute-start | bytes 294920 | tf_op jit(solution)/shard_map/ppermute | solution.py:22
  37.2 11.2 %collective-permute-start.21 = (bf16[2,32,768]{2,1,0:T(8,128)(2,1)}, bf16[2,32,768]{2,1,0:T(8,128)(2,1)}, u32[]{:S(2)}, u32[]{:S(2)}) collective-permute-start(bf16[2,32,768]{2,1,0:T(8,128)(2,1)} %pad_maximum_fusion.22), channel_id=1, source_target_pairs={{0,1},{1,0},{2,3},{3,2},{4,5},{5,4},{6,7},{7,6},{8,9},{9,8},{10,11... | collective-permute-start | bytes 294920 | tf_op jit(solution)/shard_map/ppermute | solution.py:27
  62.0 14.4 %collective-permute-start.13 = (bf16[128,384]{0,1:T(8,128)(2,1)S(1)}, bf16[128,384]{0,1:T(8,128)(2,1)S(1)}, u32[]{:S(2)}, u32[]{:S(2)}) collective-permute-start(bf16[128,384]{0,1:T(8,128)(2,1)S(1)} %pad_maximum_fusion.21), channel_id=1, source_target_pairs={{0,4},{4,8},{8,12},{12,16},{16,20},{20,24},{24,28},{1,5},{5,9},{9,... | collective-permute-start | bytes 294920 | tf_op jit(solution)/shard_map/ppermute | solution.py:22
  65.4 11.0 %collective-permute-start.12 = (bf16[128,384]{0,1:T(8,128)(2,1)S(1)}, bf16[128,384]{0,1:T(8,128)(2,1)S(1)}, u32[]{:S(2)}, u32[]{:S(2)}) collective-permute-start(bf16[128,384]{0,1:T(8,128)(2,1)S(1)} %pad_maximum_fusion.21), channel_id=1, source_target_pairs={{0,8},{4,12},{8,16},{12,20},{16,24},{20,28},{1,9},{5,13},{9,17},{1... | collective-permute-start | bytes 294920 | tf_op jit(solution)/shard_map/ppermute | solution.py:22
  107.2 14.2 %collective-permute-start.17 = (bf16[64,768]{1,0:T(8,128)(2,1)}, bf16[64,768]{1,0:T(8,128)(2,1)}, u32[]{:S(2)}, u32[]{:S(2)}) collective-permute-start(bf16[64,768]{1,0:T(8,128)(2,1)} %select_convert_fusion.4), channel_id=1, source_target_pairs={{0,1},{1,0},{2,3},{3,2},{4,5},{5,4},{6,7},{7,6},{8,9},{9,8},{10,11... | collective-permute-start | bytes 294920 | tf_op jit(solution)/shard_map/ppermute | solution.py:27
  128.1 14.6 %collective-permute-start.19 = (bf16[64,768]{1,0:T(8,128)(2,1)}, bf16[64,768]{1,0:T(8,128)(2,1)}, u32[]{:S(2)}, u32[]{:S(2)}) collective-permute-start(bf16[64,768]{1,0:T(8,128)(2,1)} %add_convert_fusion.17), channel_id=1, source_target_pairs={{0,1},{1,0},{2,3},{3,2},{4,5},{5,4},{6,7},{7,6},{8,9},{9,8},{10,11... | collective-permute-start | bytes 294920 | tf_op jit(solution)/shard_map/ppermute | solution.py:27
  173.7 17.6 %collective-permute-start.31 = (bf16[64,768]{1,0:T(8,128)(2,1)S(1)}, bf16[64,768]{1,0:T(8,128)(2,1)S(1)}, u32[]{:S(2)}, u32[]{:S(2)}) collective-permute-start(bf16[64,768]{1,0:T(8,128)(2,1)S(1)} %select_convert_fusion.1), channel_id=1, source_target_pairs={{0,1},{1,0},{2,3},{3,2},{4,5},{5,4},{6,7},{7,6},{8,9},{9,8},{10,11... | collective-permute-start | bytes 294920 | tf_op jit(solution)/shard_map/ppermute | solution.py:27
  180.6 55.9 %collective-permute-start.43 = (bf16[384,768]{0,1:T(8,128)(2,1)}, bf16[384,768]{0,1:T(8,128)(2,1)}, u32[]{:S(2)}, u32[]{:S(2)}) collective-permute-start(bf16[384,768]{0,1:T(8,128)(2,1)} %pad_maximum_fusion.5), channel_id=1, source_target_pairs={{0,4},{4,0},{8,12},{12,8},{16,20},{20,16},{24,28},{28,24},{1,5},{5... | collective-permute-start | bytes 1769480 | tf_op jit(solution)/shard_map/ppermute | solution.py:27
  186.8 103.2 %collective-permute-start.49 = (bf16[384,1536]{1,0:T(8,128)(2,1)}, bf16[384,1536]{1,0:T(8,128)(2,1)}, u32[]{:S(2)}, u32[]{:S(2)}) collective-permute-start(bf16[384,1536]{1,0:T(8,128)(2,1)} %pad_maximum_fusion.1), channel_id=1, source_target_pairs={{0,4},{4,0},{8,12},{12,8},{16,20},{20,16},{24,28},{28,24},{1,5},{5... | collective-permute-start | bytes 3538952 | tf_op jit(solution)/shard_map/ppermute | solution.py:27
  214.7 12.4 %collective-permute-start.35 = (bf16[128,384]{0,1:T(8,128)(2,1)S(1)}, bf16[128,384]{0,1:T(8,128)(2,1)}, u32[]{:S(2)}, u32[]{:S(2)}) collective-permute-start(bf16[128,384]{0,1:T(8,128)(2,1)S(1)} %get-tuple-element.102), channel_id=1, source_target_pairs={{8,0},{12,4},{16,8},{20,12},{24,16},{28,20},{9,1},{13,5},{17,9},{2... | collective-permute-start | bytes 294920 | tf_op jit(solution)/shard_map/ppermute | solution.py:22
  216.0 11.8 %collective-permute-start.34 = (bf16[128,384]{0,1:T(8,128)(2,1)S(1)}, bf16[128,384]{0,1:T(8,128)(2,1)}, u32[]{:S(2)}, u32[]{:S(2)}) collective-permute-start(bf16[128,384]{0,1:T(8,128)(2,1)S(1)} %get-tuple-element.100), channel_id=1, source_target_pairs={{4,0},{8,4},{12,8},{16,12},{20,16},{24,20},{28,24},{5,1},{9,5},{13... | collective-permute-start | bytes 294920 | tf_op jit(solution)/shard_map/ppermute | solution.py:22
  223.6 69.2 %collective-permute-start.46 = (bf16[384,1536]{1,0:T(8,128)(2,1)}, bf16[384,1536]{1,0:T(8,128)(2,1)}, u32[]{:S(2)}, u32[]{:S(2)}) collective-permute-start(bf16[384,1536]{1,0:T(8,128)(2,1)} %pad_maximum_fusion), channel_id=1, source_target_pairs={{0,4},{4,0},{8,12},{12,8},{16,20},{20,16},{24,28},{28,24},{1,5},{5... | collective-permute-start | bytes 3538952 | tf_op jit(solution)/shard_map/ppermute | solution.py:27
  231.9 46.3 %collective-permute-start.40 = (bf16[384,768]{0,1:T(8,128)(2,1)S(1)}, bf16[384,768]{0,1:T(8,128)(2,1)}, u32[]{:S(2)}, u32[]{:S(2)}) collective-permute-start(bf16[384,768]{0,1:T(8,128)(2,1)S(1)} %pad_maximum_fusion.4), channel_id=1, source_target_pairs={{0,4},{4,0},{8,12},{12,8},{16,20},{20,16},{24,28},{28,24},{1,5},{5... | collective-permute-start | bytes 1769480 | tf_op jit(solution)/shard_map/ppermute | solution.py:27
  242.5 10.9 %collective-permute-start.44 = (bf16[2,96,768]{2,1,0:T(8,128)(2,1)}, bf16[2,96,768]{2,1,0:T(8,128)(2,1)}, u32[]{:S(2)}, u32[]{:S(2)}) collective-permute-start(bf16[2,96,768]{2,1,0:T(8,128)(2,1)} %fusion.59), channel_id=1, source_target_pairs={{0,8},{4,12},{8,0},{12,4},{16,24},{20,28},{24,16},{28,20},{1,9},{5... | collective-permute-start | bytes 884744 | tf_op jit(solution)/shard_map/ppermute | solution.py:27
  251.8 15.3 %collective-permute-start.54 = (f32[24,768]{1,0:T(8,128)S(1)}, f32[24,768]{1,0:T(8,128)S(1)}, u32[]{:S(2)}, u32[]{:S(2)}) collective-permute-start(f32[24,768]{1,0:T(8,128)S(1)} %add.1366), channel_id=1, source_target_pairs={{0,4},{4,0},{8,12},{12,8},{16,20},{20,16},{24,28},{28,24},{1,5},{5... | collective-permute-start | bytes 221192 | tf_op jit(solution)/shard_map/ppermute | solution.py:27
  270.6 13.1 %collective-permute-start.45 = (bf16[1,96,768]{2,1,0:T(8,128)(2,1)}, bf16[1,96,768]{2,1,0:T(8,128)(2,1)}, u32[]{:S(2)}, u32[]{:S(2)}) collective-permute-start(bf16[1,96,768]{2,1,0:T(8,128)(2,1)} %dynamic-slice_convert_fusion.3), channel_id=1, source_target_pairs={{0,16},{4,20},{8,24},{12,28},{16,0},{20,4},{24,8},{28,12},{1,17},{... | collective-permute-start | bytes 442376 | tf_op jit(solution)/shard_map/ppermute | solution.py:27
  280.6 14.5 %collective-permute-start.41 = (bf16[2,96,768]{2,1,0:T(8,128)(2,1)}, bf16[2,96,768]{2,1,0:T(8,128)(2,1)}, u32[]{:S(2)}, u32[]{:S(2)}) collective-permute-start(bf16[2,96,768]{2,1,0:T(8,128)(2,1)} %fusion.58), channel_id=1, source_target_pairs={{0,8},{4,12},{8,0},{12,4},{16,24},{20,28},{24,16},{28,20},{1,9},{5... | collective-permute-start | bytes 884744 | tf_op jit(solution)/shard_map/ppermute | solution.py:27
  292.9 21.1 %collective-permute-start.50 = (bf16[2,96,1536]{2,1,0:T(8,128)(2,1)}, bf16[2,96,1536]{2,1,0:T(8,128)(2,1)}, u32[]{:S(2)}, u32[]{:S(2)}) collective-permute-start(bf16[2,96,1536]{2,1,0:T(8,128)(2,1)} %fusion.37), channel_id=1, source_target_pairs={{0,8},{4,12},{8,0},{12,4},{16,24},{20,28},{24,16},{28,20},{1,9},{5... | collective-permute-start | bytes 1769480 | tf_op jit(solution)/shard_map/ppermute | solution.py:27
  296.4 13.6 %collective-permute-start.42 = (bf16[1,96,768]{2,1,0:T(8,128)(2,1)S(1)}, bf16[1,96,768]{2,1,0:T(8,128)(2,1)S(1)}, u32[]{:S(2)}, u32[]{:S(2)}) collective-permute-start(bf16[1,96,768]{2,1,0:T(8,128)(2,1)S(1)} %dynamic-slice_convert_fusion.4), channel_id=1, source_target_pairs={{0,16},{4,20},{8,24},{12,28},{16,0},{20,4},{24,8},{28,12},{1,17},{... | collective-permute-start | bytes 442376 | tf_op jit(solution)/shard_map/ppermute | solution.py:27
  300.1 27.8 %collective-permute-start.47 = (bf16[2,96,1536]{2,1,0:T(8,128)(2,1)}, bf16[2,96,1536]{2,1,0:T(8,128)(2,1)}, u32[]{:S(2)}, u32[]{:S(2)}) collective-permute-start(bf16[2,96,1536]{2,1,0:T(8,128)(2,1)} %fusion.36), channel_id=1, source_target_pairs={{0,8},{4,12},{8,0},{12,4},{16,24},{20,28},{24,16},{28,20},{1,9},{5... | collective-permute-start | bytes 1769480 | tf_op jit(solution)/shard_map/ppermute | solution.py:27
  315.4 17.0 %collective-permute-start.51 = (bf16[1,96,1536]{2,1,0:T(8,128)(2,1)S(1)}, bf16[1,96,1536]{2,1,0:T(8,128)(2,1)S(1)}, u32[]{:S(2)}, u32[]{:S(2)}) collective-permute-start(bf16[1,96,1536]{2,1,0:T(8,128)(2,1)S(1)} %dynamic-slice_convert_fusion), channel_id=1, source_target_pairs={{0,16},{4,20},{8,24},{12,28},{16,0},{20,4},{24,8},{28,12},{1,17},{... | collective-permute-start | bytes 884744 | tf_op jit(solution)/shard_map/ppermute | solution.py:27
  329.1 12.5 %collective-permute-start.48 = (bf16[1,96,1536]{2,1,0:T(8,128)(2,1)S(1)}, bf16[1,96,1536]{2,1,0:T(8,128)(2,1)S(1)}, u32[]{:S(2)}, u32[]{:S(2)}) collective-permute-start(bf16[1,96,1536]{2,1,0:T(8,128)(2,1)S(1)} %dynamic-slice_convert_fusion.1), channel_id=1, source_target_pairs={{0,16},{4,20},{8,24},{12,28},{16,0},{20,4},{24,8},{28,12},{1,17},{... | collective-permute-start | bytes 884744 | tf_op jit(solution)/shard_map/ppermute | solution.py:27
  (208 other events, 922.3 us)

commit v2 on v0

v2 whole, which is shorter than its diff:
```python
import jax
import jax.numpy as jnp
from jax import lax
from jax.experimental import pallas as pl
from jax.experimental.pallas import tpu as pltpu
from jax.sharding import PartitionSpec as P

D = 768
HD = 64
FF = 3072
LAYERS = 2
SPAN = 4

epsilon = 1e-05
gelu_c = 0.7978845608028654
f32 = jnp.float32
bf16 = jnp.bfloat16
VMEM_LIMIT = 28 * 1024 * 1024


def shifted(array, axis, by):
    length = lax.axis_size(axis)
    pairs = [(i, i + by) for i in range(length) if 0 <= i + by < length]
    return lax.ppermute(array, axis, pairs)


def swapped(array, axis, bit):
    length = lax.axis_size(axis)
    return lax.ppermute(array, axis, [(i, i ^ bit) for i in range(length)])


def bits_of(axis):
    length = lax.axis_size(axis)
    found, bit = [], 1
    while bit < length:
        found.append(bit)
        bit *= 2
    assert bit == length
    return found


def call(kernel, outs, args, flops=1e8):
    spec = pl.BlockSpec(memory_space=pltpu.VMEM)
    shapes = [jax.ShapeDtypeStruct(shape, dtype) for shape, dtype in outs]
    moved = sum(a.size * a.dtype.itemsize for a in args)
    moved += sum(s.size * s.dtype.itemsize for s in shapes)
    return pl.pallas_call(
        kernel,
        out_shape=shapes,
        in_specs=[spec] * len(args),
        out_specs=[spec] * len(outs),
        compiler_params=pltpu.CompilerParams(vmem_limit_bytes=VMEM_LIMIT),
        cost_estimate=pl.CostEstimate(
            flops=int(flops), bytes_accessed=int(moved), transcendentals=0
        ),
    )(*args)


def mm(left, right, contract=((1,), (0,))):
    return lax.dot_general(left, right, (contract, ((), ())), preferred_element_type=f32)


NT = ((1,), (1,))
TN = ((0,), (0,))


def normalize(values_in):
    mean_v = jnp.mean(values_in, axis=-1, keepdims=True)
    centred = values_in - mean_v
    var_v = jnp.mean(centred * centred, axis=-1, keepdims=True)
    rstd = lax.rsqrt(var_v + epsilon)
    return (centred * rstd, rstd)


def norm_bwd(grad_in, normed, rstd, gain):
    scaled = grad_in * gain
    inner = jnp.mean(scaled, axis=-1, keepdims=True)
    along = jnp.mean(scaled * normed, axis=-1, keepdims=True)
    return rstd * (scaled - inner - normed * along)


def column_sum(values_in):
    return jnp.sum(values_in, axis=0, keepdims=True)


def gelu_pair(pre_act):
    inner = gelu_c * (pre_act + 0.044715 * pre_act * pre_act * pre_act)
    tanh_v = jnp.tanh(inner)
    value_out = 0.5 * pre_act * (1.0 + tanh_v)
    slope = 0.5 * (1.0 + tanh_v) + 0.5 * pre_act * (1.0 - tanh_v * tanh_v) * gelu_c * (
        1.0 + 3.0 * 0.044715 * pre_act * pre_act
    )
    return (value_out, slope)


def joined(own_ref, other_ref):
    return own_ref[...].astype(f32) + other_ref[...].astype(f32)


def place_pieces(pieces, out_ref):
    mine = lax.axis_index("tensor")
    rows = pieces[0].shape[0]
    for number, piece in enumerate(pieces):
        start = pl.multiple_of((mine ^ number) * rows, rows)
        out_ref[pl.ds(start, rows), :] = piece[...].astype(out_ref.dtype)


def gathered(piece):
    pieces = {0: piece}
    for bit in bits_of("tensor")[::-1]:
        for number in list(pieces):
            pieces[number ^ bit] = swapped(pieces[number], "tensor", bit)
    return [pieces[number] for number in range(len(pieces))]


def exchanged(part):
    bits = bits_of("tensor")
    for bit in bits[:-1]:
        other = swapped(part, "tensor", bit)
        part = (part.astype(f32) + other.astype(f32)).astype(bf16)
    return [part, swapped(part, "tensor", bits[-1])]


def project_rows(hidden, layer, refs, outs):
    gains, biases, w_qkv, qv_bias, pick = refs
    h_ref, picked_ref, q_ref, kv_ref = outs
    width = q_ref.shape[1]
    hat, _ = normalize(hidden)
    act = (hat * gains[layer, 0:1] + biases[layer, 0:1]).astype(bf16)
    kv = mm(act, w_qkv[layer, width:], NT)
    values = kv[:, width:] + qv_bias[layer, 1:2]
    kv_ref[...] = jnp.concatenate([kv[:, :width], values], axis=1).astype(bf16)
    query = mm(act, w_qkv[layer, :width], NT)
    q_ref[...] = (query + qv_bias[layer, 0:1]).astype(bf16)
    picked_ref[...] = mm(act, pick[...]).astype(bf16)


def project_first(pieces, params, pick):
    count = len(pieces)
    rows = count * pieces[0].shape[0]
    width = params["w_out"].shape[1]

    def kernel(*refs):
        ins, outs = refs[: count + 5], refs[count + 5 :]
        place_pieces(ins[:count], outs[0])
        project_rows(outs[0][...], 0, ins[count:], outs)

    return call(
        kernel,
        [((rows, D), f32), ((rows, D), bf16), ((rows, width), bf16), ((rows, 2 * width), bf16)],
        [*pieces, *[params[k] for k in ("gains", "biases", "w_qkv", "qv_bias")], pick],
    )


def project_next(mid, pair, layer, params, pick):
    rows = mid.shape[0]
    width = params["w_out"].shape[1]

    def kernel(mid_ref, own_ref, other_ref, *refs):
        ins, outs = refs[:5], refs[5:]
        hidden = mid_ref[...] + joined(own_ref, other_ref) + ins[1][layer - 1, 3:4]
        outs[0][...] = hidden
        project_rows(hidden, layer, ins, outs)

    return call(
        kernel,
        [((rows, D), f32), ((rows, D), bf16), ((rows, width), bf16), ((rows, 2 * width), bf16)],
        [mid, *pair, *[params[k] for k in ("gains", "biases", "w_qkv", "qv_bias")], pick],
    )


def head_lanes(shape, head):
    lane = lax.broadcasted_iota(jnp.int32, shape, 1)
    return (lane >= head * HD) & (lane < (head + 1) * HD)


def allowed_of(seg_q, seg_k, rows):
    shape = (rows, SPAN * rows)
    query = lax.broadcasted_iota(jnp.int32, shape, 0)
    key = lax.broadcasted_iota(jnp.int32, shape, 1)
    return (key <= query + (SPAN - 1) * rows) & (seg_q[...] == seg_k[...])


def attend(q, kv_parts, segs, layer, params):
    rows, width = q.shape
    heads = width // HD

    def kernel(q_ref, *refs):
        kv_refs, (seg_q, seg_k, w_out, att_ref, lse_ref, part_ref) = refs[:SPAN], refs[SPAN:]
        allowed = allowed_of(seg_q, seg_k, rows)
        kv_all = jnp.concatenate([r[...] for r in kv_refs], axis=0)
        keys, values = kv_all[:, :width], kv_all[:, width:]
        query = q_ref[...]
        mixed = jnp.zeros((rows, width), f32)
        logs = jnp.zeros((rows, 128), f32)
        lane = lax.broadcasted_iota(jnp.int32, (rows, 128), 1)
        for head in range(heads):
            inside = head_lanes((rows, width), head)
            scores = mm(jnp.where(inside, query, 0), keys, NT) * HD ** (-0.5)
            scores = jnp.where(allowed, scores, -1e30)
            top = jnp.max(scores, axis=-1, keepdims=True)
            log_total = top + jnp.log(jnp.sum(jnp.exp(scores - top), axis=-1, keepdims=True))
            weights = jnp.exp(scores - log_total).astype(bf16)
            mixed = jnp.where(inside, mm(weights, values), mixed)
            logs = jnp.where(lane == head, log_total, logs)
        att = mixed.astype(bf16)
        att_ref[...] = att
        lse_ref[...] = logs
        part_ref[...] = mm(att, w_out[layer]).astype(bf16)

    return call(
        kernel,
        [((rows, width), bf16), ((rows, 128), f32), ((rows, D), bf16)],
        [q, *kv_parts, *segs, params["w_out"]],
    )


def feed_forward(hidden, pair, picked1, att, layer, params, pick):
    rows, width = att.shape
    half = D // 2
    inner = params["w_up"].shape[2]
    pad = -(2 * half + inner + width) % 128

    def kernel(h_ref, own_ref, other_ref, p1_ref, att_ref, gains, biases, up, down, ffb, pick_ref,
               mid_ref, slope_ref, sent_ref, kept_ref, part_ref):
        mid = h_ref[...] + joined(own_ref, other_ref) + biases[layer, 1:2]
        mid_ref[...] = mid
        hat, _ = normalize(mid)
        act2 = (hat * gains[layer, 1:2] + biases[layer, 2:3]).astype(bf16)
        pre = mm(act2, up[layer]) + ffb[layer : layer + 1]
        value, slope = gelu_pair(pre)
        act3 = value.astype(bf16)
        part_ref[...] = mm(act3, down[layer]).astype(bf16)
        slope_ref[...] = slope
        picked2 = mm(act2, pick_ref[...]).astype(bf16)
        kept_ref[:, :half] = p1_ref[:, :half]
        kept_ref[:, half:] = picked2[:, :half]
        sent_ref[:, :half] = p1_ref[:, half:]
        sent_ref[:, half : 2 * half] = picked2[:, half:]
        sent_ref[:, 2 * half : 2 * half + inner] = act3
        sent_ref[:, 2 * half + inner : 2 * half + inner + width] = att_ref[...]
        if pad:
            sent_ref[:, 2 * half + inner + width :] = jnp.zeros((rows, pad), bf16)

    return call(
        kernel,
        [
            ((rows, D), f32),
            ((rows, inner), f32),
            ((rows, 2 * half + inner + width + pad), bf16),
            ((rows, D), bf16),
            ((rows, D), bf16),
        ],
        [hidden, *pair, picked1, att]
        + [params[k] for k in ("gains", "biases", "w_up", "w_down", "ff_bias")]
        + [pick],
    )


def last_rows(mid, pair, params, own_rows):
    def kernel(mid_ref, own_ref, other_ref, biases, out_ref):
        start = pl.multiple_of(lax.axis_index("tensor") * own_rows, own_rows)
        here = pl.ds(start, own_rows)
        total = mid_ref[here, :] + own_ref[here, :].astype(f32) + other_ref[here, :].astype(f32)
        out_ref[...] = (total + biases[LAYERS - 1, 3:4]).astype(bf16)

    return call(kernel, [((own_rows, D), bf16)], [mid, *pair, params["biases"]])[0]


def norm1_grad(gmid_ref, own_ref, other_ref, h_ref, gains, layer):
    d_norm = joined(own_ref, other_ref)
    hat, rstd = normalize(h_ref[...])
    grad = gmid_ref[...] + norm_bwd(d_norm, hat, rstd, gains[layer, 0:1])
    return grad, column_sum(d_norm * hat), column_sum(d_norm)


def mlp_grad(grad, layer, refs, outs):
    slope_ref, up, down, pick_ref = refs
    sent_ref, part_ref, small_ref, kept_ref = outs
    half = D // 2
    grad_b = grad.astype(bf16)
    d_pre = mm(grad_b, down[layer], NT) * slope_ref[...]
    pre_b = d_pre.astype(bf16)
    part_ref[...] = mm(pre_b, up[layer], NT).astype(bf16)
    picked = mm(grad_b, pick_ref[...]).astype(bf16)
    kept_ref[...] = picked[:, :half]
    sent_ref[:, :half] = picked[:, half:]
    sent_ref[:, half:] = pre_b
    small_ref[0:1, :] = column_sum(d_pre)
    small_ref[1:2, :] = column_sum(grad)


def mlp_outs(rows, inner):
    assert inner == D
    return [
        ((rows, D), f32),
        ((rows, D // 2 + inner), bf16),
        ((rows, D), bf16),
        ((8, D), f32),
        ((rows, D // 2), bf16),
    ]


def mlp_grad_last(pieces, slope, params, pick):
    count = len(pieces)
    rows, inner = slope.shape

    def kernel(*refs):
        ins, outs = refs[: count + 4], refs[count + 4 :]
        place_pieces(ins[:count], outs[0])
        outs[3][...] = jnp.zeros((8, D), f32)
        mlp_grad(outs[0][...], LAYERS - 1, ins[count:], outs[1:])

    return call(
        kernel,
        mlp_outs(rows, inner),
        [*pieces, slope, params["w_up"], params["w_down"], pick],
    )


def mlp_grad_next(gmid, pair, hidden, slope, layer, params, pick):
    rows, inner = slope.shape

    def kernel(gmid_ref, own_ref, other_ref, h_ref, gains, *refs):
        ins, outs = refs[:4], refs[4:]
        grad, g_gain, g_bias = norm1_grad(gmid_ref, own_ref, other_ref, h_ref, gains, layer + 1)
        outs[0][...] = grad
        outs[3][...] = jnp.zeros((8, D), f32)
        mlp_grad(grad, layer, ins, outs[1:])
        outs[3][2:3, :] = g_gain
        outs[3][3:4, :] = g_bias

    return call(
        kernel,
        mlp_outs(rows, inner),
        [gmid, *pair, hidden, params["gains"], slope, params["w_up"], params["w_down"], pick],
    )


def attend_grad(grad, pair, mid, q, kv_parts, segs, att, lse, layer, params, pick):
    rows, width = q.shape
    heads = width // HD
    back = SPAN - 1

    def kernel(g_ref, own_ref, other_ref, mid_ref, q_ref, *refs):
        kv_refs, refs = refs[:SPAN], refs[SPAN:]
        seg_q, seg_k, att_ref, lse_ref, gains, w_out, pick_ref = refs[:7]
        gmid_ref, picked_ref, dq_ref, dkv_ref, small_ref = refs[7:12]
        away_refs = refs[12:]
        d_norm = joined(own_ref, other_ref)
        hat, rstd = normalize(mid_ref[...])
        gmid = g_ref[...] + norm_bwd(d_norm, hat, rstd, gains[layer, 1:2])
        gmid_ref[...] = gmid
        mid_b = gmid.astype(bf16)
        d_att = mm(mid_b, w_out[layer], NT).astype(bf16)
        allowed = allowed_of(seg_q, seg_k, rows)
        kv_all = jnp.concatenate([r[...] for r in kv_refs], axis=0)
        keys, values = kv_all[:, :width], kv_all[:, width:]
        query, logs = q_ref[...], lse_ref[...]
        weighed = d_att.astype(f32) * att_ref[...].astype(f32)
        d_query = jnp.zeros((rows, width), f32)
        d_keys = jnp.zeros((SPAN * rows, width), f32)
        d_values = jnp.zeros((SPAN * rows, width), f32)
        for head in range(heads):
            inside = head_lanes((rows, width), head)
            query_h = jnp.where(inside, query, 0)
            d_att_h = jnp.where(inside, d_att, 0)
            scores = mm(query_h, keys, NT) * HD ** (-0.5)
            scores = jnp.where(allowed, scores, -1e30)
            probs = jnp.exp(scores - logs[:, head : head + 1])
            delta = jnp.sum(jnp.where(inside, weighed, 0.0), axis=-1, keepdims=True)
            d_prob = mm(d_att_h, values, NT)
            d_score = (probs * (d_prob - delta) * HD ** (-0.5)).astype(bf16)
            d_query = jnp.where(inside, mm(d_score, keys), d_query)
            d_keys = d_keys + mm(d_score, query_h, TN)
            d_values = d_values + mm(probs.astype(bf16), d_att_h, TN)
        d_kv = jnp.concatenate([d_keys, d_values], axis=1)
        dq_ref[...] = d_query
        dkv_ref[...] = d_kv[back * rows :]
        for distance in range(1, SPAN):
            block = back - distance
            away_refs[distance - 1][...] = d_kv[block * rows : (block + 1) * rows].astype(bf16)
        picked_ref[...] = mm(mid_b, pick_ref[...]).astype(bf16)
        small_ref[...] = jnp.zeros((8, D), f32)
        small_ref[0:1, :] = column_sum(d_norm * hat)
        small_ref[1:2, :] = column_sum(d_norm)
        small_ref[2:3, :] = column_sum(gmid)

    return call(
        kernel,
        [
            ((rows, D), f32),
            ((rows, D), bf16),
            ((rows, width), f32),
            ((rows, 2 * width), f32),
            ((8, D), f32),
        ]
        + [((rows, 2 * width), bf16)] * back,
        [grad, *pair, mid, q, *kv_parts, *segs, att, lse]
        + [params["gains"], params["w_out"], pick],
    )


def project_grad(dq, dkv, arrived, picked, layer, params):
    rows, width = dq.shape
    half = D // 2
    pad = -(half + 3 * width) % 128

    def kernel(dq_ref, dkv_ref, *refs):
        near, (picked_ref, w_qkv, sent_ref, part_ref, small_ref) = refs[: SPAN - 1], refs[SPAN - 1 :]
        d_kv = dkv_ref[...]
        for ref in near:
            d_kv = d_kv + ref[...].astype(f32)
        d_query = dq_ref[...]
        query_b, kv_b = d_query.astype(bf16), d_kv.astype(bf16)
        part = mm(kv_b, w_qkv[layer, width:]) + mm(query_b, w_qkv[layer, :width])
        part_ref[...] = part.astype(bf16)
        sent_ref[:, :half] = picked_ref[:, half:]
        sent_ref[:, half : half + 2 * width] = kv_b
        sent_ref[:, half + 2 * width : half + 3 * width] = query_b
        if pad:
            sent_ref[:, half + 3 * width :] = jnp.zeros((rows, pad), bf16)
        small_ref[...] = jnp.zeros((8, D), f32)
        small_ref[0:1, :width] = column_sum(d_query)
        small_ref[1:2, :width] = column_sum(d_kv)[:, width:]

    return call(
        kernel,
        [((rows, half + 3 * width + pad), bf16), ((rows, D), bf16), ((8, D), f32)],
        [dq, dkv, *arrived, picked, params["w_qkv"]],
    )


def own_small(mlp_small, qv_small):
    def kernel(*refs):
        mlp, qv, out = refs[:LAYERS], refs[LAYERS : 2 * LAYERS], refs[-1]
        out[...] = jnp.zeros((8, D), f32)
        for layer in range(LAYERS):
            out[layer : layer + 1, :] = mlp[layer][0:1, :]
            at = LAYERS + 2 * layer
            out[at : at + 2, :] = qv[layer][0:2, :]

    return call(kernel, [((8, D), f32)], [*mlp_small, *qv_small], 1e5)[0]


def small_rows(count):
    return 6 * LAYERS + 2 * LAYERS + LAYERS * count


def first_grad(gmid, pair, hidden, params, mlp_small, att_small, own_pieces, own_rows):
    count = len(own_pieces)
    width = params["w_out"].shape[1]
    rows_all = small_rows(count)
    padded = rows_all + -rows_all % 8

    def kernel(gmid_ref, own_ref, other_ref, h_ref, gains, *refs):
        mlp, att = refs[:LAYERS], refs[LAYERS : 2 * LAYERS]
        pieces = refs[2 * LAYERS : 2 * LAYERS + count]
        in_ref, all_ref, g_ref = refs[2 * LAYERS + count :]
        mine = lax.axis_index("tensor")
        grad, g_gain, g_bias = norm1_grad(gmid_ref, own_ref, other_ref, h_ref, gains, 0)
        g_ref[...] = grad
        start = pl.multiple_of(mine * own_rows, own_rows)
        in_ref[...] = g_ref[pl.ds(start, own_rows), :].astype(bf16)
        all_ref[...] = jnp.zeros((padded, D), f32)
        for layer in range(LAYERS):
            gain1 = g_gain if layer == 0 else mlp[layer - 1][2:3, :]
            bias1 = g_bias if layer == 0 else mlp[layer - 1][3:4, :]
            at = 2 * layer
            all_ref[at : at + 1, :] = gain1
            all_ref[at + 1 : at + 2, :] = att[layer][0:1, :]
            at = 2 * LAYERS + 4 * layer
            all_ref[at : at + 1, :] = bias1
            all_ref[at + 1 : at + 2, :] = att[layer][2:3, :]
            all_ref[at + 2 : at + 3, :] = att[layer][1:2, :]
            all_ref[at + 3 : at + 4, :] = mlp[layer][1:2, :]
        for target in range(count):
            chosen = pieces[0][...]
            for number in range(1, count):
                chosen = jnp.where((mine ^ number) == target, pieces[number][...], chosen)
            for layer in range(LAYERS):
                at = 6 * LAYERS + 2 * layer
                source = LAYERS + 2 * layer
                lanes = slice(target * width, (target + 1) * width)
                all_ref[at : at + 2, lanes] = chosen[source : source + 2, :width]
                at = 8 * LAYERS + layer * count + target
                all_ref[at : at + 1, :] = chosen[layer : layer + 1, :]

    rows = gmid.shape[0]
    got = call(
        kernel,
        [((own_rows, D), bf16), ((padded, D), f32), ((rows, D), f32)],
        [gmid, *pair, hidden, params["gains"], *mlp_small, *att_small, *own_pieces],
    )
    return got[0], got[1]


def small_outs(total, other, count):
    def kernel(total_ref, other_ref, gains, biases, qv, ffb):
        both = total_ref[...] + other_ref[...]
        for layer in range(LAYERS):
            gains[layer] = both[2 * layer : 2 * layer + 2]
            at = 2 * LAYERS + 4 * layer
            biases[layer] = both[at : at + 4]
            at = 6 * LAYERS + 2 * layer
            qv[layer] = both[at : at + 2]
            for target in range(count):
                at = 8 * LAYERS + layer * count + target
                ffb[layer : layer + 1, target * D : (target + 1) * D] = both[at : at + 1]

    return call(
        kernel,
        [
            ((LAYERS, 2, D), f32),
            ((LAYERS, 4, D), f32),
            ((LAYERS, 2, D), f32),
            ((LAYERS, count * D), f32),
        ],
        [total, other],
        1e5,
    )


def split_rows(total, bit, block, send_ref, keep_ref):
    mine = lax.axis_index("dp")
    high = jnp.where((mine & bit) != 0, 1, 0)
    pairs = total.shape[0] // (2 * block)
    for pair in range(pairs):
        for which in range(2):
            rows = total[(2 * pair + which) * block : (2 * pair + which + 1) * block]
            out = slice(pair * block, (pair + 1) * block)

            @pl.when(high == which)
            def _():
                keep_ref[out, :] = rows

            @pl.when(high != which)
            def _():
                send_ref[out, :] = rows.astype(bf16)


def split_plain(total, bit, block):
    pairs = total.shape[0] // (2 * block)
    split = total.reshape(pairs, 2, block, total.shape[1])
    high = jnp.where((lax.axis_index("dp") & bit) != 0, 1, 0)
    send = lax.dynamic_index_in_dim(split, 1 - high, 1, keepdims=False)
    keep = lax.dynamic_index_in_dim(split, high, 1, keepdims=False)
    return send.reshape(-1, total.shape[1]).astype(bf16), keep.reshape(-1, total.shape[1])


def halved(send, keep, bits, block):
    for place, bit in enumerate(bits):
        arrived = swapped(send, "dp", bit)
        if place == len(bits) - 1:
            return keep, arrived
        shape = (keep.shape[0] // 2, keep.shape[1])
        if block % 16:
            send, keep = split_plain(keep + arrived.astype(f32), bits[place + 1], block)
        else:

            def kernel(keep_ref, arrived_ref, send_ref, kept_ref, following=bits[place + 1]):
                total = keep_ref[...] + arrived_ref[...].astype(f32)
                split_rows(total, following, block, send_ref, kept_ref)

            send, keep = call(kernel, [(shape, bf16), (shape, f32)], [keep, arrived], 1e6)


def weight_parts(first, second, products, wide):
    half = D // 2
    count = lax.axis_size("dp")
    block = D // count
    bits = bits_of("dp")
    flat = []
    for sent, kept in (first, second):
        flat += [sent, swapped(sent, "dp", bits[0]), kept]
    shape = (half // 2, wide)

    def products_of(refs):
        done = []
        for (la, kept_at, sent_at), (ra, r0, r1) in products:
            kept = refs[3 * la + 2][:, kept_at : kept_at + half]
            given = refs[3 * la + 1][:, sent_at : sent_at + half]
            left = jnp.concatenate([kept, given], axis=0)
            right = jnp.concatenate([refs[3 * ra][:, r0:r1], refs[3 * ra + 1][:, r0:r1]], axis=0)
            done.append(mm(left, right, TN))
        return jnp.concatenate(done, axis=1)

    if block % 16:

        def kernel(*refs):
            refs[6][...] = products_of(refs)

        total = call(kernel, [((half, wide), f32)], flat, 3e8)[0]
        send, keep = split_plain(total, bits[1], block)
    else:

        def kernel(*refs):
            split_rows(products_of(refs), bits[1], block, refs[6], refs[7])

        send, keep = call(kernel, [(shape, bf16), (shape, f32)], flat, 3e8)
    return halved(send, keep, bits[1:], block)


def mlp_outputs(parts, block, inner):
    def kernel(*refs):
        up, down = refs[-2:]
        for layer in range(LAYERS):
            total = joined(refs[2 * layer], refs[2 * layer + 1])
            up[layer] = total[:, :inner]
            down[layer] = total[:, inner:]

    args = [a for pair in parts for a in pair]
    return call(kernel, [((LAYERS, block, inner), f32)] * 2, args, 1e6)


def att_outputs(parts, block, width):
    def kernel(*refs):
        qkv, out = refs[-2:]
        for layer in range(LAYERS):
            total = joined(refs[2 * layer], refs[2 * layer + 1])
            qkv[layer, 0] = total[:, 2 * width : 3 * width]
            qkv[layer, 1] = total[:, :width]
            qkv[layer, 2] = total[:, width : 2 * width]
            out[layer] = total[:, 3 * width :]

    args = [a for pair in parts for a in pair]
    return call(
        kernel,
        [((LAYERS, 3, block, width), f32), ((LAYERS, block, width), f32)],
        args,
        1e6,
    )


def shards(
    tokens, cotangent, segments, w_qkv, qv_bias, w_out, w_up, w_down, ff_bias, gains, biases
):
    tensor_count = lax.axis_size("tensor")
    dp_count = lax.axis_size("dp")
    dp_index = lax.axis_index("dp")
    own_rows = tokens.shape[0]
    rows = own_rows * tensor_count
    width = w_out.shape[1]
    inner = w_up.shape[2]
    half = D // 2
    block = D // dp_count
    params = {
        "w_qkv": w_qkv.transpose(0, 2, 3, 1).reshape(LAYERS, 3 * width, D),
        "qv_bias": qv_bias,
        "w_out": w_out,
        "w_up": w_up,
        "w_down": w_down,
        "ff_bias": ff_bias,
        "gains": gains,
        "biases": biases,
    }
    seg_q = lax.dynamic_slice_in_dim(segments, dp_index * rows, rows)[:, None]
    padded = jnp.concatenate([jnp.full(((SPAN - 1) * rows,), -1, jnp.int32), segments])
    seg_k = lax.dynamic_slice_in_dim(padded, dp_index * rows, SPAN * rows)[None, :]
    segs = [seg_q, seg_k]
    column = lax.broadcasted_iota(jnp.int32, (D, D), 1)
    side = (dp_index & 1) ^ (column // half)
    column = column % half
    source = (column // block) * (2 * block) + side * block + column % block
    pick = (lax.broadcasted_iota(jnp.int32, (D, D), 0) == source).astype(bf16)

    token_pieces = gathered(tokens)
    cot_pieces = gathered(cotangent)
    saved = []
    sent_fwd = []
    mid = pair = None
    for layer in range(LAYERS):
        if layer == 0:
            hidden, picked1, q, kv = project_first(token_pieces, params, pick)
        else:
            hidden, picked1, q, kv = project_next(mid, pair, layer, params, pick)
        kv_parts = [shifted(kv, "dp", distance) for distance in range(SPAN - 1, 0, -1)] + [kv]
        att, lse, part = attend(q, kv_parts, segs, layer, params)
        mid, slope, sent, kept, part = feed_forward(
            hidden, exchanged(part), picked1, att, layer, params, pick
        )
        sent_fwd.append((sent, kept))
        pair = exchanged(part)
        saved.append((hidden, q, kv_parts, att, lse, mid, slope))
    result = last_rows(mid, pair, params, own_rows)

    up_at, act3_at, att_at = half, 2 * half, 2 * half + inner
    mlp_products = [
        ((0, up_at, up_at), (1, half, half + inner)),
        ((1, 0, 0), (0, act3_at, act3_at + inner)),
    ]
    att_products = [
        ((0, 0, 0), (1, half, half + 3 * width)),
        ((1, 0, 0), (0, att_at, att_at + width)),
    ]
    mlp_small, att_small, qv_small = ([None] * LAYERS for _ in range(3))
    mlp_parts, att_parts = ([None] * LAYERS for _ in range(2))
    gmid = None
    for layer in range(LAYERS - 1, -1, -1):
        hidden, q, kv_parts, att, lse, mid, slope = saved[layer]
        if layer == LAYERS - 1:
            grad, sent1, part, mlp_small[layer], kept1 = mlp_grad_last(cot_pieces, slope, params, pick)
        else:
            grad, sent1, part, mlp_small[layer], kept1 = mlp_grad_next(
                gmid, pair, saved[layer + 1][0], slope, layer, params, pick
            )
        pair = exchanged(part)
        gmid, picked, dq, dkv, att_small[layer], *away = attend_grad(
            grad, pair, mid, q, kv_parts, segs, att, lse, layer, params, pick
        )
        arrived = [shifted(a, "dp", -(place + 1)) for place, a in enumerate(away)]
        sent2, part, qv_small[layer] = project_grad(dq, dkv, arrived, picked, layer, params)
        pair = exchanged(part)
        mlp_parts[layer] = weight_parts(sent_fwd[layer], (sent1, kept1), mlp_products, 2 * inner)
        att_parts[layer] = weight_parts(sent_fwd[layer], (sent2, picked), att_products, 4 * width)

    own_pieces = gathered(own_small(mlp_small, qv_small))
    input_grad, small = first_grad(
        gmid, pair, saved[0][0], params, mlp_small, att_small, own_pieces, own_rows
    )
    dp_bits = bits_of("dp")
    for bit in dp_bits[:-1]:
        small = small + swapped(small, "dp", bit)
    small_grads = small_outs(small, swapped(small, "dp", dp_bits[-1]), tensor_count)
    g_up, g_down = mlp_outputs(mlp_parts, block, inner)
    g_qkv, g_out = att_outputs(att_parts, block, width)
    return (
        result,
        input_grad,
        g_qkv.transpose(0, 2, 1, 3),
        g_out.transpose(0, 2, 1),
        g_up,
        g_down.transpose(0, 2, 1),
        *small_grads,
    )


def solution(mesh):
    return jax.shard_map(
        shards,
        mesh=mesh,
        in_specs=(
            P(("dp", "tensor"), None),
            P(("dp", "tensor"), None),
            P(),
            P(None, None, None, "tensor"),
            P(None, None, "tensor"),
            P(None, "tensor", None),
            P(None, None, "tensor"),
            P(None, "tensor", None),
            P(None, "tensor"),
            P(),
            P(),
        ),
        out_specs=(
            P(("dp", "tensor"), None),
            P(("dp", "tensor"), None),
            P(None, "dp", None, "tensor"),
            P(None, "tensor", "dp"),
            P(None, "dp", "tensor"),
            P(None, "tensor", "dp"),
            P(),
            P(),
            P(),
            P(),
        ),
        check_vma=False,
    )
```

time: 900 us -> 226 us (0.25)
  waiting for transfers between devices: 693 us -> 126 us
  blocking collectives: 46.3 us -> 0 us
  local copies, waits for them, and re-layouts: 47.5 us -> 6.22 us
  starting transfers between devices: 31.1 us -> 69.6 us
  matrix products: 33.3 us -> 0 us
  other arithmetic: 31 us -> 0.83 us
  Pallas kernels: 0 us -> 21.5 us
  between operations: 16 us -> 1.19 us
    unnamed x16 -> x0, waiting for transfers between devices: 296 us -> none
    reduce_scatter x9 -> x0, waiting for transfers between devices: 247 us -> none  [the longest x1 103 us: shards(): lax.psum_scatter(stacked[2], 'dp', scatter_dimension=1, tiled=True)]
    psum x1 -> x0, waiting for transfers between devices: 124 us -> none  [shards(): lax.psum((small_stack[0], small_stack[1], small_stack[2], small_stack[3])...]
    ppermute x0 -> x42, waiting for transfers between devices: none -> 105 us  [swapped(): return lax.ppermute(array, axis, [(i, i ^ bit) for i in range(length)])]
    all_gather x8 -> x0, blocking collectives: 46.3 us -> none  [the longest x2 12.4 us: layer_forward(): act1 = lax.all_gather(normed1.astype(bf16), 'tensor', axis=0, tiled=True)]
    ppermute x0 -> x42, starting transfers between devices: none -> 39 us  [swapped(): return lax.ppermute(array, axis, [(i, i ^ bit) for i in range(length)])]
    dot_general x32 -> x0, matrix products: 31.8 us -> none  [the longest x2 3.78 us: layer_backward(): jnp.dot(out_b, w_down[layer_no].T, preferred_element_type=f32) * slope]
    unnamed x177 -> x29, local copies, waits for them, and re-layouts: 33.8 us -> 5.26 us
  transfers between devices with their start and end apart: 25 -> 54, of which waited for: 20 -> 31; matrix products, arithmetic and copies ran while one was open for 6% -> 1% of each run, Pallas kernels for 0% -> 4%
where the time goes in v2:
time: 226 us; the launch traced here: 225 us
  waiting for transfers between devices  126 us (56%)
  starting transfers between devices  69.6 us (31%)
  Pallas kernels  21.5 us (10%)
  local copies, waits for them, and re-layouts  6.22 us (3%)
    ppermute x42, waiting for transfers between devices, swapped(): return lax.ppermute(array, axis, [(i, i ^ bit) for i in range(length)])  105 us
    ppermute x42, starting transfers between devices, swapped(): return lax.ppermute(array, axis, [(i, i ^ bit) for i in range(length)])  39 us
    ppermute x12, starting transfers between devices, shifted(): return lax.ppermute(array, axis, pairs)  30.6 us
    pallas_call x26, Pallas kernels, call(): pl.pallas_call(kernel, out_shape=shapes, in_specs=[spec] * len(args), out...  21.5 us
    ppermute x12, waiting for transfers between devices, shifted(): return lax.ppermute(array, axis, pairs)  21 us
    unnamed x29, local copies, waits for them, and re-layouts  5.26 us
  transfers between devices with their start and end apart: 54, of which 31 were waited for; matrix products, arithmetic and copies ran while one was open for 1% of the time, Pallas kernels for 4%

profile of v2, /device:TPU:0, one launch (start us, length us, event | category | flops | bytes accessed | tf_op | source)
XLA Modules:
  0.0 225.0 jit_solution(4080742296635533687)
XLA Ops:
  12.7 4.8 %collective-permute-start.3 = (bf16[128,384]{1,0:T(8,128)(2,1)S(1)}, bf16[128,384]{1,0:T(8,128)(2,1)S(1)}, u32[]{:S(2)}, u32[]{:S(2)}) collective-permute-start(bf16[128,384]{1,0:T(8,128)(2,1)S(1)} %get-tuple-element.94.refs_3_), channel_id=1, source_target_pairs={{0,12},{4,16},{8,20},{12,24},{16,28},{1,13},{5,17},{9,21},{13,25},... | collective-permute-start | bytes 294920 | tf_op jit(solution)/shard_map/ppermute | solution.py:24
  17.6 3.5 %collective-permute-start.4 = (bf16[128,384]{1,0:T(8,128)(2,1)S(1)}, bf16[128,384]{1,0:T(8,128)(2,1)S(1)}, u32[]{:S(2)}, u32[]{:S(2)}) collective-permute-start(bf16[128,384]{1,0:T(8,128)(2,1)S(1)} %get-tuple-element.94.refs_3_), channel_id=1, source_target_pairs={{0,8},{4,12},{8,16},{12,20},{16,24},{20,28},{1,9},{5,13},{9,17},{1... | collective-permute-start | bytes 294920 | tf_op jit(solution)/shard_map/ppermute | solution.py:24
  21.1 3.4 %collective-permute-start.5 = (bf16[128,384]{1,0:T(8,128)(2,1)S(1)}, bf16[128,384]{1,0:T(8,128)(2,1)S(1)}, u32[]{:S(2)}, u32[]{:S(2)}) collective-permute-start(bf16[128,384]{1,0:T(8,128)(2,1)S(1)} %get-tuple-element.94.refs_3_), channel_id=1, source_target_pairs={{0,4},{4,8},{8,12},{12,16},{16,20},{20,24},{24,28},{1,5},{5,9},{9,... | collective-permute-start | bytes 294920 | tf_op jit(solution)/shard_map/ppermute | solution.py:24
  31.4 5.5 %collective-permute-done.7.other_ref = bf16[128,768]{1,0:T(8,128)(2,1)S(1)} collective-permute-done((bf16[128,768]{1,0:T(8,128)(2,1)S(1)}, bf16[128,768]{1,0:T(8,128)(2,1)S(1)}, u32[]{:S(2)}, u32[]{:S(2)}) %collective-permute-start.7) | collective-permute-done | bytes 196640 | tf_op jit(solution)/shard_map/ppermute | solution.py:29
  41.1 5.5 %collective-permute-done.9.other_ref = bf16[128,768]{1,0:T(8,128)(2,1)S(1)} collective-permute-done((bf16[128,768]{1,0:T(8,128)(2,1)S(1)}, bf16[128,768]{1,0:T(8,128)(2,1)S(1)}, u32[]{:S(2)}, u32[]{:S(2)}) %collective-permute-start.9) | collective-permute-done | bytes 196640 | tf_op jit(solution)/shard_map/ppermute | solution.py:29
  47.3 3.9 %collective-permute-start.10 = (bf16[128,384]{1,0:T(8,128)(2,1)S(1)}, bf16[128,384]{1,0:T(8,128)(2,1)S(1)}, u32[]{:S(2)}, u32[]{:S(2)}) collective-permute-start(bf16[128,384]{1,0:T(8,128)(2,1)S(1)} %get-tuple-element.102.refs_3_), channel_id=1, source_target_pairs={{0,12},{4,16},{8,20},{12,24},{16,28},{1,13},{5,17},{9,21},{13,25},... | collective-permute-start | bytes 294920 | tf_op jit(solution)/shard_map/ppermute | solution.py:24
  53.9 4.4 %collective-permute-start.12 = (bf16[128,384]{1,0:T(8,128)(2,1)S(1)}, bf16[128,384]{1,0:T(8,128)(2,1)S(1)}, u32[]{:S(2)}, u32[]{:S(2)}) collective-permute-start(bf16[128,384]{1,0:T(8,128)(2,1)S(1)} %get-tuple-element.102.refs_3_), channel_id=1, source_target_pairs={{0,4},{4,8},{8,12},{12,16},{16,20},{20,24},{24,28},{1,5},{5,9},{9,... | collective-permute-start | bytes 294920 | tf_op jit(solution)/shard_map/ppermute | solution.py:24
  65.8 6.0 %collective-permute-done.18.refs_2_ = bf16[32,768]{1,0:T(8,128)(2,1)S(1)} collective-permute-done((bf16[32,768]{1,0:T(8,128)(2,1)S(1)}, bf16[32,768]{1,0:T(8,128)(2,1)S(1)}, u32[]{:S(2)}, u32[]{:S(2)}) %collective-permute-start.18) | collective-permute-done | bytes 49184 | tf_op jit(solution)/shard_map/ppermute | solution.py:29
  77.2 5.6 %collective-permute-done.21.other_ref = bf16[128,768]{1,0:T(8,128)(2,1)S(1)} collective-permute-done((bf16[128,768]{1,0:T(8,128)(2,1)S(1)}, bf16[128,768]{1,0:T(8,128)(2,1)S(1)}, u32[]{:S(2)}, u32[]{:S(2)}) %collective-permute-start.21) | collective-permute-done | bytes 196640 | tf_op jit(solution)/shard_map/ppermute | solution.py:29
  91.8 3.6 %collective-permute-done.23.refs_1_ = bf16[128,384]{1,0:T(8,128)(2,1)S(1)} collective-permute-done((bf16[128,384]{1,0:T(8,128)(2,1)S(1)}, bf16[128,384]{1,0:T(8,128)(2,1)S(1)}, u32[]{:S(2)}, u32[]{:S(2)}) %collective-permute-start.23) | collective-permute-done | bytes 98336 | tf_op jit(solution)/shard_map/ppermute | solution.py:24
  100.9 5.5 %collective-permute-done.26.other_ref = bf16[128,768]{1,0:T(8,128)(2,1)S(1)} collective-permute-done((bf16[128,768]{1,0:T(8,128)(2,1)S(1)}, bf16[128,768]{1,0:T(8,128)(2,1)S(1)}, u32[]{:S(2)}, u32[]{:S(2)}) %collective-permute-start.26) | collective-permute-done | bytes 196640 | tf_op jit(solution)/shard_map/ppermute | solution.py:29
  107.8 4.9 %collective-permute-start.41 = (bf16[128,1792]{1,0:T(8,128)(2,1)S(1)}, bf16[128,1792]{1,0:T(8,128)(2,1)S(1)}, u32[]{:S(2)}, u32[]{:S(2)}) collective-permute-start(bf16[128,1792]{1,0:T(8,128)(2,1)S(1)} %get-tuple-element.146.refs_0_), channel_id=1, source_target_pairs={{0,4},{4,0},{8,12},{12,8},{16,20},{20,16},{24,28},{28,24},{1,5},{5... | collective-permute-start | bytes 1376264 | tf_op jit(solution)/shard_map/ppermute | solution.py:29
  116.5 4.8 %collective-permute-done.28.other_ref = bf16[128,768]{1,0:T(8,128)(2,1)S(1)} collective-permute-done((bf16[128,768]{1,0:T(8,128)(2,1)S(1)}, bf16[128,768]{1,0:T(8,128)(2,1)S(1)}, u32[]{:S(2)}, u32[]{:S(2)}) %collective-permute-start.28) | collective-permute-done | bytes 196640 | tf_op jit(solution)/shard_map/ppermute | solution.py:29
  124.6 17.2 %collective-permute-done.48.refs_4_ = bf16[128,1152]{1,0:T(8,128)(2,1)S(1)} collective-permute-done((bf16[128,1152]{1,0:T(8,128)(2,1)S(1)}, bf16[128,1152]{1,0:T(8,128)(2,1)S(1)}, u32[]{:S(2)}, u32[]{:S(2)}) %collective-permute-start.48) | collective-permute-done | bytes 294944 | tf_op jit(solution)/shard_map/ppermute | solution.py:29
  145.1 3.3 %collective-permute-done.29.refs_0_ = bf16[128,384]{1,0:T(8,128)(2,1)S(1)} collective-permute-done((bf16[128,384]{1,0:T(8,128)(2,1)S(1)}, bf16[128,384]{1,0:T(8,128)(2,1)S(1)}, u32[]{:S(2)}, u32[]{:S(2)}) %collective-permute-start.29) | collective-permute-done | bytes 98336 | tf_op jit(solution)/shard_map/ppermute | solution.py:24
  148.4 4.9 %collective-permute-done.31.refs_2_ = bf16[128,384]{1,0:T(8,128)(2,1)S(1)} collective-permute-done((bf16[128,384]{1,0:T(8,128)(2,1)S(1)}, bf16[128,384]{1,0:T(8,128)(2,1)S(1)}, u32[]{:S(2)}, u32[]{:S(2)}) %collective-permute-start.31) | collective-permute-done | bytes 98336 | tf_op jit(solution)/shard_map/ppermute | solution.py:24
  154.5 4.4 %collective-permute-start.42 = (bf16[128,1024]{1,0:T(8,128)(2,1)S(1)}, bf16[128,1024]{1,0:T(8,128)(2,1)S(1)}, u32[]{:S(2)}, u32[]{:S(2)}) collective-permute-start(bf16[128,1024]{1,0:T(8,128)(2,1)S(1)} %get-tuple-element.148.refs_3_), channel_id=1, source_target_pairs={{0,4},{4,0},{8,12},{12,8},{16,20},{20,16},{24,28},{28,24},{1,5},{5... | collective-permute-start | bytes 786440 | tf_op jit(solution)/shard_map/ppermute | solution.py:29
  160.5 5.4 %collective-permute-done.42.refs_4_ = bf16[128,1024]{1,0:T(8,128)(2,1)S(1)} collective-permute-done((bf16[128,1024]{1,0:T(8,128)(2,1)S(1)}, bf16[128,1024]{1,0:T(8,128)(2,1)S(1)}, u32[]{:S(2)}, u32[]{:S(2)}) %collective-permute-start.42) | collective-permute-done | bytes 262176 | tf_op jit(solution)/shard_map/ppermute | solution.py:29
  171.7 5.5 %collective-permute-done.46.arrived_ref = bf16[192,1536]{1,0:T(8,128)(2,1)S(1)} collective-permute-done((bf16[192,1536]{1,0:T(8,128)(2,1)S(1)}, bf16[192,1536]{1,0:T(8,128)(2,1)S(1)}, u32[]{:S(2)}, u32[]{:S(2)}) %collective-permute-start.46) | collective-permute-done | bytes 589856 | tf_op jit(solution)/shard_map/ppermute | solution.py:29
  184.7 3.3 %collective-permute-done.51 = f32[24,768]{1,0:T(8,128)S(1)} collective-permute-done((f32[24,768]{1,0:T(8,128)S(1)}, f32[24,768]{1,0:T(8,128)S(1)}, u32[]{:S(2)}, u32[]{:S(2)}) %collective-permute-start.51) | collective-permute-done | bytes 73760 | tf_op jit(solution)/shard_map/ppermute | solution.py:29
  189.5 6.3 %collective-permute-done.43.arrived_ref = bf16[192,768]{1,0:T(8,128)(2,1)S(1)} collective-permute-done((bf16[192,768]{1,0:T(8,128)(2,1)S(1)}, bf16[192,768]{1,0:T(8,128)(2,1)S(1)}, u32[]{:S(2)}, u32[]{:S(2)}) %collective-permute-start.43) | collective-permute-done | bytes 294944 | tf_op jit(solution)/shard_map/ppermute | solution.py:29
  195.9 9.1 %collective-permute-done.39.arrived_ref = bf16[192,768]{1,0:T(8,128)(2,1)S(1)} collective-permute-done((bf16[192,768]{1,0:T(8,128)(2,1)S(1)}, bf16[192,768]{1,0:T(8,128)(2,1)S(1)}, u32[]{:S(2)}, u32[]{:S(2)}) %collective-permute-start.39) | collective-permute-done | bytes 294944 | tf_op jit(solution)/shard_map/ppermute | solution.py:29
  205.8 2.8 %collective-permute-start.40 = (bf16[96,768]{1,0:T(8,128)(2,1)S(1)}, bf16[96,768]{1,0:T(8,128)(2,1)S(1)}, u32[]{:S(2)}, u32[]{:S(2)}) collective-permute-start(bf16[96,768]{1,0:T(8,128)(2,1)S(1)} %get-tuple-element.145), channel_id=1, source_target_pairs={{0,16},{4,20},{8,24},{12,28},{16,0},{20,4},{24,8},{28,12},{1,17},{... | collective-permute-start | bytes 442376 | tf_op jit(solution)/shard_map/ppermute | solution.py:29
  209.4 12.0 %collective-permute-done.53.other_ref = f32[24,768]{1,0:T(8,128)S(1)} collective-permute-done((f32[24,768]{1,0:T(8,128)S(1)}, f32[24,768]{1,0:T(8,128)S(1)}, u32[]{:S(2)}, u32[]{:S(2)}) %collective-permute-start.53) | collective-permute-done | bytes 73760 | tf_op jit(solution)/shard_map/ppermute | solution.py:29
  (156 shorter events, 88.2 us)
Async XLA Ops:
  12.7 11.9 %collective-permute-start.3 = (bf16[128,384]{1,0:T(8,128)(2,1)S(1)}, bf16[128,384]{1,0:T(8,128)(2,1)S(1)}, u32[]{:S(2)}, u32[]{:S(2)}) collective-permute-start(bf16[128,384]{1,0:T(8,128)(2,1)S(1)} %get-tuple-element.94.refs_3_), channel_id=1, source_target_pairs={{0,12},{4,16},{8,20},{12,24},{16,28},{1,13},{5,17},{9,21},{13,25},... | collective-permute-start | bytes 294920 | tf_op jit(solution)/shard_map/ppermute | solution.py:24
  47.3 11.0 %collective-permute-start.10 = (bf16[128,384]{1,0:T(8,128)(2,1)S(1)}, bf16[128,384]{1,0:T(8,128)(2,1)S(1)}, u32[]{:S(2)}, u32[]{:S(2)}) collective-permute-start(bf16[128,384]{1,0:T(8,128)(2,1)S(1)} %get-tuple-element.102.refs_3_), channel_id=1, source_target_pairs={{0,12},{4,16},{8,20},{12,24},{16,28},{1,13},{5,17},{9,21},{13,25},... | collective-permute-start | bytes 294920 | tf_op jit(solution)/shard_map/ppermute | solution.py:24
  87.5 10.0 %collective-permute-start.24 = (bf16[128,384]{1,0:T(8,128)(2,1)S(1)}, bf16[128,384]{1,0:T(8,128)(2,1)S(1)}, u32[]{:S(2)}, u32[]{:S(2)}) collective-permute-start(bf16[128,384]{1,0:T(8,128)(2,1)S(1)} %get-tuple-element.117), channel_id=1, source_target_pairs={{12,0},{16,4},{20,8},{24,12},{28,16},{13,1},{17,5},{21,9},{25,13},... | collective-permute-start | bytes 294920 | tf_op jit(solution)/shard_map/ppermute | solution.py:24
  107.8 35.3 %collective-permute-start.41 = (bf16[128,1792]{1,0:T(8,128)(2,1)S(1)}, bf16[128,1792]{1,0:T(8,128)(2,1)S(1)}, u32[]{:S(2)}, u32[]{:S(2)}) collective-permute-start(bf16[128,1792]{1,0:T(8,128)(2,1)S(1)} %get-tuple-element.146.refs_0_), channel_id=1, source_target_pairs={{0,4},{4,0},{8,12},{12,8},{16,20},{20,16},{24,28},{28,24},{1,5},{5... | collective-permute-start | bytes 1376264 | tf_op jit(solution)/shard_map/ppermute | solution.py:29
  112.7 41.0 %collective-permute-start.37 = (bf16[128,1792]{1,0:T(8,128)(2,1)S(1)}, bf16[128,1792]{1,0:T(8,128)(2,1)S(1)}, u32[]{:S(2)}, u32[]{:S(2)}) collective-permute-start(bf16[128,1792]{1,0:T(8,128)(2,1)S(1)} %get-tuple-element.139.refs_0_), channel_id=1, source_target_pairs={{0,4},{4,0},{8,12},{12,8},{16,20},{20,16},{24,28},{28,24},{1,5},{5... | collective-permute-start | bytes 1376264 | tf_op jit(solution)/shard_map/ppermute | solution.py:29
  112.8 29.0 %collective-permute-start.48 = (bf16[128,1152]{1,0:T(8,128)(2,1)S(1)}, bf16[128,1152]{1,0:T(8,128)(2,1)S(1)}, u32[]{:S(2)}, u32[]{:S(2)}) collective-permute-start(bf16[128,1152]{1,0:T(8,128)(2,1)S(1)} %get-tuple-element.161.refs_3_), channel_id=1, source_target_pairs={{0,4},{4,0},{8,12},{12,8},{16,20},{20,16},{24,28},{28,24},{1,5},{5... | collective-permute-start | bytes 884744 | tf_op jit(solution)/shard_map/ppermute | solution.py:29
  116.4 37.3 %collective-permute-start.45 = (bf16[128,1152]{1,0:T(8,128)(2,1)S(1)}, bf16[128,1152]{1,0:T(8,128)(2,1)S(1)}, u32[]{:S(2)}, u32[]{:S(2)}) collective-permute-start(bf16[128,1152]{1,0:T(8,128)(2,1)S(1)} %get-tuple-element.155.refs_3_), channel_id=1, source_target_pairs={{0,4},{4,0},{8,12},{12,8},{16,20},{20,16},{24,28},{28,24},{1,5},{5... | collective-permute-start | bytes 884744 | tf_op jit(solution)/shard_map/ppermute | solution.py:29
  123.3 25.1 %collective-permute-start.29 = (bf16[128,384]{1,0:T(8,128)(2,1)S(1)}, bf16[128,384]{1,0:T(8,128)(2,1)S(1)}, u32[]{:S(2)}, u32[]{:S(2)}) collective-permute-start(bf16[128,384]{1,0:T(8,128)(2,1)S(1)} %get-tuple-element.127), channel_id=1, source_target_pairs={{4,0},{8,4},{12,8},{16,12},{20,16},{24,20},{28,24},{5,1},{9,5},{13... | collective-permute-start | bytes 294920 | tf_op jit(solution)/shard_map/ppermute | solution.py:24
  143.1 10.2 %collective-permute-start.31 = (bf16[128,384]{1,0:T(8,128)(2,1)S(1)}, bf16[128,384]{1,0:T(8,128)(2,1)S(1)}, u32[]{:S(2)}, u32[]{:S(2)}) collective-permute-start(bf16[128,384]{1,0:T(8,128)(2,1)S(1)} %get-tuple-element.129), channel_id=1, source_target_pairs={{12,0},{16,4},{20,8},{24,12},{28,16},{13,1},{17,5},{21,9},{25,13},... | collective-permute-start | bytes 294920 | tf_op jit(solution)/shard_map/ppermute | solution.py:24
  148.4 17.5 %collective-permute-start.49 = (bf16[192,1536]{1,0:T(8,128)(2,1)S(1)}, bf16[192,1536]{1,0:T(8,128)(2,1)S(1)}, u32[]{:S(2)}, u32[]{:S(2)}) collective-permute-start(bf16[192,1536]{1,0:T(8,128)(2,1)S(1)} %get-tuple-element.164), channel_id=1, source_target_pairs={{0,8},{4,12},{8,0},{12,4},{16,24},{20,28},{24,16},{28,20},{1,9},{5... | collective-permute-start | bytes 1769480 | tf_op jit(solution)/shard_map/ppermute | solution.py:29
  154.4 22.8 %collective-permute-start.46 = (bf16[192,1536]{1,0:T(8,128)(2,1)S(1)}, bf16[192,1536]{1,0:T(8,128)(2,1)S(1)}, u32[]{:S(2)}, u32[]{:S(2)}) collective-permute-start(bf16[192,1536]{1,0:T(8,128)(2,1)S(1)} %get-tuple-element.158), channel_id=1, source_target_pairs={{0,8},{4,12},{8,0},{12,4},{16,24},{20,28},{24,16},{28,20},{1,9},{5... | collective-permute-start | bytes 1769480 | tf_op jit(solution)/shard_map/ppermute | solution.py:29
  154.5 11.4 %collective-permute-start.42 = (bf16[128,1024]{1,0:T(8,128)(2,1)S(1)}, bf16[128,1024]{1,0:T(8,128)(2,1)S(1)}, u32[]{:S(2)}, u32[]{:S(2)}) collective-permute-start(bf16[128,1024]{1,0:T(8,128)(2,1)S(1)} %get-tuple-element.148.refs_3_), channel_id=1, source_target_pairs={{0,4},{4,0},{8,12},{12,8},{16,20},{20,16},{24,28},{28,24},{1,5},{5... | collective-permute-start | bytes 786440 | tf_op jit(solution)/shard_map/ppermute | solution.py:29
  158.8 12.3 %collective-permute-start.38 = (bf16[128,1024]{1,0:T(8,128)(2,1)S(1)}, bf16[128,1024]{1,0:T(8,128)(2,1)S(1)}, u32[]{:S(2)}, u32[]{:S(2)}) collective-permute-start(bf16[128,1024]{1,0:T(8,128)(2,1)S(1)} %get-tuple-element.141.refs_3_), channel_id=1, source_target_pairs={{0,4},{4,0},{8,12},{12,8},{16,20},{20,16},{24,28},{28,24},{1,5},{5... | collective-permute-start | bytes 786440 | tf_op jit(solution)/shard_map/ppermute | solution.py:29
  158.9 22.9 %collective-permute-start.33 = (bf16[128,768]{1,0:T(8,128)(2,1)S(1)}, bf16[128,768]{1,0:T(8,128)(2,1)S(1)}, u32[]{:S(2)}, u32[]{:S(2)}) collective-permute-start(bf16[128,768]{1,0:T(8,128)(2,1)S(1)} %add_convert_fusion.own_ref), channel_id=1, source_target_pairs={{0,2},{1,3},{2,0},{3,1},{4,6},{5,7},{6,4},{7,5},{8,10},{9,11},{10,... | collective-permute-start | bytes 589832 | tf_op jit(solution)/shard_map/ppermute | solution.py:29
  165.9 17.7 %collective-permute-start.15 = (bf16[128,768]{1,0:T(8,128)(2,1)S(1)}, bf16[128,768]{1,0:T(8,128)(2,1)S(1)}, u32[]{:S(2)}, u32[]{:S(2)}) collective-permute-start(bf16[128,768]{1,0:T(8,128)(2,1)S(1)} %get-tuple-element.107), channel_id=1, source_target_pairs={{0,1},{1,0},{2,3},{3,2},{4,5},{5,4},{6,7},{7,6},{8,9},{9,8},{10,11... | collective-permute-start | bytes 589832 | tf_op jit(solution)/shard_map/ppermute | solution.py:29
  177.2 18.5 %collective-permute-start.43 = (bf16[192,768]{1,0:T(8,128)(2,1)S(1)}, bf16[192,768]{1,0:T(8,128)(2,1)S(1)}, u32[]{:S(2)}, u32[]{:S(2)}) collective-permute-start(bf16[192,768]{1,0:T(8,128)(2,1)S(1)} %get-tuple-element.150), channel_id=1, source_target_pairs={{0,8},{4,12},{8,0},{12,4},{16,24},{20,28},{24,16},{28,20},{1,9},{5... | collective-permute-start | bytes 884744 | tf_op jit(solution)/shard_map/ppermute | solution.py:29
  177.4 44.6 %collective-permute-start.50 = (bf16[96,1536]{1,0:T(8,128)(2,1)S(1)}, bf16[96,1536]{1,0:T(8,128)(2,1)S(1)}, u32[]{:S(2)}, u32[]{:S(2)}) collective-permute-start(bf16[96,1536]{1,0:T(8,128)(2,1)S(1)} %get-tuple-element.166), channel_id=1, source_target_pairs={{0,16},{4,20},{8,24},{12,28},{16,0},{20,4},{24,8},{28,12},{1,17},{... | collective-permute-start | bytes 884744 | tf_op jit(solution)/shard_map/ppermute | solution.py:29
  180.1 24.9 %collective-permute-start.39 = (bf16[192,768]{1,0:T(8,128)(2,1)S(1)}, bf16[192,768]{1,0:T(8,128)(2,1)S(1)}, u32[]{:S(2)}, u32[]{:S(2)}) collective-permute-start(bf16[192,768]{1,0:T(8,128)(2,1)S(1)} %get-tuple-element.143), channel_id=1, source_target_pairs={{0,8},{4,12},{8,0},{12,4},{16,24},{20,28},{24,16},{28,20},{1,9},{5... | collective-permute-start | bytes 884744 | tf_op jit(solution)/shard_map/ppermute | solution.py:29
  181.8 40.3 %collective-permute-start.47 = (bf16[96,1536]{1,0:T(8,128)(2,1)S(1)}, bf16[96,1536]{1,0:T(8,128)(2,1)S(1)}, u32[]{:S(2)}, u32[]{:S(2)}) collective-permute-start(bf16[96,1536]{1,0:T(8,128)(2,1)S(1)} %get-tuple-element.160), channel_id=1, source_target_pairs={{0,16},{4,20},{8,24},{12,28},{16,0},{20,4},{24,8},{28,12},{1,17},{... | collective-permute-start | bytes 884744 | tf_op jit(solution)/shard_map/ppermute | solution.py:29
  188.0 20.7 %collective-permute-start.16 = (bf16[128,768]{1,0:T(8,128)(2,1)S(1)}, bf16[128,768]{1,0:T(8,128)(2,1)S(1)}, u32[]{:S(2)}, u32[]{:S(2)}) collective-permute-start(bf16[128,768]{1,0:T(8,128)(2,1)S(1)} %add_convert_fusion.4.own_ref), channel_id=1, source_target_pairs={{0,2},{1,3},{2,0},{3,1},{4,6},{5,7},{6,4},{7,5},{8,10},{9,11},{10,... | collective-permute-start | bytes 589832 | tf_op jit(solution)/shard_map/ppermute | solution.py:29
  195.7 10.0 %collective-permute-start.52 = (f32[24,768]{1,0:T(8,128)S(1)}, f32[24,768]{1,0:T(8,128)S(1)}, u32[]{:S(2)}, u32[]{:S(2)}) collective-permute-start(f32[24,768]{1,0:T(8,128)S(1)} %add.74), channel_id=1, source_target_pairs={{0,8},{4,12},{8,0},{12,4},{16,24},{20,28},{24,16},{28,20},{1,9},{5... | collective-permute-start | bytes 221192 | tf_op jit(solution)/shard_map/ppermute | solution.py:29
  205.0 18.2 %collective-permute-start.44 = (bf16[96,768]{1,0:T(8,128)(2,1)S(1)}, bf16[96,768]{1,0:T(8,128)(2,1)S(1)}, u32[]{:S(2)}, u32[]{:S(2)}) collective-permute-start(bf16[96,768]{1,0:T(8,128)(2,1)S(1)} %get-tuple-element.152), channel_id=1, source_target_pairs={{0,16},{4,20},{8,24},{12,28},{16,0},{20,4},{24,8},{28,12},{1,17},{... | collective-permute-start | bytes 442376 | tf_op jit(solution)/shard_map/ppermute | solution.py:29
  205.8 17.4 %collective-permute-start.40 = (bf16[96,768]{1,0:T(8,128)(2,1)S(1)}, bf16[96,768]{1,0:T(8,128)(2,1)S(1)}, u32[]{:S(2)}, u32[]{:S(2)}) collective-permute-start(bf16[96,768]{1,0:T(8,128)(2,1)S(1)} %get-tuple-element.145), channel_id=1, source_target_pairs={{0,16},{4,20},{8,24},{12,28},{16,0},{20,4},{24,8},{28,12},{1,17},{... | collective-permute-start | bytes 442376 | tf_op jit(solution)/shard_map/ppermute | solution.py:29
  208.6 12.8 %collective-permute-start.53 = (f32[24,768]{1,0:T(8,128)S(1)}, f32[24,768]{1,0:T(8,128)S(1)}, u32[]{:S(2)}, u32[]{:S(2)}) collective-permute-start(f32[24,768]{1,0:T(8,128)S(1)} %add.75.total_ref), channel_id=1, source_target_pairs={{0,16},{4,20},{8,24},{12,28},{16,0},{20,4},{24,8},{28,12},{1,17},{... | collective-permute-start | bytes 221192 | tf_op jit(solution)/shard_map/ppermute | solution.py:29
  (44 other events, 371.4 us)

commit v3 on v2

v3 whole, which is shorter than its diff:
```python
import jax
import jax.numpy as jnp
from jax import lax
from jax.experimental import pallas as pl
from jax.experimental.pallas import tpu as pltpu
from jax.sharding import PartitionSpec as P

D = 768
HD = 64
FF = 3072
LAYERS = 2
SPAN = 4
PAIR = 2

epsilon = 1e-05
gelu_c = 0.7978845608028654
f32 = jnp.float32
bf16 = jnp.bfloat16
VMEM_LIMIT = 28 * 1024 * 1024


def shifted(array, axis, by):
    length = lax.axis_size(axis)
    pairs = [(i, i + by) for i in range(length) if 0 <= i + by < length]
    return lax.ppermute(array, axis, pairs)


def swapped(array, axis, bit):
    length = lax.axis_size(axis)
    return lax.ppermute(array, axis, [(i, i ^ bit) for i in range(length)])


def bits_of(axis):
    length = lax.axis_size(axis)
    found, bit = [], 1
    while bit < length:
        found.append(bit)
        bit *= 2
    assert bit == length
    return found


def call(kernel, outs, args, flops=1e8):
    spec = pl.BlockSpec(memory_space=pltpu.VMEM)
    shapes = [jax.ShapeDtypeStruct(shape, dtype) for shape, dtype in outs]
    return pl.pallas_call(
        kernel,
        out_shape=shapes,
        in_specs=[spec] * len(args),
        out_specs=[spec] * len(outs),
        compiler_params=pltpu.CompilerParams(vmem_limit_bytes=VMEM_LIMIT),
        cost_estimate=pl.CostEstimate(flops=1, bytes_accessed=1, transcendentals=0),
    )(*args)


def mm(left, right, contract=((1,), (0,))):
    return lax.dot_general(left, right, (contract, ((), ())), preferred_element_type=f32)


NT = ((1,), (1,))
TN = ((0,), (0,))


def normalize(values_in):
    mean_v = jnp.mean(values_in, axis=-1, keepdims=True)
    centred = values_in - mean_v
    var_v = jnp.mean(centred * centred, axis=-1, keepdims=True)
    rstd = lax.rsqrt(var_v + epsilon)
    return (centred * rstd, rstd)


def norm_bwd(grad_in, normed, rstd, gain):
    scaled = grad_in * gain
    inner = jnp.mean(scaled, axis=-1, keepdims=True)
    along = jnp.mean(scaled * normed, axis=-1, keepdims=True)
    return rstd * (scaled - inner - normed * along)


def gain(small, layer, which):
    return small[0][layer, which : which + 1]


def bias(small, layer, which):
    return small[1][layer, which : which + 1]


def ff_bias_row(small, layer):
    return small[2][layer : layer + 1]


def qv_bias(small, layer, which):
    return small[3][layer, which : which + 1]


def column_sum(values_in):
    return jnp.sum(values_in, axis=0, keepdims=True)


def gelu_pair(pre_act):
    inner = gelu_c * (pre_act + 0.044715 * pre_act * pre_act * pre_act)
    tanh_v = jnp.tanh(inner)
    value_out = 0.5 * pre_act * (1.0 + tanh_v)
    slope = 0.5 * (1.0 + tanh_v) + 0.5 * pre_act * (1.0 - tanh_v * tanh_v) * gelu_c * (
        1.0 + 3.0 * 0.044715 * pre_act * pre_act
    )
    return (value_out, slope)


def joined(own_ref, other_ref):
    high = (lax.axis_index("tensor") & 1) == 1
    own, other = own_ref[...].astype(f32), other_ref[...].astype(f32)
    return jnp.concatenate(
        [jnp.where(high, other, own), jnp.where(high, own, other)], axis=0
    )


def split_halves(total, keep_ref, give_ref):
    half = total.shape[0] // 2
    high = (lax.axis_index("tensor") & 1) == 1
    low_rows, high_rows = total[:half], total[half:]
    keep_ref[...] = jnp.where(high, high_rows, low_rows)
    give_ref[...] = jnp.where(high, low_rows, high_rows).astype(bf16)


def place_pieces(pieces, out_ref):
    mine = lax.axis_index("tensor")
    rows = pieces[0].shape[0]
    for number, piece in enumerate(pieces):
        start = pl.multiple_of((mine ^ number) * rows, rows)
        out_ref[pl.ds(start, rows), :] = piece[...].astype(out_ref.dtype)


def gathered(piece):
    pieces = {0: piece}
    for bit in bits_of("tensor")[::-1]:
        for number in list(pieces):
            pieces[number ^ bit] = swapped(pieces[number], "tensor", bit)
    return [pieces[number] for number in range(len(pieces))]


def after(value, *others):
    return lax.optimization_barrier((value, *others))[0]


def exchanged(keep, give, launch=None, due=()):
    bits = bits_of("tensor")
    total = keep + swapped(give, "tensor", bits[0]).astype(f32)
    for bit in bits[1:]:
        rounded = after(total.astype(bf16), *due)
        other = swapped(rounded, "tensor", bit)
        if launch is not None and bit == bits[-1]:
            launch(rounded)
        total = rounded.astype(f32) + other.astype(f32)
    rounded = total.astype(bf16)
    return [rounded, swapped(rounded, "tensor", bits[0])]


def project_rows(hidden, layer, refs, outs):
    small, (w_qkv, pick) = refs[:4], refs[4:]
    h_ref, picked_ref, q_ref, kv_ref = outs
    width = q_ref.shape[1]
    hat, _ = normalize(hidden)
    act = (hat * gain(small, layer, 0) + bias(small, layer, 0)).astype(bf16)
    kv = mm(act, w_qkv[layer, width:], NT)
    values = kv[:, width:] + qv_bias(small, layer, 1)
    kv_ref[...] = jnp.concatenate([kv[:, :width], values], axis=1).astype(bf16)
    query = mm(act, w_qkv[layer, :width], NT)
    q_ref[...] = (query + qv_bias(small, layer, 0)).astype(bf16)
    picked_ref[...] = mm(act, pick[...]).astype(bf16)


def project_first(tokens, pieces, params, pick):
    count = len(pieces)
    own_rows = tokens.shape[0]
    rows = (count + 1) * own_rows
    width = params["w_out"].shape[1]
    gains, biases, _, qv = params["small"]
    far = [tokens, gains, biases, qv, params["w_qkv"]]
    near_shapes = [a.shape for a in far[:4]] + [(1,) + far[4].shape[1:]]
    many = len(far)

    def kernel(*refs):
        ins, far_refs, pick_ref = refs[:count], refs[count : count + many], refs[count + many]
        outs, near, sems = refs[-many - 5 : -many - 1], refs[-many - 1 : -1], refs[-1]
        sources = [*far_refs[:-1], far_refs[-1].at[pl.ds(0, 1)]]
        copies = [pltpu.make_async_copy(sources[k], near[k], sems.at[k]) for k in range(many)]
        for copy in copies:
            copy.start()
        for copy in copies:
            copy.wait()
        place_pieces([near[0], *ins], outs[0])
        small = (near[1], near[2], None, near[3])
        project_rows(outs[0][...], 0, [*small, near[4], pick_ref], outs)

    spec = pl.BlockSpec(memory_space=pltpu.VMEM)
    return pl.pallas_call(
        kernel,
        out_shape=[
            jax.ShapeDtypeStruct((rows, D), f32),
            jax.ShapeDtypeStruct((rows, D), bf16),
            jax.ShapeDtypeStruct((rows, width), bf16),
            jax.ShapeDtypeStruct((rows, 2 * width), bf16),
        ],
        in_specs=[spec] * count + [pl.BlockSpec(memory_space=pltpu.HBM)] * many + [spec],
        out_specs=[spec] * 4,
        scratch_shapes=[
            pltpu.VMEM(shape, a.dtype) for shape, a in zip(near_shapes, far, strict=True)
        ]
        + [pltpu.SemaphoreType.DMA((many,))],
        compiler_params=pltpu.CompilerParams(vmem_limit_bytes=VMEM_LIMIT),
        cost_estimate=pl.CostEstimate(flops=1, bytes_accessed=1, transcendentals=0),
    )(*pieces, *far, pick)


def project_next(mid, pair, layer, params, pick):
    rows = mid.shape[0]
    width = params["w_out"].shape[1]

    def kernel(mid_ref, own_ref, other_ref, *refs):
        ins, outs = refs[:6], refs[6:]
        hidden = mid_ref[...] + joined(own_ref, other_ref) + bias(ins, layer - 1, 3)
        outs[0][...] = hidden
        project_rows(hidden, layer, ins, outs)

    return call(
        kernel,
        [((rows, D), f32), ((rows, D), bf16), ((rows, width), bf16), ((rows, 2 * width), bf16)],
        [mid, *pair, *params["small"], params["w_qkv"], pick],
    )


def head_lanes(shape, head):
    lane = lax.broadcasted_iota(jnp.int32, shape, 1)
    return (lane >= head * HD) & (lane < (head + 1) * HD)


def allowed_of(seg_q, seg_k, rows):
    shape = (rows, SPAN * rows)
    query = lax.broadcasted_iota(jnp.int32, shape, 0)
    key = lax.broadcasted_iota(jnp.int32, shape, 1)
    return (key <= query + (SPAN - 1) * rows) & (seg_q[...] == seg_k[...])


def split_shapes(rows):
    return [((rows // 2, D), f32), ((rows // 2, D), bf16)]


def attend(q, kv_parts, segs, picked1, layer, params):
    rows, width = q.shape
    half = D // 2
    pad = -(half + width) % 128
    heads = width // HD

    def kernel(q_ref, *refs):
        kv_refs, refs = refs[:SPAN], refs[SPAN:]
        seg_q, seg_k, w_out, p1_ref, att_ref, lse_ref, sent_ref, keep_ref, give_ref = refs
        allowed = allowed_of(seg_q, seg_k, rows)
        kv_all = jnp.concatenate([r[...] for r in kv_refs], axis=0)
        keys, values = kv_all[:, :width], kv_all[:, width:]
        query = q_ref[...]
        mixed = jnp.zeros((rows, width), f32)
        logs = jnp.zeros((rows, 128), f32)
        lane = lax.broadcasted_iota(jnp.int32, (rows, 128), 1)
        for head in range(heads):
            inside = head_lanes((rows, width), head)
            scores = mm(jnp.where(inside, query, 0), keys, NT) * HD ** (-0.5)
            scores = jnp.where(allowed, scores, -1e30)
            top = jnp.max(scores, axis=-1, keepdims=True)
            log_total = top + jnp.log(jnp.sum(jnp.exp(scores - top), axis=-1, keepdims=True))
            weights = jnp.exp(scores - log_total).astype(bf16)
            mixed = jnp.where(inside, mm(weights, values), mixed)
            logs = jnp.where(lane == head, log_total, logs)
        att = mixed.astype(bf16)
        att_ref[...] = att
        sent_ref[:, :half] = p1_ref[:, half:]
        sent_ref[:, half : half + width] = att
        if pad:
            sent_ref[:, half + width :] = jnp.zeros((rows, pad), bf16)
        lse_ref[...] = logs
        split_halves(mm(att, w_out[layer]), keep_ref, give_ref)

    return call(
        kernel,
        [((rows, width), bf16), ((rows, 128), f32), ((rows, half + width + pad), bf16)]
        + split_shapes(rows),
        [q, *kv_parts, *segs, params["w_out"], picked1],
    )


def feed_forward(hidden, pair, layer, params, pick):
    rows = hidden.shape[0]
    half = D // 2
    inner = params["w_up"].shape[2]

    def kernel(h_ref, own_ref, other_ref, g_ref, b_ref, f_ref, q_ref, up, down, pick_ref,
               mid_ref, slope_ref, sent_ref, kept_ref, keep_ref, give_ref):
        small = (g_ref, b_ref, f_ref, q_ref)
        mid = h_ref[...] + joined(own_ref, other_ref) + bias(small, layer, 1)
        mid_ref[...] = mid
        hat, _ = normalize(mid)
        act2 = (hat * gain(small, layer, 1) + bias(small, layer, 2)).astype(bf16)
        pre = mm(act2, up[layer]) + ff_bias_row(small, layer)
        value, slope = gelu_pair(pre)
        act3 = value.astype(bf16)
        split_halves(mm(act3, down[layer]), keep_ref, give_ref)
        slope_ref[...] = slope
        picked2 = mm(act2, pick_ref[...]).astype(bf16)
        kept_ref[...] = picked2[:, :half]
        sent_ref[:, :half] = picked2[:, half:]
        sent_ref[:, half:] = act3

    return call(
        kernel,
        [
            ((rows, D), f32),
            ((rows, inner), f32),
            ((rows, half + inner), bf16),
            ((rows, half), bf16),
        ]
        + split_shapes(rows),
        [hidden, *pair]
        + [*params["small"], params["w_up"], params["w_down"]]
        + [pick],
    )


def last_rows(mid, pair, params, own_rows):
    def kernel(mid_ref, own_ref, other_ref, biases, out_ref, all_ref):
        total = mid_ref[...] + joined(own_ref, other_ref)
        all_ref[...] = total + biases[LAYERS - 1, 3:4]
        start = pl.multiple_of(lax.axis_index("tensor") * own_rows, own_rows)
        out_ref[...] = all_ref[pl.ds(start, own_rows), :].astype(bf16)

    args = [mid, *pair, params["small"][1]]
    return call(kernel, [((own_rows, D), bf16), (mid.shape, f32)], args)[0]


def norm1_grad(gmid_ref, own_ref, other_ref, h_ref, gains, layer):
    d_norm = joined(own_ref, other_ref)
    hat, rstd = normalize(h_ref[...])
    grad = gmid_ref[...] + norm_bwd(d_norm, hat, rstd, gains[layer, 0:1])
    return grad, column_sum(d_norm * hat), column_sum(d_norm)


def mlp_grad(grad, layer, refs, outs):
    slope_ref, up, down, pick_ref = refs
    sent_ref, small_ref, kept_ref, keep_ref, give_ref = outs
    half = D // 2
    grad_b = grad.astype(bf16)
    d_pre = mm(grad_b, down[layer], NT) * slope_ref[...]
    pre_b = d_pre.astype(bf16)
    split_halves(mm(pre_b, up[layer], NT), keep_ref, give_ref)
    picked = mm(grad_b, pick_ref[...]).astype(bf16)
    kept_ref[...] = picked[:, :half]
    sent_ref[:, :half] = picked[:, half:]
    sent_ref[:, half:] = pre_b
    small_ref[0:1, :] = column_sum(d_pre)
    small_ref[1:2, :] = column_sum(grad)


def mlp_outs(rows, inner):
    assert inner == D
    return [
        ((rows, D), f32),
        ((rows, D // 2 + inner), bf16),
        ((8, D), f32),
        ((rows, D // 2), bf16),
    ] + split_shapes(rows)


def mlp_grad_last(pieces, slope, params, pick):
    count = len(pieces)
    rows, inner = slope.shape

    def kernel(*refs):
        ins, outs = refs[: count + 4], refs[count + 4 :]
        place_pieces(ins[:count], outs[0])
        outs[2][...] = jnp.zeros((8, D), f32)
        mlp_grad(outs[0][...], LAYERS - 1, ins[count:], outs[1:])

    return call(
        kernel,
        mlp_outs(rows, inner),
        [*pieces, slope, params["w_up"], params["w_down"], pick],
    )


def mlp_grad_next(gmid, pair, hidden, slope, layer, params, pick):
    rows, inner = slope.shape

    def kernel(gmid_ref, own_ref, other_ref, h_ref, gains, *refs):
        ins, outs = refs[:4], refs[4:]
        grad, g_gain, g_bias = norm1_grad(gmid_ref, own_ref, other_ref, h_ref, gains, layer + 1)
        outs[0][...] = grad
        outs[2][...] = jnp.zeros((8, D), f32)
        mlp_grad(grad, layer, ins, outs[1:])
        outs[2][2:3, :] = g_gain
        outs[2][3:4, :] = g_bias

    return call(
        kernel,
        mlp_outs(rows, inner),
        [gmid, *pair, hidden, params["small"][0], slope, params["w_up"], params["w_down"], pick],
    )


def attend_grad(grad, pair, mid, q, kv_parts, segs, att, lse, layer, params, pick):
    rows, width = q.shape
    heads = width // HD
    back = SPAN - 1

    def kernel(g_ref, own_ref, other_ref, mid_ref, q_ref, *refs):
        kv_refs, refs = refs[:SPAN], refs[SPAN:]
        seg_q, seg_k, att_ref, lse_ref, gains, w_out, pick_ref = refs[:7]
        gmid_ref, picked_ref, dq_ref, dkv_ref, small_ref = refs[7:12]
        away_refs = refs[12:]
        d_norm = joined(own_ref, other_ref)
        hat, rstd = normalize(mid_ref[...])
        gmid = g_ref[...] + norm_bwd(d_norm, hat, rstd, gains[layer, 1:2])
        gmid_ref[...] = gmid
        mid_b = gmid.astype(bf16)
        d_att = mm(mid_b, w_out[layer], NT).astype(bf16)
        allowed = allowed_of(seg_q, seg_k, rows)
        kv_all = jnp.concatenate([r[...] for r in kv_refs], axis=0)
        keys, values = kv_all[:, :width], kv_all[:, width:]
        query, logs = q_ref[...], lse_ref[...]
        weighed = d_att.astype(f32) * att_ref[...].astype(f32)
        d_query = jnp.zeros((rows, width), f32)
        d_keys = jnp.zeros((SPAN * rows, width), f32)
        d_values = jnp.zeros((SPAN * rows, width), f32)
        for head in range(heads):
            inside = head_lanes((rows, width), head)
            query_h = jnp.where(inside, query, 0)
            d_att_h = jnp.where(inside, d_att, 0)
            scores = mm(query_h, keys, NT) * HD ** (-0.5)
            scores = jnp.where(allowed, scores, -1e30)
            probs = jnp.exp(scores - logs[:, head : head + 1])
            delta = jnp.sum(jnp.where(inside, weighed, 0.0), axis=-1, keepdims=True)
            d_prob = mm(d_att_h, values, NT)
            d_score = (probs * (d_prob - delta) * HD ** (-0.5)).astype(bf16)
            d_query = jnp.where(inside, mm(d_score, keys), d_query)
            d_keys = d_keys + mm(d_score, query_h, TN)
            d_values = d_values + mm(probs.astype(bf16), d_att_h, TN)
        d_kv = jnp.concatenate([d_keys, d_values], axis=1)
        dq_ref[...] = d_query
        dkv_ref[...] = d_kv[back * rows :]
        for distance in range(1, SPAN):
            block = back - distance
            away_refs[distance - 1][...] = d_kv[block * rows : (block + 1) * rows].astype(bf16)
        picked_ref[...] = mm(mid_b, pick_ref[...]).astype(bf16)
        small_ref[...] = jnp.zeros((8, D), f32)
        small_ref[0:1, :] = column_sum(d_norm * hat)
        small_ref[1:2, :] = column_sum(d_norm)
        small_ref[2:3, :] = column_sum(gmid)

    return call(
        kernel,
        [
            ((rows, D), f32),
            ((rows, D), bf16),
            ((rows, width), f32),
            ((rows, 2 * width), f32),
            ((8, D), f32),
        ]
        + [((rows, 2 * width), bf16)] * back,
        [grad, *pair, mid, q, *kv_parts, *segs, att, lse]
        + [params["small"][0], params["w_out"], pick],
    )


def project_grad(dq, dkv, arrived, picked, layer, params):
    rows, width = dq.shape
    half = D // 2
    pad = -(half + 3 * width) % 128

    def kernel(dq_ref, dkv_ref, *refs):
        near, refs = refs[: SPAN - 1], refs[SPAN - 1 :]
        picked_ref, w_qkv, sent_ref, small_ref, keep_ref, give_ref = refs
        d_kv = dkv_ref[...]
        for ref in near:
            d_kv = d_kv + ref[...].astype(f32)
        d_query = dq_ref[...]
        query_b, kv_b = d_query.astype(bf16), d_kv.astype(bf16)
        part = mm(kv_b, w_qkv[layer, width:]) + mm(query_b, w_qkv[layer, :width])
        split_halves(part, keep_ref, give_ref)
        sent_ref[:, :half] = picked_ref[:, half:]
        sent_ref[:, half : half + 2 * width] = kv_b
        sent_ref[:, half + 2 * width : half + 3 * width] = query_b
        if pad:
            sent_ref[:, half + 3 * width :] = jnp.zeros((rows, pad), bf16)
        small_ref[...] = jnp.zeros((8, D), f32)
        small_ref[0:1, :width] = column_sum(d_query)
        small_ref[1:2, :width] = column_sum(d_kv)[:, width:]

    return call(
        kernel,
        [((rows, half + 3 * width + pad), bf16), ((8, D), f32)] + split_shapes(rows),
        [dq, dkv, *arrived, picked, params["w_qkv"]],
    )


def small_rows(count):
    rows = 8 * LAYERS + LAYERS * count
    return rows + -rows % 8


def local_small(keep, give, hidden, mlp_small, att_small, qv_small, count, width):
    share = 1.0 / count

    def kernel(keep_ref, give_ref, h_ref, *refs):
        mlp, att, qv, out = refs[:LAYERS], refs[LAYERS : 2 * LAYERS], refs[2 * LAYERS : -1], refs[-1]
        mine = lax.axis_index("tensor")
        part = joined(keep_ref, give_ref)
        hat, _ = normalize(h_ref[...])
        out[...] = jnp.zeros(out.shape, f32)
        for layer in range(LAYERS):
            gain1 = column_sum(part * hat) if layer == 0 else mlp[layer - 1][2:3, :] * share
            bias1 = column_sum(part) if layer == 0 else mlp[layer - 1][3:4, :] * share
            at = 2 * layer
            out[at : at + 1, :] = gain1
            out[at + 1 : at + 2, :] = att[layer][0:1, :] * share
            at = 2 * LAYERS + 4 * layer
            out[at : at + 1, :] = bias1
            out[at + 1 : at + 2, :] = att[layer][2:3, :] * share
            out[at + 2 : at + 3, :] = att[layer][1:2, :] * share
            out[at + 3 : at + 4, :] = mlp[layer][1:2, :] * share
            for target in range(count):
                here = mine == target
                at = 6 * LAYERS + 2 * layer
                lanes = slice(target * width, (target + 1) * width)
                out[at : at + 2, lanes] = jnp.where(here, qv[layer][0:2, :width], 0.0)
                at = 8 * LAYERS + layer * count + target
                out[at : at + 1, :] = jnp.where(here, mlp[layer][0:1, :], 0.0)

    args = [keep, give, hidden, *mlp_small, *att_small, *qv_small]
    return call(kernel, [((small_rows(count), D), f32)], args, 1e6)[0]


def first_grad(gmid, pair, hidden, params, own_rows):
    def kernel(gmid_ref, own_ref, other_ref, h_ref, gains, in_ref, g_ref):
        g_ref[...] = norm1_grad(gmid_ref, own_ref, other_ref, h_ref, gains, 0)[0]
        start = pl.multiple_of(lax.axis_index("tensor") * own_rows, own_rows)
        in_ref[...] = g_ref[pl.ds(start, own_rows), :].astype(bf16)

    args = [gmid, *pair, hidden, params["small"][0]]
    return call(kernel, [((own_rows, D), bf16), (gmid.shape, f32)], args)[0]


def small_outs(total, other, count):
    def kernel(total_ref, other_ref, gains, biases, qv, ffb):
        both = total_ref[...] + other_ref[...]
        for layer in range(LAYERS):
            gains[layer] = both[2 * layer : 2 * layer + 2]
            at = 2 * LAYERS + 4 * layer
            biases[layer] = both[at : at + 4]
            at = 6 * LAYERS + 2 * layer
            qv[layer] = both[at : at + 2]
            for target in range(count):
                at = 8 * LAYERS + layer * count + target
                ffb[layer : layer + 1, target * D : (target + 1) * D] = both[at : at + 1]

    return call(
        kernel,
        [
            ((LAYERS, 2, D), f32),
            ((LAYERS, 4, D), f32),
            ((LAYERS, 2, D), f32),
            ((LAYERS, count * D), f32),
        ],
        [total, other],
        1e5,
    )


def split_rows(total, bit, block, send_ref, keep_ref):
    mine = lax.axis_index("dp")
    high = jnp.where((mine & bit) != 0, 1, 0)
    pairs = total.shape[0] // (2 * block)
    for pair in range(pairs):
        for which in range(2):
            rows = total[(2 * pair + which) * block : (2 * pair + which + 1) * block]
            out = slice(pair * block, (pair + 1) * block)

            @pl.when(high == which)
            def _():
                keep_ref[out, :] = rows

            @pl.when(high != which)
            def _():
                send_ref[out, :] = rows.astype(bf16)


def split_plain(total, bit, block):
    pairs = total.shape[0] // (2 * block)
    split = total.reshape(pairs, 2, block, total.shape[1])
    high = jnp.where((lax.axis_index("dp") & bit) != 0, 1, 0)
    send = lax.dynamic_index_in_dim(split, 1 - high, 1, keepdims=False)
    keep = lax.dynamic_index_in_dim(split, high, 1, keepdims=False)
    return send.reshape(-1, total.shape[1]).astype(bf16), keep.reshape(-1, total.shape[1])


class Halving:
    def __init__(self, products, wide):
        self.products, self.wide = products, wide
        self.bits = [bit for bit in bits_of("dp") if bit != PAIR]
        self.block = D // lax.axis_size("dp")
        self.place = 0

    def begin(self, sources):
        half = D // 2
        flat = [array for source in sources for array in source]
        shape = (half // 2, self.wide)
        spots = self.products

        def products_of(refs):
            done = []
            for (la, kept_at, sent_at), (ra, r0, r1) in spots:
                kept = refs[3 * la + 2][:, kept_at : kept_at + half]
                given = refs[3 * la + 1][:, sent_at : sent_at + half]
                left = jnp.concatenate([kept, given], axis=0)
                right = [refs[3 * ra][:, r0:r1], refs[3 * ra + 1][:, r0:r1]]
                done.append(mm(left, jnp.concatenate(right, axis=0), TN))
            return jnp.concatenate(done, axis=1)

        bit, block, count = self.bits[0], self.block, len(flat)
        if block % 16:

            def kernel(*refs):
                refs[count][...] = products_of(refs)

            total = call(kernel, [((half, self.wide), f32)], flat, 3e8)[0]
            self.send, self.keep = split_plain(total, bit, block)
        else:

            def kernel(*refs):
                split_rows(products_of(refs), bit, block, refs[count], refs[count + 1])

            self.send, self.keep = call(kernel, [(shape, bf16), (shape, f32)], flat, 3e8)

    def launch(self, *gates):
        send = after(self.send, *gates) if gates else self.send
        self.arrived = swapped(send, "dp", self.bits[self.place])

    def absorb(self):
        self.place += 1
        bit, block = self.bits[self.place], self.block
        if block % 16:
            total = self.keep + self.arrived.astype(f32)
            self.send, self.keep = split_plain(total, bit, block)
            return

        def kernel(keep_ref, arrived_ref, send_ref, kept_ref):
            total = keep_ref[...] + arrived_ref[...].astype(f32)
            split_rows(total, bit, block, send_ref, kept_ref)

        shape = (self.keep.shape[0] // 2, self.wide)
        args = [self.keep, self.arrived]
        self.send, self.keep = call(kernel, [(shape, bf16), (shape, f32)], args, 1e6)

    def finish(self):
        while self.place < len(self.bits) - 1:
            self.absorb()
            self.launch()
        return [self.keep, self.arrived]


def mlp_outputs(parts, block, inner):
    def kernel(*refs):
        up, down = refs[-2:]
        for layer in range(LAYERS):
            total = refs[2 * layer][...] + refs[2 * layer + 1][...].astype(f32)
            up[layer] = total[:, :inner]
            down[layer] = total[:, inner:]

    args = [a for pair in parts for a in pair]
    return call(kernel, [((LAYERS, block, inner), f32)] * 2, args, 1e6)


def att_outputs(parts, block, width):
    def kernel(*refs):
        qkv, out = refs[-2:]
        for layer in range(LAYERS):
            total = refs[2 * layer][...] + refs[2 * layer + 1][...].astype(f32)
            qkv[layer, 0] = total[:, 2 * width : 3 * width]
            qkv[layer, 1] = total[:, :width]
            qkv[layer, 2] = total[:, width : 2 * width]
            out[layer] = total[:, 3 * width :]

    args = [a for pair in parts for a in pair]
    return call(
        kernel,
        [((LAYERS, 3, block, width), f32), ((LAYERS, block, width), f32)],
        args,
        1e6,
    )


def shards(
    tokens, cotangent, segments, w_qkv, qv_bias, w_out, w_up, w_down, ff_bias, gains, biases
):
    tensor_count = lax.axis_size("tensor")
    dp_count = lax.axis_size("dp")
    dp_index = lax.axis_index("dp")
    own_rows = tokens.shape[0]
    rows = own_rows * tensor_count
    width = w_out.shape[1]
    inner = w_up.shape[2]
    half = D // 2
    block = D // dp_count
    joint = w_qkv.transpose(0, 2, 3, 1).reshape(LAYERS, 3 * width, D)
    params = {
        "small": [gains, biases, ff_bias, qv_bias],
        "w_qkv": joint,
        "w_out": w_out,
        "w_up": w_up,
        "w_down": w_down,
    }
    seg_q = lax.dynamic_slice_in_dim(segments, dp_index * rows, rows)[:, None]
    padded = jnp.concatenate([jnp.full(((SPAN - 1) * rows,), -1, jnp.int32), segments])
    seg_k = lax.dynamic_slice_in_dim(padded, dp_index * rows, SPAN * rows)[None, :]
    segs = [seg_q, seg_k]
    column = lax.broadcasted_iota(jnp.int32, (D, D), 1)
    side = ((dp_index >> 1) & 1) ^ (column // half)
    column = column % half
    piece = column // block
    source = ((piece // 2) * 4 + side * 2 + piece % 2) * block + column % block
    pick = (lax.broadcasted_iota(jnp.int32, (D, D), 0) == source).astype(bf16)

    def paired(sent, kept, gate):
        return [sent, swapped(after(sent, gate), "dp", PAIR), kept]

    mlp_work = [
        Halving([((0, 0, 0), (1, half, half + inner)), ((1, 0, 0), (0, half, half + inner))], 2 * inner)
        for _ in range(LAYERS)
    ]
    att_work = [
        Halving([((0, 0, 0), (1, half, half + 3 * width)), ((1, 0, 0), (0, half, half + width))], 4 * width)
        for _ in range(LAYERS)
    ]
    token_pieces = gathered(tokens)
    saved, rows_a, rows_b = [], [None] * LAYERS, [None] * LAYERS
    cot_pieces = None
    mid = pair = None
    for layer in range(LAYERS):
        if layer == 0:
            hidden, picked1, q, kv = project_first(tokens, token_pieces[1:], params, pick)
        else:
            hidden, picked1, q, kv = project_next(mid, pair, layer, params, pick)
        kv_parts = [shifted(kv, "dp", distance) for distance in range(SPAN - 1, 0, -1)] + [kv]
        if layer:
            q = after(q, rows_a[layer - 1][1], rows_b[layer - 1][1])
        att, lse, sent_a, keep, give = attend(q, kv_parts, segs, picked1, layer, params)

        def launch_a(gate):
            nonlocal cot_pieces
            rows_a[layer] = paired(sent_a, picked1, gate)
            if layer == 0:
                cot_pieces = gathered(after(cotangent, gate))

        pair = exchanged(keep, give, launch_a)
        mid, slope, sent_b, kept_b, keep, give = feed_forward(hidden, pair, layer, params, pick)
        saved.append((hidden, q, kv_parts, att, lse, mid, slope))
        if layer < LAYERS - 1:

            def launch_b(gate):
                rows_b[layer] = paired(sent_b, kept_b, gate)

            pair = exchanged(keep, give, launch_b)
            pair[0] = after(pair[0], cot_pieces[-1])
    last_total, last_give = keep, give

    mlp_small, att_small, qv_small = ([None] * LAYERS for _ in range(3))
    gmid = last_pair = None
    for layer in range(LAYERS - 1, -1, -1):
        last = layer == LAYERS - 1
        hidden, q, kv_parts, att, lse, mid, slope = saved[layer]
        if last:
            grad, sent1, mlp_small[layer], kept1, keep, give = mlp_grad_last(
                cot_pieces, slope, params, pick
            )
        else:
            grad, sent1, mlp_small[layer], kept1, keep, give = mlp_grad_next(
                gmid, pair, saved[layer + 1][0], slope, layer, params, pick
            )
        rows_1 = None

        def launch_1(gate):
            nonlocal rows_1
            if last:
                rows_b[layer] = paired(sent_b, kept_b, gate)
            rows_1 = paired(sent1, kept1, gate)

        if last:
            pair = exchanged(keep, give, launch_1)
            pair[0] = after(pair[0], rows_a[layer][1])
        else:
            later = layer + 1
            mlp_work[later].absorb()
            pair = exchanged(keep, give, launch_1, [mlp_work[later].send, att_work[later].send])
            mlp_work[later].launch()
            att_work[later].launch()
            pair[0] = after(pair[0], last_pair[1])
        gmid, picked, dq, dkv, att_small[layer], *away = attend_grad(
            grad, pair, mid, q, kv_parts, segs, att, lse, layer, params, pick
        )
        arrived = [shifted(a, "dp", -(place + 1)) for place, a in enumerate(away)]
        mlp_work[layer].begin([rows_b[layer], rows_1])
        mlp_work[layer].launch()
        due = [mlp_work[layer].send]
        if last:
            other = swapped(after(last_give, gmid), "tensor", 1)
            last_total = last_total + other.astype(f32)
            due.append(last_total)
        else:
            att_work[later].absorb()
            due += [mlp_work[later].arrived, att_work[later].send]
        sent2, qv_small[layer], keep, give = project_grad(
            dq, after(dkv, *due), arrived, picked, layer, params
        )
        rows_2 = None

        def launch_2(gate):
            nonlocal rows_2
            rows_2 = paired(sent2, picked, gate)
            if last:
                nonlocal last_total, last_pair
                for bit in bits_of("tensor")[1:]:
                    rounded = after(last_total.astype(bf16), gate)
                    other = swapped(rounded, "tensor", bit)
                    last_total = rounded.astype(f32) + other.astype(f32)
                rounded = last_total.astype(bf16)
                last_pair = [rounded, swapped(rounded, "tensor", 1)]

        if last:
            pair = exchanged(keep, give, launch_2)
        else:
            small = local_small(
                keep, give, saved[0][0], mlp_small, att_small, qv_small, tensor_count, width
            )
            att_work[later].launch()
            mlp_work[layer].absorb()
            pair = exchanged(keep, give, launch_2)
            mlp_work[layer].launch()
            pair[0] = after(pair[0], rows_2[1], mlp_work[layer].send)
        att_work[layer].begin([rows_a[layer], rows_2])
        att_work[layer].launch()
    input_grad = first_grad(gmid, pair, saved[0][0], params, own_rows)
    result = last_rows(saved[-1][5], last_pair, params, own_rows)
    for bit in bits_of("tensor"):
        small = small + swapped(small, "tensor", bit)
    gates = [mlp_work[0].send, att_work[0].send]
    att_work[0].absorb()
    att_work[0].launch()
    gates.append(att_work[0].send)
    dp_bits = bits_of("dp")
    for place, bit in enumerate(dp_bits):
        if place < len(gates):
            small = after(small, gates[place])
        arriving = swapped(small, "dp", bit)
        if bit != dp_bits[-1]:
            small = small + arriving
    small_grads = small_outs(small, arriving, tensor_count)
    mlp_parts = [work.finish() for work in mlp_work]
    att_parts = [work.finish() for work in att_work]
    g_up, g_down = mlp_outputs(mlp_parts, block, inner)
    g_qkv, g_out = att_outputs(att_parts, block, width)
    return (
        result,
        input_grad,
        g_qkv.transpose(0, 2, 1, 3),
        g_out.transpose(0, 2, 1),
        g_up,
        g_down.transpose(0, 2, 1),
        *small_grads,
    )


def solution(mesh):
    return jax.shard_map(
        shards,
        mesh=mesh,
        in_specs=(
            P(("dp", "tensor"), None),
            P(("dp", "tensor"), None),
            P(),
            P(None, None, None, "tensor"),
            P(None, None, "tensor"),
            P(None, "tensor", None),
            P(None, None, "tensor"),
            P(None, "tensor", None),
            P(None, "tensor"),
            P(),
            P(),
        ),
        out_specs=(
            P(("dp", "tensor"), None),
            P(("dp", "tensor"), None),
            P(None, "dp", None, "tensor"),
            P(None, "tensor", "dp"),
            P(None, "dp", "tensor"),
            P(None, "tensor", "dp"),
            P(),
            P(),
            P(),
            P(),
        ),
        check_vma=False,
    )
```

time: 226 us -> 201 us (0.89)
  waiting for transfers between devices: 126 us -> 87.1 us
  starting transfers between devices: 69.6 us -> 82.3 us
    ppermute x42 -> x51, waiting for transfers between devices: 105 us -> 74 us  [swapped(): return lax.ppermute(array, axis, [(i, i ^ bit) for i in range(length)])]
    ppermute x42 -> x51, starting transfers between devices: 39 us -> 49.7 us  [swapped(): return lax.ppermute(array, axis, [(i, i ^ bit) for i in range(length)])]
    ppermute x12, waiting for transfers between devices: 21 us -> 13 us  [shifted(): return lax.ppermute(array, axis, pairs)]
    pallas_call x26 -> x25, Pallas kernels: 21.5 us -> 21.4 us  [call(): pl.pallas_call(kernel, out_shape=shapes, in_specs=[spec] * len(args), out...]
  transfers between devices with their start and end apart: 54 -> 63, of which waited for: 31 -> 35; matrix products, arithmetic and copies ran while one was open for 1% -> 1% of each run, Pallas kernels for 4% -> 7%
where the time goes in v3:
time: 201 us; the launch traced here: 200 us
  waiting for transfers between devices  87.1 us (43%)
  starting transfers between devices  82.3 us (41%)
  Pallas kernels  22.5 us (11%)
  local copies, waits for them, and re-layouts  6.22 us (3%)
    ppermute x51, waiting for transfers between devices, swapped(): return lax.ppermute(array, axis, [(i, i ^ bit) for i in range(length)])  74 us
    ppermute x51, starting transfers between devices, swapped(): return lax.ppermute(array, axis, [(i, i ^ bit) for i in range(length)])  49.7 us
    ppermute x12, starting transfers between devices, shifted(): return lax.ppermute(array, axis, pairs)  32.6 us
    pallas_call x25, Pallas kernels, call(): pl.pallas_call(kernel, out_shape=shapes, in_specs=[spec] * len(args), out...  21.4 us
    ppermute x12, waiting for transfers between devices, shifted(): return lax.ppermute(array, axis, pairs)  13 us
    unnamed x29, local copies, waits for them, and re-layouts  5.26 us
  transfers between devices with their start and end apart: 63, of which 35 were waited for; matrix products, arithmetic and copies ran while one was open for 1% of the time, Pallas kernels for 7%

profile of v3, /device:TPU:0, one launch (start us, length us, event | category | flops | bytes accessed | tf_op | source)
XLA Modules:
  0.0 200.3 jit_solution(14572091428253497195)
XLA Ops:
  1.2 2.6 %collective-permute-start.1 = (bf16[32,768]{1,0:T(8,128)(2,1)}, bf16[32,768]{1,0:T(8,128)(2,1)S(1)}, u32[]{:S(2)}, u32[]{:S(2)}) collective-permute-start(bf16[32,768]{1,0:T(8,128)(2,1)} %refs_3_.2), channel_id=1, source_target_pairs={{0,2},{1,3},{2,0},{3,1},{4,6},{5,7},{6,4},{7,5},{8,10},{9,11},{10,... | collective-permute-start | bytes 147464 | tf_op jit(solution)/shard_map/ppermute | solution.py:30
  13.1 3.8 %collective-permute-start.5 = (bf16[128,384]{1,0:T(8,128)(2,1)S(1)}, bf16[128,384]{1,0:T(8,128)(2,1)S(1)}, u32[]{:S(2)}, u32[]{:S(2)}) collective-permute-start(bf16[128,384]{1,0:T(8,128)(2,1)S(1)} %get-tuple-element.126.refs_3_), channel_id=1, source_target_pairs={{0,4},{4,8},{8,12},{12,16},{16,20},{20,24},{24,28},{1,5},{5,9},{9,... | collective-permute-start | bytes 294920 | tf_op jit(solution)/shard_map/ppermute | solution.py:25
  16.9 3.5 %collective-permute-start.4 = (bf16[128,384]{1,0:T(8,128)(2,1)S(1)}, bf16[128,384]{1,0:T(8,128)(2,1)S(1)}, u32[]{:S(2)}, u32[]{:S(2)}) collective-permute-start(bf16[128,384]{1,0:T(8,128)(2,1)S(1)} %get-tuple-element.126.refs_3_), channel_id=1, source_target_pairs={{0,8},{4,12},{8,16},{12,20},{16,24},{20,28},{1,9},{5,13},{9,17},{1... | collective-permute-start | bytes 294920 | tf_op jit(solution)/shard_map/ppermute | solution.py:25
  20.4 4.4 %collective-permute-start.3 = (bf16[128,384]{1,0:T(8,128)(2,1)S(1)}, bf16[128,384]{1,0:T(8,128)(2,1)S(1)}, u32[]{:S(2)}, u32[]{:S(2)}) collective-permute-start(bf16[128,384]{1,0:T(8,128)(2,1)S(1)} %get-tuple-element.126.refs_3_), channel_id=1, source_target_pairs={{0,12},{4,16},{8,20},{12,24},{16,28},{1,13},{5,17},{9,21},{13,25},... | collective-permute-start | bytes 294920 | tf_op jit(solution)/shard_map/ppermute | solution.py:25
  31.6 3.4 %collective-permute-done.7 = bf16[64,768]{1,0:T(8,128)(2,1)S(1)} collective-permute-done((bf16[64,768]{1,0:T(8,128)(2,1)S(1)}, bf16[64,768]{1,0:T(8,128)(2,1)S(1)}, u32[]{:S(2)}, u32[]{:S(2)}) %collective-permute-start.7) | collective-permute-done | bytes 98336 | tf_op jit(solution)/shard_map/ppermute | solution.py:30
  41.0 3.3 %collective-permute-done.10 = bf16[64,768]{1,0:T(8,128)(2,1)S(1)} collective-permute-done((bf16[64,768]{1,0:T(8,128)(2,1)S(1)}, bf16[64,768]{1,0:T(8,128)(2,1)S(1)}, u32[]{:S(2)}, u32[]{:S(2)}) %collective-permute-start.10) | collective-permute-done | bytes 98336 | tf_op jit(solution)/shard_map/ppermute | solution.py:30
  46.9 5.4 %collective-permute-start.18 = (bf16[128,384]{1,0:T(8,128)(2,1)S(1)}, bf16[128,384]{1,0:T(8,128)(2,1)S(1)}, u32[]{:S(2)}, u32[]{:S(2)}) collective-permute-start(bf16[128,384]{1,0:T(8,128)(2,1)S(1)} %get-tuple-element.142.refs_3_), channel_id=1, source_target_pairs={{0,4},{4,8},{8,12},{12,16},{16,20},{20,24},{24,28},{1,5},{5,9},{9,... | collective-permute-start | bytes 294920 | tf_op jit(solution)/shard_map/ppermute | solution.py:25
  54.6 5.4 %collective-permute-start.16 = (bf16[128,384]{1,0:T(8,128)(2,1)S(1)}, bf16[128,384]{1,0:T(8,128)(2,1)S(1)}, u32[]{:S(2)}, u32[]{:S(2)}) collective-permute-start(bf16[128,384]{1,0:T(8,128)(2,1)S(1)} %get-tuple-element.142.refs_3_), channel_id=1, source_target_pairs={{0,12},{4,16},{8,20},{12,24},{16,28},{1,13},{5,17},{9,21},{13,25},... | collective-permute-start | bytes 294920 | tf_op jit(solution)/shard_map/ppermute | solution.py:25
  66.8 3.3 %collective-permute-done.20 = bf16[64,768]{1,0:T(8,128)(2,1)S(1)} collective-permute-done((bf16[64,768]{1,0:T(8,128)(2,1)S(1)}, bf16[64,768]{1,0:T(8,128)(2,1)S(1)}, u32[]{:S(2)}, u32[]{:S(2)}) %collective-permute-start.20) | collective-permute-done | bytes 98336 | tf_op jit(solution)/shard_map/ppermute | solution.py:30
  80.1 3.6 %collective-permute-done.25.refs_1_ = bf16[128,640]{1,0:T(8,128)(2,1)S(1)} collective-permute-done((bf16[128,640]{1,0:T(8,128)(2,1)S(1)}, bf16[128,640]{1,0:T(8,128)(2,1)S(1)}, u32[]{:S(2)}, u32[]{:S(2)}) %collective-permute-start.25) | collective-permute-done | bytes 163872 | tf_op jit(solution)/shard_map/ppermute | solution.py:30
  91.3 5.0 %collective-permute-done.29.refs_4_ = bf16[128,1152]{1,0:T(8,128)(2,1)S(1)} collective-permute-done((bf16[128,1152]{1,0:T(8,128)(2,1)S(1)}, bf16[128,1152]{1,0:T(8,128)(2,1)S(1)}, u32[]{:S(2)}, u32[]{:S(2)}) %collective-permute-start.29) | collective-permute-done | bytes 294944 | tf_op jit(solution)/shard_map/ppermute | solution.py:30
  97.2 4.3 %collective-permute-done.31.refs_1_ = bf16[128,384]{1,0:T(8,128)(2,1)S(1)} collective-permute-done((bf16[128,384]{1,0:T(8,128)(2,1)S(1)}, bf16[128,384]{1,0:T(8,128)(2,1)S(1)}, u32[]{:S(2)}, u32[]{:S(2)}) %collective-permute-start.31) | collective-permute-done | bytes 98336 | tf_op jit(solution)/shard_map/ppermute | solution.py:25
  104.3 4.9 %collective-permute-start.40 = (bf16[128,1024]{1,0:T(8,128)(2,1)S(1)}, bf16[128,1024]{1,0:T(8,128)(2,1)S(1)}, u32[]{:S(2)}, u32[]{:S(2)}) collective-permute-start(bf16[128,1024]{1,0:T(8,128)(2,1)S(1)} %get-tuple-element.185.refs_3_), channel_id=1, source_target_pairs={{0,8},{4,12},{8,0},{12,4},{16,24},{20,28},{24,16},{28,20},{1,9},{5... | collective-permute-start | bytes 786440 | tf_op jit(solution)/shard_map/ppermute | solution.py:30
  115.9 3.1 %collective-permute-done.39.arrived_ref = bf16[192,1536]{1,0:T(8,128)(2,1)S(1)} collective-permute-done((bf16[192,1536]{1,0:T(8,128)(2,1)S(1)}, bf16[192,1536]{1,0:T(8,128)(2,1)S(1)}, u32[]{:S(2)}, u32[]{:S(2)}) %collective-permute-start.39) | collective-permute-done | bytes 589856 | tf_op jit(solution)/shard_map/ppermute | solution.py:30
  133.7 3.0 %collective-permute-done.43.refs_4_ = bf16[128,1152]{1,0:T(8,128)(2,1)S(1)} collective-permute-done((bf16[128,1152]{1,0:T(8,128)(2,1)S(1)}, bf16[128,1152]{1,0:T(8,128)(2,1)S(1)}, u32[]{:S(2)}, u32[]{:S(2)}) %collective-permute-start.43) | collective-permute-done | bytes 294944 | tf_op jit(solution)/shard_map/ppermute | solution.py:30
  138.5 4.1 %collective-permute-done.47.refs_1_ = bf16[128,384]{1,0:T(8,128)(2,1)S(1)} collective-permute-done((bf16[128,384]{1,0:T(8,128)(2,1)S(1)}, bf16[128,384]{1,0:T(8,128)(2,1)S(1)}, u32[]{:S(2)}, u32[]{:S(2)}) %collective-permute-start.47) | collective-permute-done | bytes 98336 | tf_op jit(solution)/shard_map/ppermute | solution.py:25
  143.4 2.6 %collective-permute-start.52 = (bf16[192,1536]{1,0:T(8,128)(2,1)S(1)}, bf16[192,1536]{1,0:T(8,128)(2,1)S(1)}, u32[]{:S(2)}, u32[]{:S(2)}) collective-permute-start(bf16[192,1536]{1,0:T(8,128)(2,1)S(1)} %get-tuple-element.198), channel_id=1, source_target_pairs={{0,4},{4,0},{8,12},{12,8},{16,20},{20,16},{24,28},{28,24},{1,5},{5... | collective-permute-start | bytes 1769480 | tf_op jit(solution)/shard_map/ppermute | solution.py:30
  146.0 5.0 %collective-permute-start.51 = (bf16[128,1024]{1,0:T(8,128)(2,1)S(1)}, bf16[128,1024]{1,0:T(8,128)(2,1)S(1)}, u32[]{:S(2)}, u32[]{:S(2)}) collective-permute-start(bf16[128,1024]{1,0:T(8,128)(2,1)S(1)} %get-tuple-element.209.refs_3_), channel_id=1, source_target_pairs={{0,8},{4,12},{8,0},{12,4},{16,24},{20,28},{24,16},{28,20},{1,9},{5... | collective-permute-start | bytes 786440 | tf_op jit(solution)/shard_map/ppermute | solution.py:30
  151.0 6.6 %collective-permute-done.51.refs_4_ = bf16[128,1024]{1,0:T(8,128)(2,1)S(1)} collective-permute-done((bf16[128,1024]{1,0:T(8,128)(2,1)S(1)}, bf16[128,1024]{1,0:T(8,128)(2,1)S(1)}, u32[]{:S(2)}, u32[]{:S(2)}) %collective-permute-start.51) | collective-permute-done | bytes 262176 | tf_op jit(solution)/shard_map/ppermute | solution.py:30
  163.2 3.1 %collective-permute-done.59 = f32[24,768]{1,0:T(8,128)S(1)} collective-permute-done((f32[24,768]{1,0:T(8,128)S(1)}, f32[24,768]{1,0:T(8,128)S(1)}, u32[]{:S(2)}, u32[]{:S(2)}) %collective-permute-start.59) | collective-permute-done | bytes 73760 | tf_op jit(solution)/shard_map/ppermute | solution.py:30
  167.5 2.8 %collective-permute-start.57 = (bf16[96,1536]{1,0:T(8,128)(2,1)S(1)}, bf16[96,1536]{1,0:T(8,128)(2,1)S(1)}, u32[]{:S(2)}, u32[]{:S(2)}) collective-permute-start(bf16[96,1536]{1,0:T(8,128)(2,1)S(1)} %get-tuple-element.211), channel_id=1, source_target_pairs={{0,16},{4,20},{8,24},{12,28},{16,0},{20,4},{24,8},{28,12},{1,17},{... | collective-permute-start | bytes 884744 | tf_op jit(solution)/shard_map/ppermute | solution.py:30
  172.9 8.2 %collective-permute-done.61 = f32[24,768]{1,0:T(8,128)S(1)} collective-permute-done((f32[24,768]{1,0:T(8,128)S(1)}, f32[24,768]{1,0:T(8,128)S(1)}, u32[]{:S(2)}, u32[]{:S(2)}) %collective-permute-start.61) | collective-permute-done | bytes 73760 | tf_op jit(solution)/shard_map/ppermute | solution.py:30
  181.1 4.1 %collective-permute-start.62 = (f32[24,768]{1,0:T(8,128)S(1)}, f32[24,768]{1,0:T(8,128)S(1)}, u32[]{:S(2)}, u32[]{:S(2)}) collective-permute-start(f32[24,768]{1,0:T(8,128)S(1)} %add.127.total_ref), channel_id=1, source_target_pairs={{0,16},{4,20},{8,24},{12,28},{16,0},{20,4},{24,8},{28,12},{1,17},{... | collective-permute-start | bytes 221192 | tf_op jit(solution)/shard_map/ppermute | solution.py:30
  187.2 9.6 %collective-permute-done.55.refs_1_ = bf16[96,768]{1,0:T(8,128)(2,1)S(1)} collective-permute-done((bf16[96,768]{1,0:T(8,128)(2,1)S(1)}, bf16[96,768]{1,0:T(8,128)(2,1)S(1)}, u32[]{:S(2)}, u32[]{:S(2)}) %collective-permute-start.55) | collective-permute-done | bytes 147488 | tf_op jit(solution)/shard_map/ppermute | solution.py:30
  (184 shorter events, 93.7 us)
Async XLA Ops:
  13.1 11.9 %collective-permute-start.5 = (bf16[128,384]{1,0:T(8,128)(2,1)S(1)}, bf16[128,384]{1,0:T(8,128)(2,1)S(1)}, u32[]{:S(2)}, u32[]{:S(2)}) collective-permute-start(bf16[128,384]{1,0:T(8,128)(2,1)S(1)} %get-tuple-element.126.refs_3_), channel_id=1, source_target_pairs={{0,4},{4,8},{8,12},{12,16},{16,20},{20,24},{24,28},{1,5},{5,9},{9,... | collective-permute-start | bytes 294920 | tf_op jit(solution)/shard_map/ppermute | solution.py:25
  41.0 19.0 %collective-permute-start.15 = (bf16[128,1152]{1,0:T(8,128)(2,1)S(1)}, bf16[128,1152]{1,0:T(8,128)(2,1)S(1)}, u32[]{:S(2)}, u32[]{:S(2)}) collective-permute-start(bf16[128,1152]{1,0:T(8,128)(2,1)S(1)} %get-tuple-element.140.refs_0_), channel_id=1, source_target_pairs={{0,8},{4,12},{8,0},{12,4},{16,24},{20,28},{24,16},{28,20},{1,9},{5... | collective-permute-start | bytes 884744 | tf_op jit(solution)/shard_map/ppermute | solution.py:30
  44.4 15.6 %collective-permute-start.14 = (bf16[128,640]{1,0:T(8,128)(2,1)S(1)}, bf16[128,640]{1,0:T(8,128)(2,1)S(1)}, u32[]{:S(2)}, u32[]{:S(2)}) collective-permute-start(bf16[128,640]{1,0:T(8,128)(2,1)S(1)} %get-tuple-element.138.refs_0_), channel_id=1, source_target_pairs={{0,8},{4,12},{8,0},{12,4},{16,24},{20,28},{24,16},{28,20},{1,9},{5... | collective-permute-start | bytes 491528 | tf_op jit(solution)/shard_map/ppermute | solution.py:30
  46.9 13.2 %collective-permute-start.18 = (bf16[128,384]{1,0:T(8,128)(2,1)S(1)}, bf16[128,384]{1,0:T(8,128)(2,1)S(1)}, u32[]{:S(2)}, u32[]{:S(2)}) collective-permute-start(bf16[128,384]{1,0:T(8,128)(2,1)S(1)} %get-tuple-element.142.refs_3_), channel_id=1, source_target_pairs={{0,4},{4,8},{8,12},{12,16},{16,20},{20,24},{24,28},{1,5},{5,9},{9,... | collective-permute-start | bytes 294920 | tf_op jit(solution)/shard_map/ppermute | solution.py:25
  76.7 13.4 %collective-permute-start.28 = (bf16[128,1152]{1,0:T(8,128)(2,1)S(1)}, bf16[128,1152]{1,0:T(8,128)(2,1)S(1)}, u32[]{:S(2)}, u32[]{:S(2)}) collective-permute-start(bf16[128,1152]{1,0:T(8,128)(2,1)S(1)} %get-tuple-element.163.refs_0_), channel_id=1, source_target_pairs={{0,8},{4,12},{8,0},{12,4},{16,24},{20,28},{24,16},{28,20},{1,9},{5... | collective-permute-start | bytes 884744 | tf_op jit(solution)/shard_map/ppermute | solution.py:30
  78.7 17.7 %collective-permute-start.29 = (bf16[128,1152]{1,0:T(8,128)(2,1)S(1)}, bf16[128,1152]{1,0:T(8,128)(2,1)S(1)}, u32[]{:S(2)}, u32[]{:S(2)}) collective-permute-start(bf16[128,1152]{1,0:T(8,128)(2,1)S(1)} %get-tuple-element.166.refs_3_), channel_id=1, source_target_pairs={{0,8},{4,12},{8,0},{12,4},{16,24},{20,28},{24,16},{28,20},{1,9},{5... | collective-permute-start | bytes 884744 | tf_op jit(solution)/shard_map/ppermute | solution.py:30
  85.7 11.5 %collective-permute-start.27 = (bf16[64,768]{1,0:T(8,128)(2,1)S(1)}, bf16[64,768]{1,0:T(8,128)(2,1)S(1)}, u32[]{:S(2)}, u32[]{:S(2)}) collective-permute-start(bf16[64,768]{1,0:T(8,128)(2,1)S(1)} %get-tuple-element.159), channel_id=1, source_target_pairs={{0,1},{1,0},{2,3},{3,2},{4,5},{5,4},{6,7},{7,6},{8,9},{9,8},{10,11... | collective-permute-start | bytes 294920 | tf_op jit(solution)/shard_map/ppermute | solution.py:30
  85.8 11.5 %collective-permute-start.30 = (bf16[128,384]{1,0:T(8,128)(2,1)S(1)}, bf16[128,384]{1,0:T(8,128)(2,1)S(1)}, u32[]{:S(2)}, u32[]{:S(2)}) collective-permute-start(bf16[128,384]{1,0:T(8,128)(2,1)S(1)} %get-tuple-element.170), channel_id=1, source_target_pairs={{4,0},{8,4},{12,8},{16,12},{20,16},{24,20},{28,24},{5,1},{9,5},{13... | collective-permute-start | bytes 294920 | tf_op jit(solution)/shard_map/ppermute | solution.py:25
  87.1 14.5 %collective-permute-start.31 = (bf16[128,384]{1,0:T(8,128)(2,1)S(1)}, bf16[128,384]{1,0:T(8,128)(2,1)S(1)}, u32[]{:S(2)}, u32[]{:S(2)}) collective-permute-start(bf16[128,384]{1,0:T(8,128)(2,1)S(1)} %get-tuple-element.171), channel_id=1, source_target_pairs={{8,0},{12,4},{16,8},{20,12},{24,16},{28,20},{9,1},{13,5},{17,9},{2... | collective-permute-start | bytes 294920 | tf_op jit(solution)/shard_map/ppermute | solution.py:25
  90.0 11.5 %collective-permute-start.32 = (bf16[128,384]{1,0:T(8,128)(2,1)S(1)}, bf16[128,384]{1,0:T(8,128)(2,1)S(1)}, u32[]{:S(2)}, u32[]{:S(2)}) collective-permute-start(bf16[128,384]{1,0:T(8,128)(2,1)S(1)} %get-tuple-element.172), channel_id=1, source_target_pairs={{12,0},{16,4},{20,8},{24,12},{28,16},{13,1},{17,5},{21,9},{25,13},... | collective-permute-start | bytes 294920 | tf_op jit(solution)/shard_map/ppermute | solution.py:25
  103.9 15.1 %collective-permute-start.39 = (bf16[192,1536]{1,0:T(8,128)(2,1)S(1)}, bf16[192,1536]{1,0:T(8,128)(2,1)S(1)}, u32[]{:S(2)}, u32[]{:S(2)}) collective-permute-start(bf16[192,1536]{1,0:T(8,128)(2,1)S(1)} %get-tuple-element.168), channel_id=1, source_target_pairs={{0,4},{4,0},{8,12},{12,8},{16,20},{20,16},{24,28},{28,24},{1,5},{5... | collective-permute-start | bytes 1769480 | tf_op jit(solution)/shard_map/ppermute | solution.py:30
  120.9 11.4 %collective-permute-start.45 = (bf16[192,768]{1,0:T(8,128)(2,1)S(1)}, bf16[192,768]{1,0:T(8,128)(2,1)S(1)}, u32[]{:S(2)}, u32[]{:S(2)}) collective-permute-start(bf16[192,768]{1,0:T(8,128)(2,1)S(1)} %get-tuple-element.186), channel_id=1, source_target_pairs={{0,4},{4,0},{8,12},{12,8},{16,20},{20,16},{24,28},{28,24},{1,5},{5... | collective-permute-start | bytes 884744 | tf_op jit(solution)/shard_map/ppermute | solution.py:30
  121.4 17.1 %collective-permute-start.44 = (bf16[96,1536]{1,0:T(8,128)(2,1)S(1)}, bf16[96,1536]{1,0:T(8,128)(2,1)S(1)}, u32[]{:S(2)}, u32[]{:S(2)}) collective-permute-start(bf16[96,1536]{1,0:T(8,128)(2,1)S(1)} %get-tuple-element.183), channel_id=1, source_target_pairs={{0,16},{4,20},{8,24},{12,28},{16,0},{20,4},{24,8},{28,12},{1,17},{... | collective-permute-start | bytes 884744 | tf_op jit(solution)/shard_map/ppermute | solution.py:30
  123.8 13.0 %collective-permute-start.43 = (bf16[128,1152]{1,0:T(8,128)(2,1)S(1)}, bf16[128,1152]{1,0:T(8,128)(2,1)S(1)}, u32[]{:S(2)}, u32[]{:S(2)}) collective-permute-start(bf16[128,1152]{1,0:T(8,128)(2,1)S(1)} %get-tuple-element.196.refs_3_), channel_id=1, source_target_pairs={{0,8},{4,12},{8,0},{12,4},{16,24},{20,28},{24,16},{28,20},{1,9},{5... | collective-permute-start | bytes 884744 | tf_op jit(solution)/shard_map/ppermute | solution.py:30
  131.0 11.6 %collective-permute-start.47 = (bf16[128,384]{1,0:T(8,128)(2,1)S(1)}, bf16[128,384]{1,0:T(8,128)(2,1)S(1)}, u32[]{:S(2)}, u32[]{:S(2)}) collective-permute-start(bf16[128,384]{1,0:T(8,128)(2,1)S(1)} %get-tuple-element.203), channel_id=1, source_target_pairs={{8,0},{12,4},{16,8},{20,12},{24,16},{28,20},{9,1},{13,5},{17,9},{2... | collective-permute-start | bytes 294920 | tf_op jit(solution)/shard_map/ppermute | solution.py:25
  143.4 22.9 %collective-permute-start.52 = (bf16[192,1536]{1,0:T(8,128)(2,1)S(1)}, bf16[192,1536]{1,0:T(8,128)(2,1)S(1)}, u32[]{:S(2)}, u32[]{:S(2)}) collective-permute-start(bf16[192,1536]{1,0:T(8,128)(2,1)S(1)} %get-tuple-element.198), channel_id=1, source_target_pairs={{0,4},{4,0},{8,12},{12,8},{16,20},{20,16},{24,28},{28,24},{1,5},{5... | collective-permute-start | bytes 1769480 | tf_op jit(solution)/shard_map/ppermute | solution.py:30
  146.0 11.6 %collective-permute-start.51 = (bf16[128,1024]{1,0:T(8,128)(2,1)S(1)}, bf16[128,1024]{1,0:T(8,128)(2,1)S(1)}, u32[]{:S(2)}, u32[]{:S(2)}) collective-permute-start(bf16[128,1024]{1,0:T(8,128)(2,1)S(1)} %get-tuple-element.209.refs_3_), channel_id=1, source_target_pairs={{0,8},{4,12},{8,0},{12,4},{16,24},{20,28},{24,16},{28,20},{1,9},{5... | collective-permute-start | bytes 786440 | tf_op jit(solution)/shard_map/ppermute | solution.py:30
  158.2 12.1 %collective-permute-start.54 = (bf16[192,768]{1,0:T(8,128)(2,1)S(1)}, bf16[192,768]{1,0:T(8,128)(2,1)S(1)}, u32[]{:S(2)}, u32[]{:S(2)}) collective-permute-start(bf16[192,768]{1,0:T(8,128)(2,1)S(1)} %get-tuple-element.215), channel_id=1, source_target_pairs={{0,4},{4,0},{8,12},{12,8},{16,20},{20,16},{24,28},{28,24},{1,5},{5... | collective-permute-start | bytes 884744 | tf_op jit(solution)/shard_map/ppermute | solution.py:30
  161.7 11.1 %collective-permute-start.50 = (bf16[64,768]{1,0:T(8,128)(2,1)S(1)}, bf16[64,768]{1,0:T(8,128)(2,1)S(1)}, u32[]{:S(2)}, u32[]{:S(2)}) collective-permute-start(bf16[64,768]{1,0:T(8,128)(2,1)S(1)} %add_convert_fusion.1), channel_id=1, source_target_pairs={{0,2},{1,3},{2,0},{3,1},{4,6},{5,7},{6,4},{7,5},{8,10},{9,11},{10,... | collective-permute-start | bytes 294920 | tf_op jit(solution)/shard_map/ppermute | solution.py:30
  167.4 19.8 %collective-permute-start.56 = (bf16[96,768]{1,0:T(8,128)(2,1)S(1)}, bf16[96,768]{1,0:T(8,128)(2,1)S(1)}, u32[]{:S(2)}, u32[]{:S(2)}) collective-permute-start(bf16[96,768]{1,0:T(8,128)(2,1)S(1)} %get-tuple-element.200), channel_id=1, source_target_pairs={{0,16},{4,20},{8,24},{12,28},{16,0},{20,4},{24,8},{28,12},{1,17},{... | collective-permute-start | bytes 442376 | tf_op jit(solution)/shard_map/ppermute | solution.py:30
  167.5 31.7 %collective-permute-start.57 = (bf16[96,1536]{1,0:T(8,128)(2,1)S(1)}, bf16[96,1536]{1,0:T(8,128)(2,1)S(1)}, u32[]{:S(2)}, u32[]{:S(2)}) collective-permute-start(bf16[96,1536]{1,0:T(8,128)(2,1)S(1)} %get-tuple-element.211), channel_id=1, source_target_pairs={{0,16},{4,20},{8,24},{12,28},{16,0},{20,4},{24,8},{28,12},{1,17},{... | collective-permute-start | bytes 884744 | tf_op jit(solution)/shard_map/ppermute | solution.py:30
  170.4 26.4 %collective-permute-start.55 = (bf16[96,768]{1,0:T(8,128)(2,1)S(1)}, bf16[96,768]{1,0:T(8,128)(2,1)S(1)}, u32[]{:S(2)}, u32[]{:S(2)}) collective-permute-start(bf16[96,768]{1,0:T(8,128)(2,1)S(1)} %get-tuple-element.217), channel_id=1, source_target_pairs={{0,16},{4,20},{8,24},{12,28},{16,0},{20,4},{24,8},{28,12},{1,17},{... | collective-permute-start | bytes 442376 | tf_op jit(solution)/shard_map/ppermute | solution.py:30
  172.8 13.2 %collective-permute-start.53 = (bf16[64,768]{1,0:T(8,128)(2,1)S(1)}, bf16[64,768]{1,0:T(8,128)(2,1)S(1)}, u32[]{:S(2)}, u32[]{:S(2)}) collective-permute-start(bf16[64,768]{1,0:T(8,128)(2,1)S(1)} %add_convert_fusion.own_ref), channel_id=1, source_target_pairs={{0,1},{1,0},{2,3},{3,2},{4,5},{5,4},{6,7},{7,6},{8,9},{9,8},{10,11... | collective-permute-start | bytes 294920 | tf_op jit(solution)/shard_map/ppermute | solution.py:30
  181.1 17.5 %collective-permute-start.62 = (f32[24,768]{1,0:T(8,128)S(1)}, f32[24,768]{1,0:T(8,128)S(1)}, u32[]{:S(2)}, u32[]{:S(2)}) collective-permute-start(f32[24,768]{1,0:T(8,128)S(1)} %add.127.total_ref), channel_id=1, source_target_pairs={{0,16},{4,20},{8,24},{12,28},{16,0},{20,4},{24,8},{28,12},{1,17},{... | collective-permute-start | bytes 221192 | tf_op jit(solution)/shard_map/ppermute | solution.py:30
  (53 other events, 372.0 us)

commit v4 on v3

--- a/solution.py
+++ b/solution.py
@@ -10,7 +10,6 @@
 FF = 3072
 LAYERS = 2
 SPAN = 4
-PAIR = 2
 
 epsilon = 1e-05
 gelu_c = 0.7978845608028654
@@ -40,7 +39,7 @@
     return found
 
 
-def call(kernel, outs, args, flops=1e8):
+def call(kernel, outs, args, flops=1, moved=1):
     spec = pl.BlockSpec(memory_space=pltpu.VMEM)
     shapes = [jax.ShapeDtypeStruct(shape, dtype) for shape, dtype in outs]
     return pl.pallas_call(
@@ -49,8 +48,22 @@
         in_specs=[spec] * len(args),
         out_specs=[spec] * len(outs),
         compiler_params=pltpu.CompilerParams(vmem_limit_bytes=VMEM_LIMIT),
-        cost_estimate=pl.CostEstimate(flops=1, bytes_accessed=1, transcendentals=0),
+        cost_estimate=pl.CostEstimate(
+            flops=int(flops), bytes_accessed=int(moved), transcendentals=0
+        ),
     )(*args)
+
+
+def picked_halves(rows):
+    wide = rows.shape[1] // 4
+    high = (lax.axis_index("dp") // (lax.axis_size("dp") // 4)) % 2 == 1
+    quarters = [rows[:, k * wide : (k + 1) * wide] for k in range(4)]
+    return tuple(
+        jnp.concatenate(
+            [jnp.where(high, quarters[k + one], quarters[k + zero]) for k in (0, 2)], axis=1
+        )
+        for zero, one in ((0, 1), (1, 0))
+    )
 
 
 def mm(left, right, contract=((1,), (0,))):
@@ -156,7 +169,7 @@
 
 
 def project_rows(hidden, layer, refs, outs):
-    small, (w_qkv, pick) = refs[:4], refs[4:]
+    small, w_qkv = refs[:4], refs[4]
     h_ref, picked_ref, q_ref, kv_ref = outs
     width = q_ref.shape[1]
     hat, _ = normalize(hidden)
@@ -166,58 +179,55 @@
     kv_ref[...] = jnp.concatenate([kv[:, :width], values], axis=1).astype(bf16)
     query = mm(act, w_qkv[layer, :width], NT)
     q_ref[...] = (query + qv_bias(small, layer, 0)).astype(bf16)
-    picked_ref[...] = mm(act, pick[...]).astype(bf16)
-
-
-def project_first(tokens, pieces, params, pick):
+    half = act.shape[1] // 2
+    picked_ref[:, :half], picked_ref[:, half:] = picked_halves(act)
+
+
+def project_first(tokens, pieces, params):
     count = len(pieces)
     own_rows = tokens.shape[0]
     rows = (count + 1) * own_rows
     width = params["w_out"].shape[1]
     gains, biases, _, qv = params["small"]
     far = [tokens, gains, biases, qv, params["w_qkv"]]
-    near_shapes = [a.shape for a in far[:4]] + [(1,) + far[4].shape[1:]]
     many = len(far)
 
     def kernel(*refs):
-        ins, far_refs, pick_ref = refs[:count], refs[count : count + many], refs[count + many]
-        outs, near, sems = refs[-many - 5 : -many - 1], refs[-many - 1 : -1], refs[-1]
-        sources = [*far_refs[:-1], far_refs[-1].at[pl.ds(0, 1)]]
-        copies = [pltpu.make_async_copy(sources[k], near[k], sems.at[k]) for k in range(many)]
-        for copy in copies:
-            copy.start()
-        for copy in copies:
-            copy.wait()
+        ins, near = refs[:count], refs[count : count + many]
+        outs = refs[-4:]
         place_pieces([near[0], *ins], outs[0])
         small = (near[1], near[2], None, near[3])
-        project_rows(outs[0][...], 0, [*small, near[4], pick_ref], outs)
+        project_rows(outs[0][...], 0, [*small, near[4]], outs)
+
+    def whole(array):
+        zeros = (0,) * array.ndim
+        return pl.BlockSpec(array.shape, lambda step: zeros)
 
     spec = pl.BlockSpec(memory_space=pltpu.VMEM)
     return pl.pallas_call(
         kernel,
+        grid=(1,),
         out_shape=[
             jax.ShapeDtypeStruct((rows, D), f32),
             jax.ShapeDtypeStruct((rows, D), bf16),
             jax.ShapeDtypeStruct((rows, width), bf16),
             jax.ShapeDtypeStruct((rows, 2 * width), bf16),
         ],
-        in_specs=[spec] * count + [pl.BlockSpec(memory_space=pltpu.HBM)] * many + [spec],
+        in_specs=[spec] * count
+        + [whole(a) for a in far[:-1]]
+        + [pl.BlockSpec((1,) + far[-1].shape[1:], lambda step: (0, 0, 0))],
         out_specs=[spec] * 4,
-        scratch_shapes=[
-            pltpu.VMEM(shape, a.dtype) for shape, a in zip(near_shapes, far, strict=True)
-        ]
-        + [pltpu.SemaphoreType.DMA((many,))],
         compiler_params=pltpu.CompilerParams(vmem_limit_bytes=VMEM_LIMIT),
         cost_estimate=pl.CostEstimate(flops=1, bytes_accessed=1, transcendentals=0),
-    )(*pieces, *far, pick)
-
-
-def project_next(mid, pair, layer, params, pick):
+    )(*pieces, *far)
+
+
+def project_next(mid, pair, layer, params):
     rows = mid.shape[0]
     width = params["w_out"].shape[1]
 
     def kernel(mid_ref, own_ref, other_ref, *refs):
-        ins, outs = refs[:6], refs[6:]
+        ins, outs = refs[:5], refs[5:]
         hidden = mid_ref[...] + joined(own_ref, other_ref) + bias(ins, layer - 1, 3)
         outs[0][...] = hidden
         project_rows(hidden, layer, ins, outs)
@@ -225,7 +235,7 @@
     return call(
         kernel,
         [((rows, D), f32), ((rows, D), bf16), ((rows, width), bf16), ((rows, 2 * width), bf16)],
-        [mid, *pair, *params["small"], params["w_qkv"], pick],
+        [mid, *pair, *params["small"], params["w_qkv"]],
     )
 
 
@@ -234,18 +244,30 @@
     return (lane >= head * HD) & (lane < (head + 1) * HD)
 
 
-def allowed_of(seg_q, seg_k, rows):
-    shape = (rows, SPAN * rows)
-    query = lax.broadcasted_iota(jnp.int32, shape, 0)
-    key = lax.broadcasted_iota(jnp.int32, shape, 1)
-    return (key <= query + (SPAN - 1) * rows) & (seg_q[...] == seg_k[...])
+def allowed_rows(segments, rows):
+    def kernel(seg_ref, out_ref):
+        mine = lax.axis_index("dp")
+        here = seg_ref[:, pl.ds(pl.multiple_of(mine * rows, rows), rows)].astype(f32)
+        query_seg = jnp.broadcast_to(here, (rows, rows)).T
+        query = lax.broadcasted_iota(jnp.int32, (rows, rows), 0)
+        key = lax.broadcasted_iota(jnp.int32, (rows, rows), 1)
+        for place in range(SPAN):
+            behind = SPAN - 1 - place
+            start = jnp.maximum(mine - behind, 0) * rows
+            key_seg = seg_ref[:, pl.ds(pl.multiple_of(start, rows), rows)].astype(f32)
+            same = (query_seg == key_seg) & (key <= query + behind * rows)
+            seen = jnp.where(same, 1.0, 0.0) * jnp.where(mine >= behind, 1.0, 0.0)
+            out_ref[:, place * rows : (place + 1) * rows] = seen
+
+    row = segments[None, :]
+    return call(kernel, [((rows, SPAN * rows), f32)], [row], 1e10, 1e8)[0]
 
 
 def split_shapes(rows):
     return [((rows // 2, D), f32), ((rows // 2, D), bf16)]
 
 
-def attend(q, kv_parts, segs, picked1, layer, params):
+def attend(q, kv_parts, mask, picked1, layer, params):
     rows, width = q.shape
     half = D // 2
     pad = -(half + width) % 128
@@ -253,8 +275,8 @@
 
     def kernel(q_ref, *refs):
         kv_refs, refs = refs[:SPAN], refs[SPAN:]
-        seg_q, seg_k, w_out, p1_ref, att_ref, lse_ref, sent_ref, keep_ref, give_ref = refs
-        allowed = allowed_of(seg_q, seg_k, rows)
+        mask_ref, w_out, p1_ref, att_ref, lse_ref, sent_ref, keep_ref, give_ref = refs
+        allowed = mask_ref[...] > 0.0
         kv_all = jnp.concatenate([r[...] for r in kv_refs], axis=0)
         keys, values = kv_all[:, :width], kv_all[:, width:]
         query = q_ref[...]
@@ -283,16 +305,16 @@
         kernel,
         [((rows, width), bf16), ((rows, 128), f32), ((rows, half + width + pad), bf16)]
         + split_shapes(rows),
-        [q, *kv_parts, *segs, params["w_out"], picked1],
-    )
-
-
-def feed_forward(hidden, pair, layer, params, pick):
+        [q, *kv_parts, mask, params["w_out"], picked1],
+    )
+
+
+def feed_forward(hidden, pair, layer, params):
     rows = hidden.shape[0]
     half = D // 2
     inner = params["w_up"].shape[2]
 
-    def kernel(h_ref, own_ref, other_ref, g_ref, b_ref, f_ref, q_ref, up, down, pick_ref,
+    def kernel(h_ref, own_ref, other_ref, g_ref, b_ref, f_ref, q_ref, up, down,
                mid_ref, slope_ref, sent_ref, kept_ref, keep_ref, give_ref):
         small = (g_ref, b_ref, f_ref, q_ref)
         mid = h_ref[...] + joined(own_ref, other_ref) + bias(small, layer, 1)
@@ -304,9 +326,7 @@
         act3 = value.astype(bf16)
         split_halves(mm(act3, down[layer]), keep_ref, give_ref)
         slope_ref[...] = slope
-        picked2 = mm(act2, pick_ref[...]).astype(bf16)
-        kept_ref[...] = picked2[:, :half]
-        sent_ref[:, :half] = picked2[:, half:]
+        kept_ref[...], sent_ref[:, :half] = picked_halves(act2)
         sent_ref[:, half:] = act3
 
     return call(
@@ -319,14 +339,14 @@
         ]
         + split_shapes(rows),
         [hidden, *pair]
-        + [*params["small"], params["w_up"], params["w_down"]]
-        + [pick],
+        + [*params["small"], params["w_up"], params["w_down"]],
     )
 
 
 def last_rows(mid, pair, params, own_rows):
     def kernel(mid_ref, own_ref, other_ref, biases, out_ref, all_ref):
-        total = mid_ref[...] + joined(own_ref, other_ref)
+        own = mid_ref.shape[0] // 2
+        total = mid_ref[...] + joined(own_ref.at[own:], other_ref.at[own:])
         all_ref[...] = total + biases[LAYERS - 1, 3:4]
         start = pl.multiple_of(lax.axis_index("tensor") * own_rows, own_rows)
         out_ref[...] = all_ref[pl.ds(start, own_rows), :].astype(bf16)
@@ -343,16 +363,14 @@
 
 
 def mlp_grad(grad, layer, refs, outs):
-    slope_ref, up, down, pick_ref = refs
+    slope_ref, up, down = refs
     sent_ref, small_ref, kept_ref, keep_ref, give_ref = outs
     half = D // 2
     grad_b = grad.astype(bf16)
     d_pre = mm(grad_b, down[layer], NT) * slope_ref[...]
     pre_b = d_pre.astype(bf16)
     split_halves(mm(pre_b, up[layer], NT), keep_ref, give_ref)
-    picked = mm(grad_b, pick_ref[...]).astype(bf16)
-    kept_ref[...] = picked[:, :half]
-    sent_ref[:, :half] = picked[:, half:]
+    kept_ref[...], sent_ref[:, :half] = picked_halves(grad_b)
     sent_ref[:, half:] = pre_b
     small_ref[0:1, :] = column_sum(d_pre)
     small_ref[1:2, :] = column_sum(grad)
@@ -368,12 +386,12 @@
     ] + split_shapes(rows)
 
 
-def mlp_grad_last(pieces, slope, params, pick):
+def mlp_grad_last(pieces, slope, params):
     count = len(pieces)
     rows, inner = slope.shape
 
     def kernel(*refs):
-        ins, outs = refs[: count + 4], refs[count + 4 :]
+        ins, outs = refs[: count + 3], refs[count + 3 :]
         place_pieces(ins[:count], outs[0])
         outs[2][...] = jnp.zeros((8, D), f32)
         mlp_grad(outs[0][...], LAYERS - 1, ins[count:], outs[1:])
@@ -381,15 +399,15 @@
     return call(
         kernel,
         mlp_outs(rows, inner),
-        [*pieces, slope, params["w_up"], params["w_down"], pick],
-    )
-
-
-def mlp_grad_next(gmid, pair, hidden, slope, layer, params, pick):
+        [*pieces, slope, params["w_up"], params["w_down"]],
+    )
+
+
+def mlp_grad_next(gmid, pair, hidden, slope, layer, params):
     rows, inner = slope.shape
 
     def kernel(gmid_ref, own_ref, other_ref, h_ref, gains, *refs):
-        ins, outs = refs[:4], refs[4:]
+        ins, outs = refs[:3], refs[3:]
         grad, g_gain, g_bias = norm1_grad(gmid_ref, own_ref, other_ref, h_ref, gains, layer + 1)
         outs[0][...] = grad
         outs[2][...] = jnp.zeros((8, D), f32)
@@ -400,27 +418,27 @@
     return call(
         kernel,
         mlp_outs(rows, inner),
-        [gmid, *pair, hidden, params["small"][0], slope, params["w_up"], params["w_down"], pick],
-    )
-
-
-def attend_grad(grad, pair, mid, q, kv_parts, segs, att, lse, layer, params, pick):
+        [gmid, *pair, hidden, params["small"][0], slope, params["w_up"], params["w_down"]],
+    )
+
+
+def attend_grad(grad, pair, mid, q, kv_parts, mask, att, lse, layer, params):
     rows, width = q.shape
     heads = width // HD
     back = SPAN - 1
 
     def kernel(g_ref, own_ref, other_ref, mid_ref, q_ref, *refs):
         kv_refs, refs = refs[:SPAN], refs[SPAN:]
-        seg_q, seg_k, att_ref, lse_ref, gains, w_out, pick_ref = refs[:7]
-        gmid_ref, picked_ref, dq_ref, dkv_ref, small_ref = refs[7:12]
-        away_refs = refs[12:]
+        mask_ref, att_ref, lse_ref, gains, w_out = refs[:5]
+        gmid_ref, picked_ref, dq_ref, dkv_ref, small_ref = refs[5:10]
+        away_refs = refs[10:]
         d_norm = joined(own_ref, other_ref)
         hat, rstd = normalize(mid_ref[...])
         gmid = g_ref[...] + norm_bwd(d_norm, hat, rstd, gains[layer, 1:2])
         gmid_ref[...] = gmid
         mid_b = gmid.astype(bf16)
         d_att = mm(mid_b, w_out[layer], NT).astype(bf16)
-        allowed = allowed_of(seg_q, seg_k, rows)
+        allowed = mask_ref[...] > 0.0
         kv_all = jnp.concatenate([r[...] for r in kv_refs], axis=0)
         keys, values = kv_all[:, :width], kv_all[:, width:]
         query, logs = q_ref[...], lse_ref[...]
@@ -447,7 +465,8 @@
         for distance in range(1, SPAN):
             block = back - distance
             away_refs[distance - 1][...] = d_kv[block * rows : (block + 1) * rows].astype(bf16)
-        picked_ref[...] = mm(mid_b, pick_ref[...]).astype(bf16)
+        half = D // 2
+        picked_ref[:, :half], picked_ref[:, half:] = picked_halves(mid_b)
         small_ref[...] = jnp.zeros((8, D), f32)
         small_ref[0:1, :] = column_sum(d_norm * hat)
         small_ref[1:2, :] = column_sum(d_norm)
@@ -463,26 +482,30 @@
             ((8, D), f32),
         ]
         + [((rows, 2 * width), bf16)] * back,
-        [grad, *pair, mid, q, *kv_parts, *segs, att, lse]
-        + [params["small"][0], params["w_out"], pick],
-    )
-
-
-def project_grad(dq, dkv, arrived, picked, layer, params):
+        [grad, *pair, mid, q, *kv_parts, mask, att, lse]
+        + [params["small"][0], params["w_out"]],
+    )
+
+
+def project_grad(dq, dkv, arrived, picked, layer, params, more=()):
     rows, width = dq.shape
     half = D // 2
     pad = -(half + 3 * width) % 128
 
     def kernel(dq_ref, dkv_ref, *refs):
         near, refs = refs[: SPAN - 1], refs[SPAN - 1 :]
-        picked_ref, w_qkv, sent_ref, small_ref, keep_ref, give_ref = refs
+        picked_ref, w_qkv = refs[:2]
+        sent_ref, small_ref, keep_ref, give_ref = refs[-4:]
         d_kv = dkv_ref[...]
         for ref in near:
             d_kv = d_kv + ref[...].astype(f32)
         d_query = dq_ref[...]
         query_b, kv_b = d_query.astype(bf16), d_kv.astype(bf16)
         part = mm(kv_b, w_qkv[layer, width:]) + mm(query_b, w_qkv[layer, :width])
-        split_halves(part, keep_ref, give_ref)
+        own = rows // 2
+        split_halves(part, keep_ref.at[:own], give_ref.at[:own])
+        for ref, source in zip((keep_ref, give_ref), refs[2:-4]):
+            ref[own:, :] = source[...]
         sent_ref[:, :half] = picked_ref[:, half:]
         sent_ref[:, half : half + 2 * width] = kv_b
         sent_ref[:, half + 2 * width : half + 3 * width] = query_b
@@ -494,8 +517,9 @@
 
     return call(
         kernel,
-        [((rows, half + 3 * width + pad), bf16), ((8, D), f32)] + split_shapes(rows),
-        [dq, dkv, *arrived, picked, params["w_qkv"]],
+        [((rows, half + 3 * width + pad), bf16), ((8, D), f32)]
+        + split_shapes(rows * (2 if more else 1)),
+        [dq, dkv, *arrived, picked, params["w_qkv"], *more],
     )
 
 
@@ -510,7 +534,8 @@
     def kernel(keep_ref, give_ref, h_ref, *refs):
         mlp, att, qv, out = refs[:LAYERS], refs[LAYERS : 2 * LAYERS], refs[2 * LAYERS : -1], refs[-1]
         mine = lax.axis_index("tensor")
-        part = joined(keep_ref, give_ref)
+        own = h_ref.shape[0] // 2
+        part = joined(keep_ref.at[:own], give_ref.at[:own])
         hat, _ = normalize(h_ref[...])
         out[...] = jnp.zeros(out.shape, f32)
         for layer in range(LAYERS):
@@ -533,12 +558,14 @@
                 out[at : at + 1, :] = jnp.where(here, mlp[layer][0:1, :], 0.0)
 
     args = [keep, give, hidden, *mlp_small, *att_small, *qv_small]
-    return call(kernel, [((small_rows(count), D), f32)], args, 1e6)[0]
+    return call(kernel, [((small_rows(count), D), f32)], args)[0]
 
 
 def first_grad(gmid, pair, hidden, params, own_rows):
     def kernel(gmid_ref, own_ref, other_ref, h_ref, gains, in_ref, g_ref):
-        g_ref[...] = norm1_grad(gmid_ref, own_ref, other_ref, h_ref, gains, 0)[0]
+        own = h_ref.shape[0] // 2
+        near, away = own_ref.at[:own], other_ref.at[:own]
+        g_ref[...] = norm1_grad(gmid_ref, near, away, h_ref, gains, 0)[0]
         start = pl.multiple_of(lax.axis_index("tensor") * own_rows, own_rows)
         in_ref[...] = g_ref[pl.ds(start, own_rows), :].astype(bf16)
 
@@ -568,7 +595,6 @@
             ((LAYERS, count * D), f32),
         ],
         [total, other],
-        1e5,
     )
 
 
@@ -602,7 +628,7 @@
 class Halving:
     def __init__(self, products, wide):
         self.products, self.wide = products, wide
-        self.bits = [bit for bit in bits_of("dp") if bit != PAIR]
+        self.bits = [bit for bit in bits_of("dp") if bit != lax.axis_size("dp") // 4]
         self.block = D // lax.axis_size("dp")
         self.place = 0
 
@@ -628,14 +654,14 @@
             def kernel(*refs):
                 refs[count][...] = products_of(refs)
 
-            total = call(kernel, [((half, self.wide), f32)], flat, 3e8)[0]
+            total = call(kernel, [((half, self.wide), f32)], flat)[0]
             self.send, self.keep = split_plain(total, bit, block)
         else:
 
             def kernel(*refs):
                 split_rows(products_of(refs), bit, block, refs[count], refs[count + 1])
 
-            self.send, self.keep = call(kernel, [(shape, bf16), (shape, f32)], flat, 3e8)
+            self.send, self.keep = call(kernel, [(shape, bf16), (shape, f32)], flat)
 
     def launch(self, *gates):
         send = after(self.send, *gates) if gates else self.send
@@ -655,7 +681,7 @@
 
         shape = (self.keep.shape[0] // 2, self.wide)
         args = [self.keep, self.arrived]
-        self.send, self.keep = call(kernel, [(shape, bf16), (shape, f32)], args, 1e6)
+        self.send, self.keep = call(kernel, [(shape, bf16), (shape, f32)], args)
 
     def finish(self):
         while self.place < len(self.bits) - 1:
@@ -673,7 +699,7 @@
             down[layer] = total[:, inner:]
 
     args = [a for pair in parts for a in pair]
-    return call(kernel, [((LAYERS, block, inner), f32)] * 2, args, 1e6)
+    return call(kernel, [((LAYERS, block, inner), f32)] * 2, args)
 
 
 def att_outputs(parts, block, width):
@@ -684,14 +710,13 @@
             qkv[layer, 0] = total[:, 2 * width : 3 * width]
             qkv[layer, 1] = total[:, :width]
             qkv[layer, 2] = total[:, width : 2 * width]
-            out[layer] = total[:, 3 * width :]
+            out[layer] = total[:, 3 * width :].T
 
     args = [a for pair in parts for a in pair]
     return call(
         kernel,
-        [((LAYERS, 3, block, width), f32), ((LAYERS, block, width), f32)],
+        [((LAYERS, 3, block, width), f32), ((LAYERS, width, block), f32)],
         args,
-        1e6,
     )
 
 
@@ -700,7 +725,6 @@
 ):
     tensor_count = lax.axis_size("tensor")
     dp_count = lax.axis_size("dp")
-    dp_index = lax.axis_index("dp")
     own_rows = tokens.shape[0]
     rows = own_rows * tensor_count
     width = w_out.shape[1]
@@ -715,19 +739,11 @@
         "w_up": w_up,
         "w_down": w_down,
     }
-    seg_q = lax.dynamic_slice_in_dim(segments, dp_index * rows, rows)[:, None]
-    padded = jnp.concatenate([jnp.full(((SPAN - 1) * rows,), -1, jnp.int32), segments])
-    seg_k = lax.dynamic_slice_in_dim(padded, dp_index * rows, SPAN * rows)[None, :]
-    segs = [seg_q, seg_k]
-    column = lax.broadcasted_iota(jnp.int32, (D, D), 1)
-    side = ((dp_index >> 1) & 1) ^ (column // half)
-    column = column % half
-    piece = column // block
-    source = ((piece // 2) * 4 + side * 2 + piece % 2) * block + column % block
-    pick = (lax.broadcasted_iota(jnp.int32, (D, D), 0) == source).astype(bf16)
+    mask = allowed_rows(segments, rows)
+    near = dp_count // 4
 
     def paired(sent, kept, gate):
-        return [sent, swapped(after(sent, gate), "dp", PAIR), kept]
+        return [sent, swapped(after(sent, gate), "dp", near), kept]
 
     mlp_work = [
         Halving([((0, 0, 0), (1, half, half + inner)), ((1, 0, 0), (0, half, half + inner))], 2 * inner)
@@ -738,18 +754,19 @@
         for _ in range(LAYERS)
     ]
     token_pieces = gathered(tokens)
+    token_pieces[-1] = after(token_pieces[-1], mask)
     saved, rows_a, rows_b = [], [None] * LAYERS, [None] * LAYERS
     cot_pieces = None
     mid = pair = None
     for layer in range(LAYERS):
         if layer == 0:
-            hidden, picked1, q, kv = project_first(tokens, token_pieces[1:], params, pick)
+            hidden, picked1, q, kv = project_first(tokens, token_pieces[1:], params)
         else:
-            hidden, picked1, q, kv = project_next(mid, pair, layer, params, pick)
+            hidden, picked1, q, kv = project_next(mid, pair, layer, params)
         kv_parts = [shifted(kv, "dp", distance) for distance in range(SPAN - 1, 0, -1)] + [kv]
         if layer:
             q = after(q, rows_a[layer - 1][1], rows_b[layer - 1][1])
-        att, lse, sent_a, keep, give = attend(q, kv_parts, segs, picked1, layer, params)
+        att, lse, sent_a, keep, give = attend(q, kv_parts, mask, picked1, layer, params)
 
         def launch_a(gate):
             nonlocal cot_pieces
@@ -758,7 +775,7 @@
                 cot_pieces = gathered(after(cotangent, gate))
 
         pair = exchanged(keep, give, launch_a)
-        mid, slope, sent_b, kept_b, keep, give = feed_forward(hidden, pair, layer, params, pick)
+        mid, slope, sent_b, kept_b, keep, give = feed_forward(hidden, pair, layer, params)
         saved.append((hidden, q, kv_parts, att, lse, mid, slope))
         if layer < LAYERS - 1:
 
@@ -767,20 +784,21 @@
 
             pair = exchanged(keep, give, launch_b)
             pair[0] = after(pair[0], cot_pieces[-1])
-    last_total, last_give = keep, give
+    last_keep, last_give = keep, give
 
     mlp_small, att_small, qv_small = ([None] * LAYERS for _ in range(3))
     gmid = last_pair = None
     for layer in range(LAYERS - 1, -1, -1):
         last = layer == LAYERS - 1
+        later = layer + 1
         hidden, q, kv_parts, att, lse, mid, slope = saved[layer]
         if last:
             grad, sent1, mlp_small[layer], kept1, keep, give = mlp_grad_last(
-                cot_pieces, slope, params, pick
+                cot_pieces, slope, params
             )
         else:
             grad, sent1, mlp_small[layer], kept1, keep, give = mlp_grad_next(
-                gmid, pair, saved[layer + 1][0], slope, layer, params, pick
+                gmid, pair, saved[layer + 1][0], slope, layer, params
             )
         rows_1 = None
 
@@ -790,76 +808,76 @@
                 rows_b[layer] = paired(sent_b, kept_b, gate)
             rows_1 = paired(sent1, kept1, gate)
 
+        pair = exchanged(keep, give, launch_1)
         if last:
-            pair = exchanged(keep, give, launch_1)
             pair[0] = after(pair[0], rows_a[layer][1])
-        else:
-            later = layer + 1
-            mlp_work[later].absorb()
-            pair = exchanged(keep, give, launch_1, [mlp_work[later].send, att_work[later].send])
-            mlp_work[later].launch()
-            att_work[later].launch()
-            pair[0] = after(pair[0], last_pair[1])
         gmid, picked, dq, dkv, att_small[layer], *away = attend_grad(
-            grad, pair, mid, q, kv_parts, segs, att, lse, layer, params, pick
+            grad, pair, mid, q, kv_parts, mask, att, lse, layer, params
         )
         arrived = [shifted(a, "dp", -(place + 1)) for place, a in enumerate(away)]
         mlp_work[layer].begin([rows_b[layer], rows_1])
-        mlp_work[layer].launch()
         due = [mlp_work[layer].send]
         if last:
-            other = swapped(after(last_give, gmid), "tensor", 1)
-            last_total = last_total + other.astype(f32)
-            due.append(last_total)
+            mlp_work[layer].launch()
         else:
-            att_work[later].absorb()
-            due += [mlp_work[later].arrived, att_work[later].send]
+            mlp_work[later].absorb()
+            due += [mlp_work[later].send, att_work[later].send]
         sent2, qv_small[layer], keep, give = project_grad(
-            dq, after(dkv, *due), arrived, picked, layer, params
+            dq,
+            after(dkv, *due),
+            arrived,
+            picked,
+            layer,
+            params,
+            () if last else (last_keep, last_give),
         )
         rows_2 = None
 
         def launch_2(gate):
             nonlocal rows_2
             rows_2 = paired(sent2, picked, gate)
-            if last:
-                nonlocal last_total, last_pair
-                for bit in bits_of("tensor")[1:]:
-                    rounded = after(last_total.astype(bf16), gate)
-                    other = swapped(rounded, "tensor", bit)
-                    last_total = rounded.astype(f32) + other.astype(f32)
-                rounded = last_total.astype(bf16)
-                last_pair = [rounded, swapped(rounded, "tensor", 1)]
 
         if last:
             pair = exchanged(keep, give, launch_2)
-        else:
-            small = local_small(
-                keep, give, saved[0][0], mlp_small, att_small, qv_small, tensor_count, width
-            )
-            att_work[later].launch()
-            mlp_work[layer].absorb()
-            pair = exchanged(keep, give, launch_2)
-            mlp_work[layer].launch()
-            pair[0] = after(pair[0], rows_2[1], mlp_work[layer].send)
-        att_work[layer].begin([rows_a[layer], rows_2])
-        att_work[layer].launch()
+            att_work[layer].begin([rows_a[layer], rows_2])
+    small = local_small(
+        keep, give, saved[0][0], mlp_small, att_small, qv_small, tensor_count, width
+    )
+    rows_2 = [sent2, swapped(sent2, "dp", near), picked]
+    mlp_work[1].launch()
+    att_work[1].launch()
+    mlp_work[0].launch()
+    bits = bits_of("tensor")
+    dp_bits = bits_of("dp")
+    dp_bits = [near] + [bit for bit in dp_bits if bit != near]
+    total = keep
+    for place, bit in enumerate(bits):
+        rounded = give if place == 0 else total.astype(bf16)
+        other = swapped(rounded, "tensor", bit)
+        total = (total if place == 0 else rounded.astype(f32)) + other.astype(f32)
+        small = small + swapped(small, "tensor", bit)
+        total, small = lax.optimization_barrier((total, small))
+    total = after(total, mlp_work[1].arrived, att_work[1].arrived)
+    att_work[1].absorb()
+    att_work[1].launch()
+    rounded = total.astype(bf16)
+    pair = [rounded, swapped(rounded, "tensor", bits[0])]
+    small = small + swapped(after(small, total), "dp", dp_bits[0])
+    pair[0] = after(pair[0], small)
     input_grad = first_grad(gmid, pair, saved[0][0], params, own_rows)
-    result = last_rows(saved[-1][5], last_pair, params, own_rows)
-    for bit in bits_of("tensor"):
-        small = small + swapped(small, "tensor", bit)
-    gates = [mlp_work[0].send, att_work[0].send]
+    result = last_rows(saved[-1][5], pair, params, own_rows)
+    rows_2[1] = after(rows_2[1], input_grad, result)
+    att_work[0].begin([rows_a[0], rows_2])
+    att_work[0].launch()
+    mlp_work[0].arrived = after(mlp_work[0].arrived, att_work[0].send, att_work[1].arrived)
+    mlp_work[0].absorb()
+    mlp_work[0].launch()
+    small = after(small, mlp_work[0].send)
+    for bit in dp_bits[1:-1]:
+        small = small + swapped(small, "dp", bit)
     att_work[0].absorb()
     att_work[0].launch()
-    gates.append(att_work[0].send)
-    dp_bits = bits_of("dp")
-    for place, bit in enumerate(dp_bits):
-        if place < len(gates):
-            small = after(small, gates[place])
-        arriving = swapped(small, "dp", bit)
-        if bit != dp_bits[-1]:
-            small = small + arriving
-    small_grads = small_outs(small, arriving, tensor_count)
+    small_grads = small_outs(small, swapped(small, "dp", dp_bits[-1]), tensor_count)
     mlp_parts = [work.finish() for work in mlp_work]
     att_parts = [work.finish() for work in att_work]
     g_up, g_down = mlp_outputs(mlp_parts, block, inner)
@@ -868,7 +886,7 @@
         result,
         input_grad,
         g_qkv.transpose(0, 2, 1, 3),
-        g_out.transpose(0, 2, 1),
+        g_out,
         g_up,
         g_down.transpose(0, 2, 1),
         *small_grads,

time: 201 us -> 192 us (0.955)
  starting transfers between devices: 82.3 us -> 73.1 us
  waiting for transfers between devices: 87.1 us -> 93.7 us
  local copies, waits for them, and re-layouts: 6.22 us -> 1.84 us
    ppermute x51 -> x48, waiting for transfers between devices: 74 us -> 81.9 us  [swapped(): return lax.ppermute(array, axis, [(i, i ^ bit) for i in range(length)])]
    ppermute x51 -> x48, starting transfers between devices: 49.7 us -> 43.2 us  [swapped(): return lax.ppermute(array, axis, [(i, i ^ bit) for i in range(length)])]
    unnamed x29 -> x22, local copies, waits for them, and re-layouts: 5.26 us -> 1.84 us
    ppermute x12, starting transfers between devices: 32.6 us -> 29.9 us  [shifted(): return lax.ppermute(array, axis, pairs)]
    pallas_call x25 -> x26, Pallas kernels: 21.4 us -> 21 us  [call(): pl.pallas_call(kernel, out_shape=shapes, in_specs=[spec] * len(args), out...]
  transfers between devices with their start and end apart: 63 -> 60, of which waited for: 35 -> 35; matrix products, arithmetic and copies ran while one was open for 1% -> 0% of each run, Pallas kernels for 7% -> 7%
where the time goes in v4:
time: 192 us
  waiting for transfers between devices  93.7 us (49%)
  starting transfers between devices  73.1 us (38%)
  Pallas kernels  21.6 us (11%)
    ppermute x48, waiting for transfers between devices, swapped(): return lax.ppermute(array, axis, [(i, i ^ bit) for i in range(length)])  81.9 us
    ppermute x48, starting transfers between devices, swapped(): return lax.ppermute(array, axis, [(i, i ^ bit) for i in range(length)])  43.2 us
    ppermute x12, starting transfers between devices, shifted(): return lax.ppermute(array, axis, pairs)  29.9 us
    pallas_call x26, Pallas kernels, call(): pl.pallas_call(kernel, out_shape=shapes, in_specs=[spec] * len(args), out...  21 us
    ppermute x12, waiting for transfers between devices, shifted(): return lax.ppermute(array, axis, pairs)  11.8 us
  transfers between devices with their start and end apart: 60, of which 35 were waited for; matrix products, arithmetic and copies ran while one was open for 0% of the time, Pallas kernels for 7%

profile of v4, /device:TPU:0, one launch (start us, length us, event | category | flops | bytes accessed | tf_op | source)
XLA Modules:
  0.0 191.9 jit_solution(15897974798413301407)
XLA Ops:
  0.6 3.0 %collective-permute-start.1 = (bf16[32,768]{1,0:T(8,128)(2,1)}, bf16[32,768]{1,0:T(8,128)(2,1)S(1)}, u32[]{:S(2)}, u32[]{:S(2)}) collective-permute-start(bf16[32,768]{1,0:T(8,128)(2,1)} %refs_3_.2), channel_id=1, source_target_pairs={{0,2},{1,3},{2,0},{3,1},{4,6},{5,7},{6,4},{7,5},{8,10},{9,11},{10,... | collective-permute-start | bytes 147464 | tf_op jit(solution)/shard_map/ppermute | solution.py:29
  8.9 5.1 %collective-permute-start.3 = (bf16[128,384]{1,0:T(8,128)(2,1)S(1)}, bf16[128,384]{1,0:T(8,128)(2,1)S(1)}, u32[]{:S(2)}, u32[]{:S(2)}) collective-permute-start(bf16[128,384]{1,0:T(8,128)(2,1)S(1)} %get-tuple-element.129.refs_3_), channel_id=1, source_target_pairs={{0,12},{4,16},{8,20},{12,24},{16,28},{1,13},{5,17},{9,21},{13,25},... | collective-permute-start | bytes 294920 | tf_op jit(solution)/shard_map/ppermute | solution.py:24
  14.0 3.5 %collective-permute-start.4 = (bf16[128,384]{1,0:T(8,128)(2,1)S(1)}, bf16[128,384]{1,0:T(8,128)(2,1)S(1)}, u32[]{:S(2)}, u32[]{:S(2)}) collective-permute-start(bf16[128,384]{1,0:T(8,128)(2,1)S(1)} %get-tuple-element.129.refs_3_), channel_id=1, source_target_pairs={{0,8},{4,12},{8,16},{12,20},{16,24},{20,28},{1,9},{5,13},{9,17},{1... | collective-permute-start | bytes 294920 | tf_op jit(solution)/shard_map/ppermute | solution.py:24
  17.5 3.4 %collective-permute-start.5 = (bf16[128,384]{1,0:T(8,128)(2,1)S(1)}, bf16[128,384]{1,0:T(8,128)(2,1)S(1)}, u32[]{:S(2)}, u32[]{:S(2)}) collective-permute-start(bf16[128,384]{1,0:T(8,128)(2,1)S(1)} %get-tuple-element.129.refs_3_), channel_id=1, source_target_pairs={{0,4},{4,8},{8,12},{12,16},{16,20},{20,24},{24,28},{1,5},{5,9},{9,... | collective-permute-start | bytes 294920 | tf_op jit(solution)/shard_map/ppermute | solution.py:24
  27.7 3.4 %collective-permute-done.7 = bf16[64,768]{1,0:T(8,128)(2,1)S(1)} collective-permute-done((bf16[64,768]{1,0:T(8,128)(2,1)S(1)}, bf16[64,768]{1,0:T(8,128)(2,1)S(1)}, u32[]{:S(2)}, u32[]{:S(2)}) %collective-permute-start.7) | collective-permute-done | bytes 98336 | tf_op jit(solution)/shard_map/ppermute | solution.py:29
  37.0 3.4 %collective-permute-start.15 = (bf16[128,1152]{1,0:T(8,128)(2,1)S(1)}, bf16[128,1152]{1,0:T(8,128)(2,1)S(1)}, u32[]{:S(2)}, u32[]{:S(2)}) collective-permute-start(bf16[128,1152]{1,0:T(8,128)(2,1)S(1)} %get-tuple-element.143.refs_0_), channel_id=1, source_target_pairs={{0,8},{4,12},{8,0},{12,4},{16,24},{20,28},{24,16},{28,20},{1,9},{5... | collective-permute-start | bytes 884744 | tf_op jit(solution)/shard_map/ppermute | solution.py:29
  40.5 3.4 %collective-permute-start.14 = (bf16[128,640]{1,0:T(8,128)(2,1)S(1)}, bf16[128,640]{1,0:T(8,128)(2,1)S(1)}, u32[]{:S(2)}, u32[]{:S(2)}) collective-permute-start(bf16[128,640]{1,0:T(8,128)(2,1)S(1)} %get-tuple-element.141.refs_0_), channel_id=1, source_target_pairs={{0,8},{4,12},{8,0},{12,4},{16,24},{20,28},{24,16},{28,20},{1,9},{5... | collective-permute-start | bytes 491528 | tf_op jit(solution)/shard_map/ppermute | solution.py:29
  45.7 2.4 %collective-permute-start.16 = (bf16[128,384]{1,0:T(8,128)(2,1)S(1)}, bf16[128,384]{1,0:T(8,128)(2,1)S(1)}, u32[]{:S(2)}, u32[]{:S(2)}) collective-permute-start(bf16[128,384]{1,0:T(8,128)(2,1)S(1)} %get-tuple-element.145.refs_3_), channel_id=1, source_target_pairs={{0,12},{4,16},{8,20},{12,24},{16,28},{1,13},{5,17},{9,21},{13,25},... | collective-permute-start | bytes 294920 | tf_op jit(solution)/shard_map/ppermute | solution.py:24
  49.5 6.4 %collective-permute-start.18 = (bf16[128,384]{1,0:T(8,128)(2,1)S(1)}, bf16[128,384]{1,0:T(8,128)(2,1)S(1)}, u32[]{:S(2)}, u32[]{:S(2)}) collective-permute-start(bf16[128,384]{1,0:T(8,128)(2,1)S(1)} %get-tuple-element.145.refs_3_), channel_id=1, source_target_pairs={{0,4},{4,8},{8,12},{12,16},{16,20},{20,24},{24,28},{1,5},{5,9},{9,... | collective-permute-start | bytes 294920 | tf_op jit(solution)/shard_map/ppermute | solution.py:24
  62.6 3.4 %collective-permute-done.20 = bf16[64,768]{1,0:T(8,128)(2,1)S(1)} collective-permute-done((bf16[64,768]{1,0:T(8,128)(2,1)S(1)}, bf16[64,768]{1,0:T(8,128)(2,1)S(1)}, u32[]{:S(2)}, u32[]{:S(2)}) %collective-permute-start.20) | collective-permute-done | bytes 98336 | tf_op jit(solution)/shard_map/ppermute | solution.py:29
  76.5 2.9 %collective-permute-done.25.refs_1_ = bf16[128,640]{1,0:T(8,128)(2,1)S(1)} collective-permute-done((bf16[128,640]{1,0:T(8,128)(2,1)S(1)}, bf16[128,640]{1,0:T(8,128)(2,1)S(1)}, u32[]{:S(2)}, u32[]{:S(2)}) %collective-permute-start.25) | collective-permute-done | bytes 163872 | tf_op jit(solution)/shard_map/ppermute | solution.py:29
  85.7 7.4 %collective-permute-done.27.refs_1_ = bf16[128,1152]{1,0:T(8,128)(2,1)S(1)} collective-permute-done((bf16[128,1152]{1,0:T(8,128)(2,1)S(1)}, bf16[128,1152]{1,0:T(8,128)(2,1)S(1)}, u32[]{:S(2)}, u32[]{:S(2)}) %collective-permute-start.27) | collective-permute-done | bytes 294944 | tf_op jit(solution)/shard_map/ppermute | solution.py:29
  93.9 3.6 %collective-permute-done.30.refs_1_ = bf16[128,384]{1,0:T(8,128)(2,1)S(1)} collective-permute-done((bf16[128,384]{1,0:T(8,128)(2,1)S(1)}, bf16[128,384]{1,0:T(8,128)(2,1)S(1)}, u32[]{:S(2)}, u32[]{:S(2)}) %collective-permute-start.30) | collective-permute-done | bytes 98336 | tf_op jit(solution)/shard_map/ppermute | solution.py:24
  99.9 4.3 %collective-permute-done.33 = bf16[64,768]{1,0:T(8,128)(2,1)S(1)} collective-permute-done((bf16[64,768]{1,0:T(8,128)(2,1)S(1)}, bf16[64,768]{1,0:T(8,128)(2,1)S(1)}, u32[]{:S(2)}, u32[]{:S(2)}) %collective-permute-start.33) | collective-permute-done | bytes 98336 | tf_op jit(solution)/shard_map/ppermute | solution.py:29
  108.8 3.9 %collective-permute-start.40 = (bf16[128,1024]{1,0:T(8,128)(2,1)S(1)}, bf16[128,1024]{1,0:T(8,128)(2,1)S(1)}, u32[]{:S(2)}, u32[]{:S(2)}) collective-permute-start(bf16[128,1024]{1,0:T(8,128)(2,1)S(1)} %get-tuple-element.192.refs_3_), channel_id=1, source_target_pairs={{0,8},{4,12},{8,0},{12,4},{16,24},{20,28},{24,16},{28,20},{1,9},{5... | collective-permute-start | bytes 786440 | tf_op jit(solution)/shard_map/ppermute | solution.py:29
  123.4 2.7 %collective-permute-done.38.refs_4_ = bf16[128,1152]{1,0:T(8,128)(2,1)S(1)} collective-permute-done((bf16[128,1152]{1,0:T(8,128)(2,1)S(1)}, bf16[128,1152]{1,0:T(8,128)(2,1)S(1)}, u32[]{:S(2)}, u32[]{:S(2)}) %collective-permute-start.38) | collective-permute-done | bytes 294944 | tf_op jit(solution)/shard_map/ppermute | solution.py:29
  126.8 3.8 %collective-permute-done.42.refs_1_ = bf16[128,384]{1,0:T(8,128)(2,1)S(1)} collective-permute-done((bf16[128,384]{1,0:T(8,128)(2,1)S(1)}, bf16[128,384]{1,0:T(8,128)(2,1)S(1)}, u32[]{:S(2)}, u32[]{:S(2)}) %collective-permute-start.42) | collective-permute-done | bytes 98336 | tf_op jit(solution)/shard_map/ppermute | solution.py:24
  134.9 4.4 %collective-permute-start.49 = (bf16[192,768]{1,0:T(8,128)(2,1)S(1)}, bf16[192,768]{1,0:T(8,128)(2,1)S(1)}, u32[]{:S(2)}, u32[]{:S(2)}) collective-permute-start(bf16[192,768]{1,0:T(8,128)(2,1)S(1)} %get-tuple-element.193), channel_id=1, source_target_pairs={{0,4},{4,0},{8,12},{12,8},{16,20},{20,16},{24,28},{28,24},{1,5},{5... | collective-permute-start | bytes 884744 | tf_op jit(solution)/shard_map/ppermute | solution.py:29
  143.4 3.7 %collective-permute-done.49.arrived_ref = bf16[192,768]{1,0:T(8,128)(2,1)S(1)} collective-permute-done((bf16[192,768]{1,0:T(8,128)(2,1)S(1)}, bf16[192,768]{1,0:T(8,128)(2,1)S(1)}, u32[]{:S(2)}, u32[]{:S(2)}) %collective-permute-start.49) | collective-permute-done | bytes 294944 | tf_op jit(solution)/shard_map/ppermute | solution.py:29
  147.2 6.9 %collective-permute-done.48.refs_3_ = bf16[96,1536]{1,0:T(8,128)(2,1)S(1)} collective-permute-done((bf16[96,1536]{1,0:T(8,128)(2,1)S(1)}, bf16[96,1536]{1,0:T(8,128)(2,1)S(1)}, u32[]{:S(2)}, u32[]{:S(2)}) %collective-permute-start.48) | collective-permute-done | bytes 294944 | tf_op jit(solution)/shard_map/ppermute | solution.py:29
  155.1 4.9 %collective-permute-done.50 = f32[24,768]{1,0:T(8,128)S(1)} collective-permute-done((f32[24,768]{1,0:T(8,128)S(1)}, f32[24,768]{1,0:T(8,128)S(1)}, u32[]{:S(2)}, u32[]{:S(2)}) %collective-permute-start.50) | collective-permute-done | bytes 73760 | tf_op jit(solution)/shard_map/ppermute | solution.py:29
  165.3 7.0 %collective-permute-done.53.arrived_ref = bf16[192,768]{1,0:T(8,128)(2,1)S(1)} collective-permute-done((bf16[192,768]{1,0:T(8,128)(2,1)S(1)}, bf16[192,768]{1,0:T(8,128)(2,1)S(1)}, u32[]{:S(2)}, u32[]{:S(2)}) %collective-permute-start.53) | collective-permute-done | bytes 294944 | tf_op jit(solution)/shard_map/ppermute | solution.py:29
  173.1 2.4 %collective-permute-start.59 = (f32[24,768]{1,0:T(8,128)S(1)}, f32[24,768]{1,0:T(8,128)S(1)}, u32[]{:S(2)}, u32[]{:S(2)}) collective-permute-start(f32[24,768]{1,0:T(8,128)S(1)} %add.71.total_ref), channel_id=1, source_target_pairs={{0,16},{4,20},{8,24},{12,28},{16,0},{20,4},{24,8},{28,12},{1,17},{... | collective-permute-start | bytes 221192 | tf_op jit(solution)/shard_map/ppermute | solution.py:29
  175.4 13.6 %collective-permute-done.59.other_ref = f32[24,768]{1,0:T(8,128)S(1)} collective-permute-done((f32[24,768]{1,0:T(8,128)S(1)}, f32[24,768]{1,0:T(8,128)S(1)}, u32[]{:S(2)}, u32[]{:S(2)}) %collective-permute-start.59) | collective-permute-done | bytes 73760 | tf_op jit(solution)/shard_map/ppermute | solution.py:29
  (163 shorter events, 81.8 us)
Async XLA Ops:
  8.9 12.0 %collective-permute-start.3 = (bf16[128,384]{1,0:T(8,128)(2,1)S(1)}, bf16[128,384]{1,0:T(8,128)(2,1)S(1)}, u32[]{:S(2)}, u32[]{:S(2)}) collective-permute-start(bf16[128,384]{1,0:T(8,128)(2,1)S(1)} %get-tuple-element.129.refs_3_), channel_id=1, source_target_pairs={{0,12},{4,16},{8,20},{12,24},{16,28},{1,13},{5,17},{9,21},{13,25},... | collective-permute-start | bytes 294920 | tf_op jit(solution)/shard_map/ppermute | solution.py:24
  37.0 18.9 %collective-permute-start.15 = (bf16[128,1152]{1,0:T(8,128)(2,1)S(1)}, bf16[128,1152]{1,0:T(8,128)(2,1)S(1)}, u32[]{:S(2)}, u32[]{:S(2)}) collective-permute-start(bf16[128,1152]{1,0:T(8,128)(2,1)S(1)} %get-tuple-element.143.refs_0_), channel_id=1, source_target_pairs={{0,8},{4,12},{8,0},{12,4},{16,24},{20,28},{24,16},{28,20},{1,9},{5... | collective-permute-start | bytes 884744 | tf_op jit(solution)/shard_map/ppermute | solution.py:29
  40.5 15.4 %collective-permute-start.14 = (bf16[128,640]{1,0:T(8,128)(2,1)S(1)}, bf16[128,640]{1,0:T(8,128)(2,1)S(1)}, u32[]{:S(2)}, u32[]{:S(2)}) collective-permute-start(bf16[128,640]{1,0:T(8,128)(2,1)S(1)} %get-tuple-element.141.refs_0_), channel_id=1, source_target_pairs={{0,8},{4,12},{8,0},{12,4},{16,24},{20,28},{24,16},{28,20},{1,9},{5... | collective-permute-start | bytes 491528 | tf_op jit(solution)/shard_map/ppermute | solution.py:29
  45.7 10.2 %collective-permute-start.16 = (bf16[128,384]{1,0:T(8,128)(2,1)S(1)}, bf16[128,384]{1,0:T(8,128)(2,1)S(1)}, u32[]{:S(2)}, u32[]{:S(2)}) collective-permute-start(bf16[128,384]{1,0:T(8,128)(2,1)S(1)} %get-tuple-element.145.refs_3_), channel_id=1, source_target_pairs={{0,12},{4,16},{8,20},{12,24},{16,28},{1,13},{5,17},{9,21},{13,25},... | collective-permute-start | bytes 294920 | tf_op jit(solution)/shard_map/ppermute | solution.py:24
  74.3 11.3 %collective-permute-start.28 = (bf16[128,1152]{1,0:T(8,128)(2,1)S(1)}, bf16[128,1152]{1,0:T(8,128)(2,1)S(1)}, u32[]{:S(2)}, u32[]{:S(2)}) collective-permute-start(bf16[128,1152]{1,0:T(8,128)(2,1)S(1)} %get-tuple-element.166.refs_3_), channel_id=1, source_target_pairs={{0,8},{4,12},{8,0},{12,4},{16,24},{20,28},{24,16},{28,20},{1,9},{5... | collective-permute-start | bytes 884744 | tf_op jit(solution)/shard_map/ppermute | solution.py:29
  74.3 18.7 %collective-permute-start.27 = (bf16[128,1152]{1,0:T(8,128)(2,1)S(1)}, bf16[128,1152]{1,0:T(8,128)(2,1)S(1)}, u32[]{:S(2)}, u32[]{:S(2)}) collective-permute-start(bf16[128,1152]{1,0:T(8,128)(2,1)S(1)} %get-tuple-element.163.refs_0_), channel_id=1, source_target_pairs={{0,8},{4,12},{8,0},{12,4},{16,24},{20,28},{24,16},{28,20},{1,9},{5... | collective-permute-start | bytes 884744 | tf_op jit(solution)/shard_map/ppermute | solution.py:29
  81.3 12.6 %collective-permute-start.29 = (bf16[128,384]{1,0:T(8,128)(2,1)S(1)}, bf16[128,384]{1,0:T(8,128)(2,1)S(1)}, u32[]{:S(2)}, u32[]{:S(2)}) collective-permute-start(bf16[128,384]{1,0:T(8,128)(2,1)S(1)} %get-tuple-element.170), channel_id=1, source_target_pairs={{4,0},{8,4},{12,8},{16,12},{20,16},{24,20},{28,24},{5,1},{9,5},{13... | collective-permute-start | bytes 294920 | tf_op jit(solution)/shard_map/ppermute | solution.py:24
  82.6 14.9 %collective-permute-start.30 = (bf16[128,384]{1,0:T(8,128)(2,1)S(1)}, bf16[128,384]{1,0:T(8,128)(2,1)S(1)}, u32[]{:S(2)}, u32[]{:S(2)}) collective-permute-start(bf16[128,384]{1,0:T(8,128)(2,1)S(1)} %get-tuple-element.171), channel_id=1, source_target_pairs={{8,0},{12,4},{16,8},{20,12},{24,16},{28,20},{9,1},{13,5},{17,9},{2... | collective-permute-start | bytes 294920 | tf_op jit(solution)/shard_map/ppermute | solution.py:24
  83.9 13.6 %collective-permute-start.31 = (bf16[128,384]{1,0:T(8,128)(2,1)S(1)}, bf16[128,384]{1,0:T(8,128)(2,1)S(1)}, u32[]{:S(2)}, u32[]{:S(2)}) collective-permute-start(bf16[128,384]{1,0:T(8,128)(2,1)S(1)} %get-tuple-element.172), channel_id=1, source_target_pairs={{12,0},{16,4},{20,8},{24,12},{28,16},{13,1},{17,5},{21,9},{25,13},... | collective-permute-start | bytes 294920 | tf_op jit(solution)/shard_map/ppermute | solution.py:24
  107.1 16.2 %collective-permute-start.39 = (bf16[192,1536]{1,0:T(8,128)(2,1)S(1)}, bf16[192,1536]{1,0:T(8,128)(2,1)S(1)}, u32[]{:S(2)}, u32[]{:S(2)}) collective-permute-start(bf16[192,1536]{1,0:T(8,128)(2,1)S(1)} %get-tuple-element.168), channel_id=1, source_target_pairs={{0,4},{4,0},{8,12},{12,8},{16,20},{20,16},{24,28},{28,24},{1,5},{5... | collective-permute-start | bytes 1769480 | tf_op jit(solution)/shard_map/ppermute | solution.py:29
  108.8 11.0 %collective-permute-start.40 = (bf16[128,1024]{1,0:T(8,128)(2,1)S(1)}, bf16[128,1024]{1,0:T(8,128)(2,1)S(1)}, u32[]{:S(2)}, u32[]{:S(2)}) collective-permute-start(bf16[128,1024]{1,0:T(8,128)(2,1)S(1)} %get-tuple-element.192.refs_3_), channel_id=1, source_target_pairs={{0,8},{4,12},{8,0},{12,4},{16,24},{20,28},{24,16},{28,20},{1,9},{5... | collective-permute-start | bytes 786440 | tf_op jit(solution)/shard_map/ppermute | solution.py:29
  112.7 13.5 %collective-permute-start.38 = (bf16[128,1152]{1,0:T(8,128)(2,1)S(1)}, bf16[128,1152]{1,0:T(8,128)(2,1)S(1)}, u32[]{:S(2)}, u32[]{:S(2)}) collective-permute-start(bf16[128,1152]{1,0:T(8,128)(2,1)S(1)} %get-tuple-element.186.refs_3_), channel_id=1, source_target_pairs={{0,8},{4,12},{8,0},{12,4},{16,24},{20,28},{24,16},{28,20},{1,9},{5... | collective-permute-start | bytes 884744 | tf_op jit(solution)/shard_map/ppermute | solution.py:29
  116.6 10.3 %collective-permute-start.41 = (bf16[128,384]{1,0:T(8,128)(2,1)S(1)}, bf16[128,384]{1,0:T(8,128)(2,1)S(1)}, u32[]{:S(2)}, u32[]{:S(2)}) collective-permute-start(bf16[128,384]{1,0:T(8,128)(2,1)S(1)} %get-tuple-element.195), channel_id=1, source_target_pairs={{4,0},{8,4},{12,8},{16,12},{20,16},{24,20},{28,24},{5,1},{9,5},{13... | collective-permute-start | bytes 294920 | tf_op jit(solution)/shard_map/ppermute | solution.py:24
  117.9 12.8 %collective-permute-start.42 = (bf16[128,384]{1,0:T(8,128)(2,1)S(1)}, bf16[128,384]{1,0:T(8,128)(2,1)S(1)}, u32[]{:S(2)}, u32[]{:S(2)}) collective-permute-start(bf16[128,384]{1,0:T(8,128)(2,1)S(1)} %get-tuple-element.196), channel_id=1, source_target_pairs={{8,0},{12,4},{16,8},{20,12},{24,16},{28,20},{9,1},{13,5},{17,9},{2... | collective-permute-start | bytes 294920 | tf_op jit(solution)/shard_map/ppermute | solution.py:24
  119.8 10.8 %collective-permute-start.43 = (bf16[128,384]{1,0:T(8,128)(2,1)S(1)}, bf16[128,384]{1,0:T(8,128)(2,1)S(1)}, u32[]{:S(2)}, u32[]{:S(2)}) collective-permute-start(bf16[128,384]{1,0:T(8,128)(2,1)S(1)} %get-tuple-element.197), channel_id=1, source_target_pairs={{12,0},{16,4},{20,8},{24,12},{28,16},{13,1},{17,5},{21,9},{25,13},... | collective-permute-start | bytes 294920 | tf_op jit(solution)/shard_map/ppermute | solution.py:24
  132.8 10.5 %collective-permute-start.46 = (bf16[128,768]{1,0:T(8,128)(2,1)S(1)}, bf16[128,768]{1,0:T(8,128)(2,1)S(1)}, u32[]{:S(2)}, u32[]{:S(2)}) collective-permute-start(bf16[128,768]{1,0:T(8,128)(2,1)S(1)} %convert_add_fusion.1), channel_id=1, source_target_pairs={{0,2},{1,3},{2,0},{3,1},{4,6},{5,7},{6,4},{7,5},{8,10},{9,11},{10,... | collective-permute-start | bytes 589832 | tf_op jit(solution)/shard_map/ppermute | solution.py:29
  134.9 12.2 %collective-permute-start.49 = (bf16[192,768]{1,0:T(8,128)(2,1)S(1)}, bf16[192,768]{1,0:T(8,128)(2,1)S(1)}, u32[]{:S(2)}, u32[]{:S(2)}) collective-permute-start(bf16[192,768]{1,0:T(8,128)(2,1)S(1)} %get-tuple-element.193), channel_id=1, source_target_pairs={{0,4},{4,0},{8,12},{12,8},{16,20},{20,16},{24,28},{28,24},{1,5},{5... | collective-permute-start | bytes 884744 | tf_op jit(solution)/shard_map/ppermute | solution.py:29
  139.3 14.8 %collective-permute-start.48 = (bf16[96,1536]{1,0:T(8,128)(2,1)S(1)}, bf16[96,1536]{1,0:T(8,128)(2,1)S(1)}, u32[]{:S(2)}, u32[]{:S(2)}) collective-permute-start(bf16[96,1536]{1,0:T(8,128)(2,1)S(1)} %get-tuple-element.190), channel_id=1, source_target_pairs={{0,16},{4,20},{8,24},{12,28},{16,0},{20,4},{24,8},{28,12},{1,17},{... | collective-permute-start | bytes 884744 | tf_op jit(solution)/shard_map/ppermute | solution.py:29
  139.3 25.5 %collective-permute-start.56 = (bf16[192,1536]{1,0:T(8,128)(2,1)S(1)}, bf16[192,1536]{1,0:T(8,128)(2,1)S(1)}, u32[]{:S(2)}, u32[]{:S(2)}) collective-permute-start(bf16[192,1536]{1,0:T(8,128)(2,1)S(1)} %get-tuple-element.188), channel_id=1, source_target_pairs={{0,4},{4,0},{8,12},{12,8},{16,20},{20,16},{24,28},{28,24},{1,5},{5... | collective-permute-start | bytes 1769480 | tf_op jit(solution)/shard_map/ppermute | solution.py:29
  141.6 20.4 %collective-permute-start.52 = (bf16[128,1024]{1,0:T(8,128)(2,1)S(1)}, bf16[128,1024]{1,0:T(8,128)(2,1)S(1)}, u32[]{:S(2)}, u32[]{:S(2)}) collective-permute-start(bf16[128,1024]{1,0:T(8,128)(2,1)S(1)} %get-tuple-element.219.refs_3_), channel_id=1, source_target_pairs={{0,8},{4,12},{8,0},{12,4},{16,24},{20,28},{24,16},{28,20},{1,9},{5... | collective-permute-start | bytes 786440 | tf_op jit(solution)/shard_map/ppermute | solution.py:29
  154.2 10.6 %collective-permute-start.55 = (bf16[96,768]{1,0:T(8,128)(2,1)S(1)}, bf16[96,768]{1,0:T(8,128)(2,1)S(1)}, u32[]{:S(2)}, u32[]{:S(2)}) collective-permute-start(bf16[96,768]{1,0:T(8,128)(2,1)S(1)} %get-tuple-element.227), channel_id=1, source_target_pairs={{0,16},{4,20},{8,24},{12,28},{16,0},{20,4},{24,8},{28,12},{1,17},{... | collective-permute-start | bytes 442376 | tf_op jit(solution)/shard_map/ppermute | solution.py:29
  165.1 24.6 %collective-permute-start.57 = (bf16[96,1536]{1,0:T(8,128)(2,1)S(1)}, bf16[96,1536]{1,0:T(8,128)(2,1)S(1)}, u32[]{:S(2)}, u32[]{:S(2)}) collective-permute-start(bf16[96,1536]{1,0:T(8,128)(2,1)S(1)} %get-tuple-element.233), channel_id=1, source_target_pairs={{0,16},{4,20},{8,24},{12,28},{16,0},{20,4},{24,8},{28,12},{1,17},{... | collective-permute-start | bytes 884744 | tf_op jit(solution)/shard_map/ppermute | solution.py:29
  172.4 18.5 %collective-permute-start.54 = (bf16[96,768]{1,0:T(8,128)(2,1)S(1)}, bf16[96,768]{1,0:T(8,128)(2,1)S(1)}, u32[]{:S(2)}, u32[]{:S(2)}) collective-permute-start(bf16[96,768]{1,0:T(8,128)(2,1)S(1)} %get-tuple-element.224), channel_id=1, source_target_pairs={{0,16},{4,20},{8,24},{12,28},{16,0},{20,4},{24,8},{28,12},{1,17},{... | collective-permute-start | bytes 442376 | tf_op jit(solution)/shard_map/ppermute | solution.py:29
  173.1 16.0 %collective-permute-start.59 = (f32[24,768]{1,0:T(8,128)S(1)}, f32[24,768]{1,0:T(8,128)S(1)}, u32[]{:S(2)}, u32[]{:S(2)}) collective-permute-start(f32[24,768]{1,0:T(8,128)S(1)} %add.71.total_ref), channel_id=1, source_target_pairs={{0,16},{4,20},{8,24},{12,28},{16,0},{20,4},{24,8},{28,12},{1,17},{... | collective-permute-start | bytes 221192 | tf_op jit(solution)/shard_map/ppermute | solution.py:29
  (47 other events, 252.6 us)

commit v5 on v4

--- a/solution.py
+++ b/solution.py
@@ -775,6 +775,8 @@
                 cot_pieces = gathered(after(cotangent, gate))
 
         pair = exchanged(keep, give, launch_a)
+        if layer == LAYERS - 1:
+            pair[0] = after(pair[0], rows_a[layer][1])
         mid, slope, sent_b, kept_b, keep, give = feed_forward(hidden, pair, layer, params)
         saved.append((hidden, q, kv_parts, att, lse, mid, slope))
         if layer < LAYERS - 1:
@@ -806,22 +808,21 @@
             nonlocal rows_1
             if last:
                 rows_b[layer] = paired(sent_b, kept_b, gate)
-            rows_1 = paired(sent1, kept1, gate)
+            else:
+                rows_1 = paired(sent1, kept1, gate)
 
         pair = exchanged(keep, give, launch_1)
-        if last:
-            pair[0] = after(pair[0], rows_a[layer][1])
         gmid, picked, dq, dkv, att_small[layer], *away = attend_grad(
             grad, pair, mid, q, kv_parts, mask, att, lse, layer, params
         )
         arrived = [shifted(a, "dp", -(place + 1)) for place, a in enumerate(away)]
-        mlp_work[layer].begin([rows_b[layer], rows_1])
-        due = [mlp_work[layer].send]
+        due = []
         if last:
-            mlp_work[layer].launch()
+            due.append(rows_b[layer][1])
         else:
+            mlp_work[layer].begin([rows_b[layer], rows_1])
             mlp_work[later].absorb()
-            due += [mlp_work[later].send, att_work[later].send]
+            due += [mlp_work[layer].send, mlp_work[later].send, att_work[later].send]
         sent2, qv_small[layer], keep, give = project_grad(
             dq,
             after(dkv, *due),
@@ -838,18 +839,23 @@
             rows_2 = paired(sent2, picked, gate)
 
         if last:
-            pair = exchanged(keep, give, launch_2)
+
+            def launch_late(gate):
+                nonlocal rows_1
+                rows_1 = paired(sent1, kept1, gate)
+                launch_2(gate)
+
+            pair = exchanged(keep, give, launch_late)
+            mlp_work[layer].begin([rows_b[layer], rows_1])
+            mlp_work[layer].launch()
             att_work[layer].begin([rows_a[layer], rows_2])
     small = local_small(
         keep, give, saved[0][0], mlp_small, att_small, qv_small, tensor_count, width
     )
     rows_2 = [sent2, swapped(sent2, "dp", near), picked]
     mlp_work[1].launch()
-    att_work[1].launch()
     mlp_work[0].launch()
-    bits = bits_of("tensor")
-    dp_bits = bits_of("dp")
-    dp_bits = [near] + [bit for bit in dp_bits if bit != near]
+    bits, dp_bits = bits_of("tensor"), bits_of("dp")
     total = keep
     for place, bit in enumerate(bits):
         rounded = give if place == 0 else total.astype(bf16)
@@ -857,13 +863,13 @@
         total = (total if place == 0 else rounded.astype(f32)) + other.astype(f32)
         small = small + swapped(small, "tensor", bit)
         total, small = lax.optimization_barrier((total, small))
-    total = after(total, mlp_work[1].arrived, att_work[1].arrived)
+    att_work[1].launch(total)
+    small = small + swapped(small, "dp", dp_bits[-1])
+    total = after(total, small, mlp_work[1].arrived, att_work[1].arrived)
     att_work[1].absorb()
     att_work[1].launch()
     rounded = total.astype(bf16)
     pair = [rounded, swapped(rounded, "tensor", bits[0])]
-    small = small + swapped(after(small, total), "dp", dp_bits[0])
-    pair[0] = after(pair[0], small)
     input_grad = first_grad(gmid, pair, saved[0][0], params, own_rows)
     result = last_rows(saved[-1][5], pair, params, own_rows)
     rows_2[1] = after(rows_2[1], input_grad, result)
@@ -873,11 +879,14 @@
     mlp_work[0].absorb()
     mlp_work[0].launch()
     small = after(small, mlp_work[0].send)
-    for bit in dp_bits[1:-1]:
+    hops = dp_bits[:-1]
+    for bit in hops[:-1]:
         small = small + swapped(small, "dp", bit)
+    att_work[0].arrived = after(att_work[0].arrived, small)
     att_work[0].absorb()
     att_work[0].launch()
-    small_grads = small_outs(small, swapped(small, "dp", dp_bits[-1]), tensor_count)
+    small = after(small, att_work[0].send)
+    small_grads = small_outs(small, swapped(small, "dp", hops[-1]), tensor_count)
     mlp_parts = [work.finish() for work in mlp_work]
     att_parts = [work.finish() for work in att_work]
     g_up, g_down = mlp_outputs(mlp_parts, block, inner)

time: 192 us -> 187 us (0.974)
  waiting for transfers between devices: 93.7 us -> 90.6 us
  starting transfers between devices: 73.1 us -> 70.9 us
    ppermute x48, waiting for transfers between devices: 81.9 us -> 74.7 us  [swapped(): return lax.ppermute(array, axis, [(i, i ^ bit) for i in range(length)])]
    ppermute x48, starting transfers between devices: 43.2 us -> 37.9 us  [swapped(): return lax.ppermute(array, axis, [(i, i ^ bit) for i in range(length)])]
    ppermute x12, waiting for transfers between devices: 11.8 us -> 15.8 us  [shifted(): return lax.ppermute(array, axis, pairs)]
    ppermute x12, starting transfers between devices: 29.9 us -> 33 us  [shifted(): return lax.ppermute(array, axis, pairs)]
  transfers between devices with their start and end apart: 60 -> 60, of which waited for: 35 -> 38; matrix products, arithmetic and copies ran while one was open for 0% -> 0% of each run, Pallas kernels for 7% -> 8%
where the time goes in v5:
time: 187 us
  waiting for transfers between devices  90.6 us (48%)
  starting transfers between devices  70.9 us (38%)
  Pallas kernels  21.6 us (12%)
    ppermute x48, waiting for transfers between devices, swapped(): return lax.ppermute(array, axis, [(i, i ^ bit) for i in range(length)])  74.7 us
    ppermute x48, starting transfers between devices, swapped(): return lax.ppermute(array, axis, [(i, i ^ bit) for i in range(length)])  37.9 us
    ppermute x12, starting transfers between devices, shifted(): return lax.ppermute(array, axis, pairs)  33 us
    pallas_call x26, Pallas kernels, call(): pl.pallas_call(kernel, out_shape=shapes, in_specs=[spec] * len(args), out...  21 us
    ppermute x12, waiting for transfers between devices, shifted(): return lax.ppermute(array, axis, pairs)  15.8 us
  transfers between devices with their start and end apart: 60, of which 38 were waited for; matrix products, arithmetic and copies ran while one was open for 0% of the time, Pallas kernels for 8%

profile of v5, /device:TPU:0, one launch (start us, length us, event | category | flops | bytes accessed | tf_op | source)
XLA Modules:
  0.0 186.7 jit_solution(8177480677515406825)
XLA Ops:
  0.6 3.0 %collective-permute-start.1 = (bf16[32,768]{1,0:T(8,128)(2,1)}, bf16[32,768]{1,0:T(8,128)(2,1)S(1)}, u32[]{:S(2)}, u32[]{:S(2)}) collective-permute-start(bf16[32,768]{1,0:T(8,128)(2,1)} %refs_3_.2), channel_id=1, source_target_pairs={{0,2},{1,3},{2,0},{3,1},{4,6},{5,7},{6,4},{7,5},{8,10},{9,11},{10,... | collective-permute-start | bytes 147464 | tf_op jit(solution)/shard_map/ppermute | solution.py:29
  8.9 4.1 %collective-permute-start.5 = (bf16[128,384]{1,0:T(8,128)(2,1)S(1)}, bf16[128,384]{1,0:T(8,128)(2,1)S(1)}, u32[]{:S(2)}, u32[]{:S(2)}) collective-permute-start(bf16[128,384]{1,0:T(8,128)(2,1)S(1)} %get-tuple-element.130.refs_3_), channel_id=1, source_target_pairs={{0,4},{4,8},{8,12},{12,16},{16,20},{20,24},{24,28},{1,5},{5,9},{9,... | collective-permute-start | bytes 294920 | tf_op jit(solution)/shard_map/ppermute | solution.py:24
  13.0 3.5 %collective-permute-start.4 = (bf16[128,384]{1,0:T(8,128)(2,1)S(1)}, bf16[128,384]{1,0:T(8,128)(2,1)S(1)}, u32[]{:S(2)}, u32[]{:S(2)}) collective-permute-start(bf16[128,384]{1,0:T(8,128)(2,1)S(1)} %get-tuple-element.130.refs_3_), channel_id=1, source_target_pairs={{0,8},{4,12},{8,16},{12,20},{16,24},{20,28},{1,9},{5,13},{9,17},{1... | collective-permute-start | bytes 294920 | tf_op jit(solution)/shard_map/ppermute | solution.py:24
  16.5 4.4 %collective-permute-start.3 = (bf16[128,384]{1,0:T(8,128)(2,1)S(1)}, bf16[128,384]{1,0:T(8,128)(2,1)S(1)}, u32[]{:S(2)}, u32[]{:S(2)}) collective-permute-start(bf16[128,384]{1,0:T(8,128)(2,1)S(1)} %get-tuple-element.130.refs_3_), channel_id=1, source_target_pairs={{0,12},{4,16},{8,20},{12,24},{16,28},{1,13},{5,17},{9,21},{13,25},... | collective-permute-start | bytes 294920 | tf_op jit(solution)/shard_map/ppermute | solution.py:24
  27.7 3.4 %collective-permute-done.7 = bf16[64,768]{1,0:T(8,128)(2,1)S(1)} collective-permute-done((bf16[64,768]{1,0:T(8,128)(2,1)S(1)}, bf16[64,768]{1,0:T(8,128)(2,1)S(1)}, u32[]{:S(2)}, u32[]{:S(2)}) %collective-permute-start.7) | collective-permute-done | bytes 98336 | tf_op jit(solution)/shard_map/ppermute | solution.py:29
  37.2 3.1 %collective-permute-done.10 = bf16[64,768]{1,0:T(8,128)(2,1)S(1)} collective-permute-done((bf16[64,768]{1,0:T(8,128)(2,1)S(1)}, bf16[64,768]{1,0:T(8,128)(2,1)S(1)}, u32[]{:S(2)}, u32[]{:S(2)}) %collective-permute-start.10) | collective-permute-done | bytes 98336 | tf_op jit(solution)/shard_map/ppermute | solution.py:29
  42.7 5.5 %collective-permute-start.18 = (bf16[128,384]{1,0:T(8,128)(2,1)S(1)}, bf16[128,384]{1,0:T(8,128)(2,1)S(1)}, u32[]{:S(2)}, u32[]{:S(2)}) collective-permute-start(bf16[128,384]{1,0:T(8,128)(2,1)S(1)} %get-tuple-element.146.refs_3_), channel_id=1, source_target_pairs={{0,4},{4,8},{8,12},{12,16},{16,20},{20,24},{24,28},{1,5},{5,9},{9,... | collective-permute-start | bytes 294920 | tf_op jit(solution)/shard_map/ppermute | solution.py:24
  50.4 5.5 %collective-permute-start.16 = (bf16[128,384]{1,0:T(8,128)(2,1)S(1)}, bf16[128,384]{1,0:T(8,128)(2,1)S(1)}, u32[]{:S(2)}, u32[]{:S(2)}) collective-permute-start(bf16[128,384]{1,0:T(8,128)(2,1)S(1)} %get-tuple-element.146.refs_3_), channel_id=1, source_target_pairs={{0,12},{4,16},{8,20},{12,24},{16,28},{1,13},{5,17},{9,21},{13,25},... | collective-permute-start | bytes 294920 | tf_op jit(solution)/shard_map/ppermute | solution.py:24
  62.8 3.4 %collective-permute-done.20 = bf16[64,768]{1,0:T(8,128)(2,1)S(1)} collective-permute-done((bf16[64,768]{1,0:T(8,128)(2,1)S(1)}, bf16[64,768]{1,0:T(8,128)(2,1)S(1)}, u32[]{:S(2)}, u32[]{:S(2)}) %collective-permute-start.20) | collective-permute-done | bytes 98336 | tf_op jit(solution)/shard_map/ppermute | solution.py:29
  73.0 4.0 %collective-permute-done.25 = bf16[64,768]{1,0:T(8,128)(2,1)S(1)} collective-permute-done((bf16[64,768]{1,0:T(8,128)(2,1)S(1)}, bf16[64,768]{1,0:T(8,128)(2,1)S(1)}, u32[]{:S(2)}, u32[]{:S(2)}) %collective-permute-start.25) | collective-permute-done | bytes 98336 | tf_op jit(solution)/shard_map/ppermute | solution.py:29
  84.3 3.2 %collective-permute-done.28.refs_0_ = bf16[128,384]{1,0:T(8,128)(2,1)S(1)} collective-permute-done((bf16[128,384]{1,0:T(8,128)(2,1)S(1)}, bf16[128,384]{1,0:T(8,128)(2,1)S(1)}, u32[]{:S(2)}, u32[]{:S(2)}) %collective-permute-start.28) | collective-permute-done | bytes 98336 | tf_op jit(solution)/shard_map/ppermute | solution.py:24
  87.5 3.3 %collective-permute-done.29.refs_1_ = bf16[128,384]{1,0:T(8,128)(2,1)S(1)} collective-permute-done((bf16[128,384]{1,0:T(8,128)(2,1)S(1)}, bf16[128,384]{1,0:T(8,128)(2,1)S(1)}, u32[]{:S(2)}, u32[]{:S(2)}) %collective-permute-start.29) | collective-permute-done | bytes 98336 | tf_op jit(solution)/shard_map/ppermute | solution.py:24
  95.0 2.5 %collective-permute-start.38 = (bf16[128,1152]{1,0:T(8,128)(2,1)S(1)}, bf16[128,1152]{1,0:T(8,128)(2,1)S(1)}, u32[]{:S(2)}, u32[]{:S(2)}) collective-permute-start(bf16[128,1152]{1,0:T(8,128)(2,1)S(1)} %get-tuple-element.187.refs_3_), channel_id=1, source_target_pairs={{0,8},{4,12},{8,0},{12,4},{16,24},{20,28},{24,16},{28,20},{1,9},{5... | collective-permute-start | bytes 884744 | tf_op jit(solution)/shard_map/ppermute | solution.py:29
  102.3 2.3 %collective-permute-done.38.refs_4_ = bf16[128,1152]{1,0:T(8,128)(2,1)S(1)} collective-permute-done((bf16[128,1152]{1,0:T(8,128)(2,1)S(1)}, bf16[128,1152]{1,0:T(8,128)(2,1)S(1)}, u32[]{:S(2)}, u32[]{:S(2)}) %collective-permute-start.38) | collective-permute-done | bytes 294944 | tf_op jit(solution)/shard_map/ppermute | solution.py:29
  105.4 4.2 %collective-permute-start.39 = (bf16[192,1536]{1,0:T(8,128)(2,1)S(1)}, bf16[192,1536]{1,0:T(8,128)(2,1)S(1)}, u32[]{:S(2)}, u32[]{:S(2)}) collective-permute-start(bf16[192,1536]{1,0:T(8,128)(2,1)S(1)} %get-tuple-element.190), channel_id=1, source_target_pairs={{0,4},{4,0},{8,12},{12,8},{16,20},{20,16},{24,28},{28,24},{1,5},{5... | collective-permute-start | bytes 1769480 | tf_op jit(solution)/shard_map/ppermute | solution.py:29
  122.3 4.0 %collective-permute-done.37.refs_4_ = bf16[128,1152]{1,0:T(8,128)(2,1)S(1)} collective-permute-done((bf16[128,1152]{1,0:T(8,128)(2,1)S(1)}, bf16[128,1152]{1,0:T(8,128)(2,1)S(1)}, u32[]{:S(2)}, u32[]{:S(2)}) %collective-permute-start.37) | collective-permute-done | bytes 294944 | tf_op jit(solution)/shard_map/ppermute | solution.py:29
  127.2 3.1 %collective-permute-done.42.refs_1_ = bf16[128,384]{1,0:T(8,128)(2,1)S(1)} collective-permute-done((bf16[128,384]{1,0:T(8,128)(2,1)S(1)}, bf16[128,384]{1,0:T(8,128)(2,1)S(1)}, u32[]{:S(2)}, u32[]{:S(2)}) %collective-permute-start.42) | collective-permute-done | bytes 98336 | tf_op jit(solution)/shard_map/ppermute | solution.py:24
  136.3 5.0 %collective-permute-done.47 = f32[24,768]{1,0:T(8,128)S(1)} collective-permute-done((f32[24,768]{1,0:T(8,128)S(1)}, f32[24,768]{1,0:T(8,128)S(1)}, u32[]{:S(2)}, u32[]{:S(2)}) %collective-permute-start.47) | collective-permute-done | bytes 73760 | tf_op jit(solution)/shard_map/ppermute | solution.py:29
  141.4 3.2 %collective-permute-start.50 = (bf16[192,768]{1,0:T(8,128)(2,1)S(1)}, bf16[192,768]{1,0:T(8,128)(2,1)S(1)}, u32[]{:S(2)}, u32[]{:S(2)}) collective-permute-start(bf16[192,768]{1,0:T(8,128)(2,1)S(1)} %get-tuple-element.214), channel_id=1, source_target_pairs={{0,4},{4,0},{8,12},{12,8},{16,20},{20,16},{24,28},{28,24},{1,5},{5... | collective-permute-start | bytes 884744 | tf_op jit(solution)/shard_map/ppermute | solution.py:29
  145.3 8.1 %collective-permute-done.48 = f32[24,768]{1,0:T(8,128)S(1)} collective-permute-done((f32[24,768]{1,0:T(8,128)S(1)}, f32[24,768]{1,0:T(8,128)S(1)}, u32[]{:S(2)}, u32[]{:S(2)}) %collective-permute-start.48) | collective-permute-done | bytes 73760 | tf_op jit(solution)/shard_map/ppermute | solution.py:29
  157.9 3.5 %collective-permute-start.53 = (bf16[192,768]{1,0:T(8,128)(2,1)S(1)}, bf16[192,768]{1,0:T(8,128)(2,1)S(1)}, u32[]{:S(2)}, u32[]{:S(2)}) collective-permute-start(bf16[192,768]{1,0:T(8,128)(2,1)S(1)} %get-tuple-element.222), channel_id=1, source_target_pairs={{0,4},{4,0},{8,12},{12,8},{16,20},{20,16},{24,28},{28,24},{1,5},{5... | collective-permute-start | bytes 884744 | tf_op jit(solution)/shard_map/ppermute | solution.py:29
  161.4 3.7 %collective-permute-done.54.arrived_ref = bf16[192,1536]{1,0:T(8,128)(2,1)S(1)} collective-permute-done((bf16[192,1536]{1,0:T(8,128)(2,1)S(1)}, bf16[192,1536]{1,0:T(8,128)(2,1)S(1)}, u32[]{:S(2)}, u32[]{:S(2)}) %collective-permute-start.54) | collective-permute-done | bytes 589856 | tf_op jit(solution)/shard_map/ppermute | solution.py:29
  167.5 4.3 %collective-permute-done.56 = f32[24,768]{1,0:T(8,128)S(1)} collective-permute-done((f32[24,768]{1,0:T(8,128)S(1)}, f32[24,768]{1,0:T(8,128)S(1)}, u32[]{:S(2)}, u32[]{:S(2)}) %collective-permute-start.56) | collective-permute-done | bytes 73760 | tf_op jit(solution)/shard_map/ppermute | solution.py:29
  173.4 9.1 %collective-permute-done.58.refs_1_ = bf16[96,1536]{1,0:T(8,128)(2,1)S(1)} collective-permute-done((bf16[96,1536]{1,0:T(8,128)(2,1)S(1)}, bf16[96,1536]{1,0:T(8,128)(2,1)S(1)}, u32[]{:S(2)}, u32[]{:S(2)}) %collective-permute-start.58) | collective-permute-done | bytes 294944 | tf_op jit(solution)/shard_map/ppermute | solution.py:29
  (163 shorter events, 86.0 us)
Async XLA Ops:
  8.9 12.0 %collective-permute-start.5 = (bf16[128,384]{1,0:T(8,128)(2,1)S(1)}, bf16[128,384]{1,0:T(8,128)(2,1)S(1)}, u32[]{:S(2)}, u32[]{:S(2)}) collective-permute-start(bf16[128,384]{1,0:T(8,128)(2,1)S(1)} %get-tuple-element.130.refs_3_), channel_id=1, source_target_pairs={{0,4},{4,8},{8,12},{12,16},{16,20},{20,24},{24,28},{1,5},{5,9},{9,... | collective-permute-start | bytes 294920 | tf_op jit(solution)/shard_map/ppermute | solution.py:24
  37.0 19.0 %collective-permute-start.15 = (bf16[128,1152]{1,0:T(8,128)(2,1)S(1)}, bf16[128,1152]{1,0:T(8,128)(2,1)S(1)}, u32[]{:S(2)}, u32[]{:S(2)}) collective-permute-start(bf16[128,1152]{1,0:T(8,128)(2,1)S(1)} %get-tuple-element.144.refs_0_), channel_id=1, source_target_pairs={{0,8},{4,12},{8,0},{12,4},{16,24},{20,28},{24,16},{28,20},{1,9},{5... | collective-permute-start | bytes 884744 | tf_op jit(solution)/shard_map/ppermute | solution.py:29
  40.4 15.6 %collective-permute-start.14 = (bf16[128,640]{1,0:T(8,128)(2,1)S(1)}, bf16[128,640]{1,0:T(8,128)(2,1)S(1)}, u32[]{:S(2)}, u32[]{:S(2)}) collective-permute-start(bf16[128,640]{1,0:T(8,128)(2,1)S(1)} %get-tuple-element.142.refs_0_), channel_id=1, source_target_pairs={{0,8},{4,12},{8,0},{12,4},{16,24},{20,28},{24,16},{28,20},{1,9},{5... | collective-permute-start | bytes 491528 | tf_op jit(solution)/shard_map/ppermute | solution.py:29
  42.7 13.3 %collective-permute-start.18 = (bf16[128,384]{1,0:T(8,128)(2,1)S(1)}, bf16[128,384]{1,0:T(8,128)(2,1)S(1)}, u32[]{:S(2)}, u32[]{:S(2)}) collective-permute-start(bf16[128,384]{1,0:T(8,128)(2,1)S(1)} %get-tuple-element.146.refs_3_), channel_id=1, source_target_pairs={{0,4},{4,8},{8,12},{12,16},{16,20},{20,24},{24,28},{1,5},{5,9},{9,... | collective-permute-start | bytes 294920 | tf_op jit(solution)/shard_map/ppermute | solution.py:24
  72.7 11.6 %collective-permute-start.27 = (bf16[128,1152]{1,0:T(8,128)(2,1)S(1)}, bf16[128,1152]{1,0:T(8,128)(2,1)S(1)}, u32[]{:S(2)}, u32[]{:S(2)}) collective-permute-start(bf16[128,1152]{1,0:T(8,128)(2,1)S(1)} %get-tuple-element.164.refs_0_), channel_id=1, source_target_pairs={{0,8},{4,12},{8,0},{12,4},{16,24},{20,28},{24,16},{28,20},{1,9},{5... | collective-permute-start | bytes 884744 | tf_op jit(solution)/shard_map/ppermute | solution.py:29
  81.7 9.1 %collective-permute-start.29 = (bf16[128,384]{1,0:T(8,128)(2,1)S(1)}, bf16[128,384]{1,0:T(8,128)(2,1)S(1)}, u32[]{:S(2)}, u32[]{:S(2)}) collective-permute-start(bf16[128,384]{1,0:T(8,128)(2,1)S(1)} %get-tuple-element.167), channel_id=1, source_target_pairs={{8,0},{12,4},{16,8},{20,12},{24,16},{28,20},{9,1},{13,5},{17,9},{2... | collective-permute-start | bytes 294920 | tf_op jit(solution)/shard_map/ppermute | solution.py:24
  83.0 9.7 %collective-permute-start.30 = (bf16[128,384]{1,0:T(8,128)(2,1)S(1)}, bf16[128,384]{1,0:T(8,128)(2,1)S(1)}, u32[]{:S(2)}, u32[]{:S(2)}) collective-permute-start(bf16[128,384]{1,0:T(8,128)(2,1)S(1)} %get-tuple-element.168), channel_id=1, source_target_pairs={{12,0},{16,4},{20,8},{24,12},{28,16},{13,1},{17,5},{21,9},{25,13},... | collective-permute-start | bytes 294920 | tf_op jit(solution)/shard_map/ppermute | solution.py:24
  95.0 9.5 %collective-permute-start.38 = (bf16[128,1152]{1,0:T(8,128)(2,1)S(1)}, bf16[128,1152]{1,0:T(8,128)(2,1)S(1)}, u32[]{:S(2)}, u32[]{:S(2)}) collective-permute-start(bf16[128,1152]{1,0:T(8,128)(2,1)S(1)} %get-tuple-element.187.refs_3_), channel_id=1, source_target_pairs={{0,8},{4,12},{8,0},{12,4},{16,24},{20,28},{24,16},{28,20},{1,9},{5... | collective-permute-start | bytes 884744 | tf_op jit(solution)/shard_map/ppermute | solution.py:29
  105.4 21.6 %collective-permute-start.39 = (bf16[192,1536]{1,0:T(8,128)(2,1)S(1)}, bf16[192,1536]{1,0:T(8,128)(2,1)S(1)}, u32[]{:S(2)}, u32[]{:S(2)}) collective-permute-start(bf16[192,1536]{1,0:T(8,128)(2,1)S(1)} %get-tuple-element.190), channel_id=1, source_target_pairs={{0,4},{4,0},{8,12},{12,8},{16,20},{20,16},{24,28},{28,24},{1,5},{5... | collective-permute-start | bytes 1769480 | tf_op jit(solution)/shard_map/ppermute | solution.py:29
  111.2 9.2 %collective-permute-start.40 = (bf16[128,1024]{1,0:T(8,128)(2,1)S(1)}, bf16[128,1024]{1,0:T(8,128)(2,1)S(1)}, u32[]{:S(2)}, u32[]{:S(2)}) collective-permute-start(bf16[128,1024]{1,0:T(8,128)(2,1)S(1)} %get-tuple-element.193.refs_3_), channel_id=1, source_target_pairs={{0,8},{4,12},{8,0},{12,4},{16,24},{20,28},{24,16},{28,20},{1,9},{5... | collective-permute-start | bytes 786440 | tf_op jit(solution)/shard_map/ppermute | solution.py:29
  111.5 14.8 %collective-permute-start.37 = (bf16[128,1152]{1,0:T(8,128)(2,1)S(1)}, bf16[128,1152]{1,0:T(8,128)(2,1)S(1)}, u32[]{:S(2)}, u32[]{:S(2)}) collective-permute-start(bf16[128,1152]{1,0:T(8,128)(2,1)S(1)} %get-tuple-element.182.refs_3_), channel_id=1, source_target_pairs={{0,8},{4,12},{8,0},{12,4},{16,24},{20,28},{24,16},{28,20},{1,9},{5... | collective-permute-start | bytes 884744 | tf_op jit(solution)/shard_map/ppermute | solution.py:29
  117.7 9.5 %collective-permute-start.41 = (bf16[128,384]{1,0:T(8,128)(2,1)S(1)}, bf16[128,384]{1,0:T(8,128)(2,1)S(1)}, u32[]{:S(2)}, u32[]{:S(2)}) collective-permute-start(bf16[128,384]{1,0:T(8,128)(2,1)S(1)} %get-tuple-element.196), channel_id=1, source_target_pairs={{4,0},{8,4},{12,8},{16,12},{20,16},{24,20},{28,24},{5,1},{9,5},{13... | collective-permute-start | bytes 294920 | tf_op jit(solution)/shard_map/ppermute | solution.py:24
  119.0 11.2 %collective-permute-start.42 = (bf16[128,384]{1,0:T(8,128)(2,1)S(1)}, bf16[128,384]{1,0:T(8,128)(2,1)S(1)}, u32[]{:S(2)}, u32[]{:S(2)}) collective-permute-start(bf16[128,384]{1,0:T(8,128)(2,1)S(1)} %get-tuple-element.197), channel_id=1, source_target_pairs={{8,0},{12,4},{16,8},{20,12},{24,16},{28,20},{9,1},{13,5},{17,9},{2... | collective-permute-start | bytes 294920 | tf_op jit(solution)/shard_map/ppermute | solution.py:24
  120.5 9.8 %collective-permute-start.43 = (bf16[128,384]{1,0:T(8,128)(2,1)S(1)}, bf16[128,384]{1,0:T(8,128)(2,1)S(1)}, u32[]{:S(2)}, u32[]{:S(2)}) collective-permute-start(bf16[128,384]{1,0:T(8,128)(2,1)S(1)} %get-tuple-element.198), channel_id=1, source_target_pairs={{12,0},{16,4},{20,8},{24,12},{28,16},{13,1},{17,5},{21,9},{25,13},... | collective-permute-start | bytes 294920 | tf_op jit(solution)/shard_map/ppermute | solution.py:24
  132.5 8.8 %collective-permute-start.46 = (bf16[128,768]{1,0:T(8,128)(2,1)S(1)}, bf16[128,768]{1,0:T(8,128)(2,1)S(1)}, u32[]{:S(2)}, u32[]{:S(2)}) collective-permute-start(bf16[128,768]{1,0:T(8,128)(2,1)S(1)} %convert_add_fusion.1), channel_id=1, source_target_pairs={{0,2},{1,3},{2,0},{3,1},{4,6},{5,7},{6,4},{7,5},{8,10},{9,11},{10,... | collective-permute-start | bytes 589832 | tf_op jit(solution)/shard_map/ppermute | solution.py:29
  134.6 18.8 %collective-permute-start.49 = (bf16[96,1536]{1,0:T(8,128)(2,1)S(1)}, bf16[96,1536]{1,0:T(8,128)(2,1)S(1)}, u32[]{:S(2)}, u32[]{:S(2)}) collective-permute-start(bf16[96,1536]{1,0:T(8,128)(2,1)S(1)} %get-tuple-element.191), channel_id=1, source_target_pairs={{0,16},{4,20},{8,24},{12,28},{16,0},{20,4},{24,8},{28,12},{1,17},{... | collective-permute-start | bytes 884744 | tf_op jit(solution)/shard_map/ppermute | solution.py:29
  141.4 12.1 %collective-permute-start.50 = (bf16[192,768]{1,0:T(8,128)(2,1)S(1)}, bf16[192,768]{1,0:T(8,128)(2,1)S(1)}, u32[]{:S(2)}, u32[]{:S(2)}) collective-permute-start(bf16[192,768]{1,0:T(8,128)(2,1)S(1)} %get-tuple-element.214), channel_id=1, source_target_pairs={{0,4},{4,0},{8,12},{12,8},{16,20},{20,16},{24,28},{28,24},{1,5},{5... | collective-permute-start | bytes 884744 | tf_op jit(solution)/shard_map/ppermute | solution.py:29
  144.6 20.5 %collective-permute-start.54 = (bf16[192,1536]{1,0:T(8,128)(2,1)S(1)}, bf16[192,1536]{1,0:T(8,128)(2,1)S(1)}, u32[]{:S(2)}, u32[]{:S(2)}) collective-permute-start(bf16[192,1536]{1,0:T(8,128)(2,1)S(1)} %get-tuple-element.184), channel_id=1, source_target_pairs={{0,4},{4,0},{8,12},{12,8},{16,20},{20,16},{24,28},{28,24},{1,5},{5... | collective-permute-start | bytes 1769480 | tf_op jit(solution)/shard_map/ppermute | solution.py:29
  145.1 12.2 %collective-permute-start.52 = (bf16[128,1024]{1,0:T(8,128)(2,1)S(1)}, bf16[128,1024]{1,0:T(8,128)(2,1)S(1)}, u32[]{:S(2)}, u32[]{:S(2)}) collective-permute-start(bf16[128,1024]{1,0:T(8,128)(2,1)S(1)} %get-tuple-element.219.refs_3_), channel_id=1, source_target_pairs={{0,8},{4,12},{8,0},{12,4},{16,24},{20,28},{24,16},{28,20},{1,9},{5... | collective-permute-start | bytes 786440 | tf_op jit(solution)/shard_map/ppermute | solution.py:29
  153.6 11.5 %collective-permute-start.55 = (bf16[96,768]{1,0:T(8,128)(2,1)S(1)}, bf16[96,768]{1,0:T(8,128)(2,1)S(1)}, u32[]{:S(2)}, u32[]{:S(2)}) collective-permute-start(bf16[96,768]{1,0:T(8,128)(2,1)S(1)} %get-tuple-element.225), channel_id=1, source_target_pairs={{0,16},{4,20},{8,24},{12,28},{16,0},{20,4},{24,8},{28,12},{1,17},{... | collective-permute-start | bytes 442376 | tf_op jit(solution)/shard_map/ppermute | solution.py:29
  157.9 13.9 %collective-permute-start.53 = (bf16[192,768]{1,0:T(8,128)(2,1)S(1)}, bf16[192,768]{1,0:T(8,128)(2,1)S(1)}, u32[]{:S(2)}, u32[]{:S(2)}) collective-permute-start(bf16[192,768]{1,0:T(8,128)(2,1)S(1)} %get-tuple-element.222), channel_id=1, source_target_pairs={{0,4},{4,0},{8,12},{12,8},{16,20},{20,16},{24,28},{28,24},{1,5},{5... | collective-permute-start | bytes 884744 | tf_op jit(solution)/shard_map/ppermute | solution.py:29
  165.3 17.2 %collective-permute-start.58 = (bf16[96,1536]{1,0:T(8,128)(2,1)S(1)}, bf16[96,1536]{1,0:T(8,128)(2,1)S(1)}, u32[]{:S(2)}, u32[]{:S(2)}) collective-permute-start(bf16[96,1536]{1,0:T(8,128)(2,1)S(1)} %get-tuple-element.227), channel_id=1, source_target_pairs={{0,16},{4,20},{8,24},{12,28},{16,0},{20,4},{24,8},{28,12},{1,17},{... | collective-permute-start | bytes 884744 | tf_op jit(solution)/shard_map/ppermute | solution.py:29
  172.0 13.6 %collective-permute-start.57 = (bf16[96,768]{1,0:T(8,128)(2,1)S(1)}, bf16[96,768]{1,0:T(8,128)(2,1)S(1)}, u32[]{:S(2)}, u32[]{:S(2)}) collective-permute-start(bf16[96,768]{1,0:T(8,128)(2,1)S(1)} %get-tuple-element.231), channel_id=1, source_target_pairs={{0,16},{4,20},{8,24},{12,28},{16,0},{20,4},{24,8},{28,12},{1,17},{... | collective-permute-start | bytes 442376 | tf_op jit(solution)/shard_map/ppermute | solution.py:29
  172.9 10.8 %collective-permute-start.59 = (f32[24,768]{1,0:T(8,128)S(1)}, f32[24,768]{1,0:T(8,128)S(1)}, u32[]{:S(2)}, u32[]{:S(2)}) collective-permute-start(f32[24,768]{1,0:T(8,128)S(1)} %add.71.total_ref), channel_id=1, source_target_pairs={{0,8},{4,12},{8,0},{12,4},{16,24},{20,28},{24,16},{28,20},{1,9},{5... | collective-permute-start | bytes 221192 | tf_op jit(solution)/shard_map/ppermute | solution.py:29
  (47 other events, 247.8 us)

commit v6 on v5

--- a/solution.py
+++ b/solution.py
@@ -815,7 +815,7 @@
         gmid, picked, dq, dkv, att_small[layer], *away = attend_grad(
             grad, pair, mid, q, kv_parts, mask, att, lse, layer, params
         )
-        arrived = [shifted(a, "dp", -(place + 1)) for place, a in enumerate(away)]
+        arrived = [shifted(away[by - 1], "dp", -by) for by in range(SPAN - 1, 0, -1)]
         due = []
         if last:
             due.append(rows_b[layer][1])

time: 187 us -> 185 us (0.989)
  waiting for transfers between devices: 90.6 us -> 86.5 us
  starting transfers between devices: 70.9 us -> 73.2 us
    ppermute x12, waiting for transfers between devices: 15.8 us -> 11.5 us  [shifted(): return lax.ppermute(array, axis, pairs)]
    ppermute x48, starting transfers between devices: 37.9 us -> 40.1 us  [swapped(): return lax.ppermute(array, axis, [(i, i ^ bit) for i in range(length)])]
  transfers between devices with their start and end apart: 60 -> 60, of which waited for: 38 -> 37; matrix products, arithmetic and copies ran while one was open for 0% -> 0% of each run, Pallas kernels for 8% -> 8%
where the time goes in v6:
time: 185 us
  waiting for transfers between devices  86.5 us (47%)
  starting transfers between devices  73.2 us (40%)
  Pallas kernels  21.6 us (12%)
    ppermute x48, waiting for transfers between devices, swapped(): return lax.ppermute(array, axis, [(i, i ^ bit) for i in range(length)])  75 us
    ppermute x48, starting transfers between devices, swapped(): return lax.ppermute(array, axis, [(i, i ^ bit) for i in range(length)])  40.1 us
    ppermute x12, starting transfers between devices, shifted(): return lax.ppermute(array, axis, pairs)  33 us
    pallas_call x26, Pallas kernels, call(): pl.pallas_call(kernel, out_shape=shapes, in_specs=[spec] * len(args), out...  21 us
    ppermute x12, waiting for transfers between devices, shifted(): return lax.ppermute(array, axis, pairs)  11.5 us
  transfers between devices with their start and end apart: 60, of which 37 were waited for; matrix products, arithmetic and copies ran while one was open for 0% of the time, Pallas kernels for 8%

profile of v6, /device:TPU:0, one launch (start us, length us, event | category | flops | bytes accessed | tf_op | source)
XLA Modules:
  0.0 184.8 jit_solution(3028882203786753228)
XLA Ops:
  0.6 3.0 %collective-permute-start.1 = (bf16[32,768]{1,0:T(8,128)(2,1)}, bf16[32,768]{1,0:T(8,128)(2,1)S(1)}, u32[]{:S(2)}, u32[]{:S(2)}) collective-permute-start(bf16[32,768]{1,0:T(8,128)(2,1)} %refs_3_.2), channel_id=1, source_target_pairs={{0,2},{1,3},{2,0},{3,1},{4,6},{5,7},{6,4},{7,5},{8,10},{9,11},{10,... | collective-permute-start | bytes 147464 | tf_op jit(solution)/shard_map/ppermute | solution.py:29
  3.7 2.3 %collective-permute-done.1.refs_1_ = bf16[32,768]{1,0:T(8,128)(2,1)S(1)} collective-permute-done((bf16[32,768]{1,0:T(8,128)(2,1)}, bf16[32,768]{1,0:T(8,128)(2,1)S(1)}, u32[]{:S(2)}, u32[]{:S(2)}) %collective-permute-start.1) | collective-permute-done | bytes 49184 | tf_op jit(solution)/shard_map/ppermute | solution.py:29
  8.9 4.1 %collective-permute-start.5 = (bf16[128,384]{1,0:T(8,128)(2,1)S(1)}, bf16[128,384]{1,0:T(8,128)(2,1)S(1)}, u32[]{:S(2)}, u32[]{:S(2)}) collective-permute-start(bf16[128,384]{1,0:T(8,128)(2,1)S(1)} %get-tuple-element.130.refs_3_), channel_id=1, source_target_pairs={{0,4},{4,8},{8,12},{12,16},{16,20},{20,24},{24,28},{1,5},{5,9},{9,... | collective-permute-start | bytes 294920 | tf_op jit(solution)/shard_map/ppermute | solution.py:24
  13.0 3.5 %collective-permute-start.4 = (bf16[128,384]{1,0:T(8,128)(2,1)S(1)}, bf16[128,384]{1,0:T(8,128)(2,1)S(1)}, u32[]{:S(2)}, u32[]{:S(2)}) collective-permute-start(bf16[128,384]{1,0:T(8,128)(2,1)S(1)} %get-tuple-element.130.refs_3_), channel_id=1, source_target_pairs={{0,8},{4,12},{8,16},{12,20},{16,24},{20,28},{1,9},{5,13},{9,17},{1... | collective-permute-start | bytes 294920 | tf_op jit(solution)/shard_map/ppermute | solution.py:24
  16.5 4.4 %collective-permute-start.3 = (bf16[128,384]{1,0:T(8,128)(2,1)S(1)}, bf16[128,384]{1,0:T(8,128)(2,1)S(1)}, u32[]{:S(2)}, u32[]{:S(2)}) collective-permute-start(bf16[128,384]{1,0:T(8,128)(2,1)S(1)} %get-tuple-element.130.refs_3_), channel_id=1, source_target_pairs={{0,12},{4,16},{8,20},{12,24},{16,28},{1,13},{5,17},{9,21},{13,25},... | collective-permute-start | bytes 294920 | tf_op jit(solution)/shard_map/ppermute | solution.py:24
  27.7 3.4 %collective-permute-done.7 = bf16[64,768]{1,0:T(8,128)(2,1)S(1)} collective-permute-done((bf16[64,768]{1,0:T(8,128)(2,1)S(1)}, bf16[64,768]{1,0:T(8,128)(2,1)S(1)}, u32[]{:S(2)}, u32[]{:S(2)}) %collective-permute-start.7) | collective-permute-done | bytes 98336 | tf_op jit(solution)/shard_map/ppermute | solution.py:29
  37.2 3.1 %collective-permute-done.10 = bf16[64,768]{1,0:T(8,128)(2,1)S(1)} collective-permute-done((bf16[64,768]{1,0:T(8,128)(2,1)S(1)}, bf16[64,768]{1,0:T(8,128)(2,1)S(1)}, u32[]{:S(2)}, u32[]{:S(2)}) %collective-permute-start.10) | collective-permute-done | bytes 98336 | tf_op jit(solution)/shard_map/ppermute | solution.py:29
  42.7 5.5 %collective-permute-start.18 = (bf16[128,384]{1,0:T(8,128)(2,1)S(1)}, bf16[128,384]{1,0:T(8,128)(2,1)S(1)}, u32[]{:S(2)}, u32[]{:S(2)}) collective-permute-start(bf16[128,384]{1,0:T(8,128)(2,1)S(1)} %get-tuple-element.146.refs_3_), channel_id=1, source_target_pairs={{0,4},{4,8},{8,12},{12,16},{16,20},{20,24},{24,28},{1,5},{5,9},{9,... | collective-permute-start | bytes 294920 | tf_op jit(solution)/shard_map/ppermute | solution.py:24
  48.2 2.3 %collective-permute-start.17 = (bf16[128,384]{1,0:T(8,128)(2,1)S(1)}, bf16[128,384]{1,0:T(8,128)(2,1)S(1)}, u32[]{:S(2)}, u32[]{:S(2)}) collective-permute-start(bf16[128,384]{1,0:T(8,128)(2,1)S(1)} %get-tuple-element.146.refs_3_), channel_id=1, source_target_pairs={{0,8},{4,12},{8,16},{12,20},{16,24},{20,28},{1,9},{5,13},{9,17},{1... | collective-permute-start | bytes 294920 | tf_op jit(solution)/shard_map/ppermute | solution.py:24
  50.4 5.5 %collective-permute-start.16 = (bf16[128,384]{1,0:T(8,128)(2,1)S(1)}, bf16[128,384]{1,0:T(8,128)(2,1)S(1)}, u32[]{:S(2)}, u32[]{:S(2)}) collective-permute-start(bf16[128,384]{1,0:T(8,128)(2,1)S(1)} %get-tuple-element.146.refs_3_), channel_id=1, source_target_pairs={{0,12},{4,16},{8,20},{12,24},{16,28},{1,13},{5,17},{9,21},{13,25},... | collective-permute-start | bytes 294920 | tf_op jit(solution)/shard_map/ppermute | solution.py:24
  62.8 3.4 %collective-permute-done.20 = bf16[64,768]{1,0:T(8,128)(2,1)S(1)} collective-permute-done((bf16[64,768]{1,0:T(8,128)(2,1)S(1)}, bf16[64,768]{1,0:T(8,128)(2,1)S(1)}, u32[]{:S(2)}, u32[]{:S(2)}) %collective-permute-start.20) | collective-permute-done | bytes 98336 | tf_op jit(solution)/shard_map/ppermute | solution.py:29
  73.0 4.0 %collective-permute-done.25 = bf16[64,768]{1,0:T(8,128)(2,1)S(1)} collective-permute-done((bf16[64,768]{1,0:T(8,128)(2,1)S(1)}, bf16[64,768]{1,0:T(8,128)(2,1)S(1)}, u32[]{:S(2)}, u32[]{:S(2)}) %collective-permute-start.25) | collective-permute-done | bytes 98336 | tf_op jit(solution)/shard_map/ppermute | solution.py:29
  84.3 4.5 %collective-permute-done.28.refs_0_ = bf16[128,384]{1,0:T(8,128)(2,1)S(1)} collective-permute-done((bf16[128,384]{1,0:T(8,128)(2,1)S(1)}, bf16[128,384]{1,0:T(8,128)(2,1)S(1)}, u32[]{:S(2)}, u32[]{:S(2)}) %collective-permute-start.28) | collective-permute-done | bytes 98336 | tf_op jit(solution)/shard_map/ppermute | solution.py:24
  93.1 4.4 %collective-permute-start.38 = (bf16[128,1152]{1,0:T(8,128)(2,1)S(1)}, bf16[128,1152]{1,0:T(8,128)(2,1)S(1)}, u32[]{:S(2)}, u32[]{:S(2)}) collective-permute-start(bf16[128,1152]{1,0:T(8,128)(2,1)S(1)} %get-tuple-element.187.refs_3_), channel_id=1, source_target_pairs={{0,8},{4,12},{8,0},{12,4},{16,24},{20,28},{24,16},{28,20},{1,9},{5... | collective-permute-start | bytes 884744 | tf_op jit(solution)/shard_map/ppermute | solution.py:29
  100.4 4.1 %collective-permute-done.38.refs_4_ = bf16[128,1152]{1,0:T(8,128)(2,1)S(1)} collective-permute-done((bf16[128,1152]{1,0:T(8,128)(2,1)S(1)}, bf16[128,1152]{1,0:T(8,128)(2,1)S(1)}, u32[]{:S(2)}, u32[]{:S(2)}) %collective-permute-start.38) | collective-permute-done | bytes 294944 | tf_op jit(solution)/shard_map/ppermute | solution.py:29
  105.4 2.9 %collective-permute-start.39 = (bf16[192,1536]{1,0:T(8,128)(2,1)S(1)}, bf16[192,1536]{1,0:T(8,128)(2,1)S(1)}, u32[]{:S(2)}, u32[]{:S(2)}) collective-permute-start(bf16[192,1536]{1,0:T(8,128)(2,1)S(1)} %get-tuple-element.190), channel_id=1, source_target_pairs={{0,4},{4,0},{8,12},{12,8},{16,20},{20,16},{24,28},{28,24},{1,5},{5... | collective-permute-start | bytes 1769480 | tf_op jit(solution)/shard_map/ppermute | solution.py:29
  120.9 5.9 %collective-permute-done.37.refs_4_ = bf16[128,1152]{1,0:T(8,128)(2,1)S(1)} collective-permute-done((bf16[128,1152]{1,0:T(8,128)(2,1)S(1)}, bf16[128,1152]{1,0:T(8,128)(2,1)S(1)}, u32[]{:S(2)}, u32[]{:S(2)}) %collective-permute-start.37) | collective-permute-done | bytes 294944 | tf_op jit(solution)/shard_map/ppermute | solution.py:29
  133.9 5.5 %collective-permute-done.47 = f32[24,768]{1,0:T(8,128)S(1)} collective-permute-done((f32[24,768]{1,0:T(8,128)S(1)}, f32[24,768]{1,0:T(8,128)S(1)}, u32[]{:S(2)}, u32[]{:S(2)}) %collective-permute-start.47) | collective-permute-done | bytes 73760 | tf_op jit(solution)/shard_map/ppermute | solution.py:29
  139.5 2.6 %collective-permute-start.50 = (bf16[192,768]{1,0:T(8,128)(2,1)S(1)}, bf16[192,768]{1,0:T(8,128)(2,1)S(1)}, u32[]{:S(2)}, u32[]{:S(2)}) collective-permute-start(bf16[192,768]{1,0:T(8,128)(2,1)S(1)} %get-tuple-element.214), channel_id=1, source_target_pairs={{0,4},{4,0},{8,12},{12,8},{16,20},{20,16},{24,28},{28,24},{1,5},{5... | collective-permute-start | bytes 884744 | tf_op jit(solution)/shard_map/ppermute | solution.py:29
  144.3 7.5 %collective-permute-done.48 = f32[24,768]{1,0:T(8,128)S(1)} collective-permute-done((f32[24,768]{1,0:T(8,128)S(1)}, f32[24,768]{1,0:T(8,128)S(1)}, u32[]{:S(2)}, u32[]{:S(2)}) %collective-permute-start.48) | collective-permute-done | bytes 73760 | tf_op jit(solution)/shard_map/ppermute | solution.py:29
  156.4 2.6 %collective-permute-start.53 = (bf16[192,768]{1,0:T(8,128)(2,1)S(1)}, bf16[192,768]{1,0:T(8,128)(2,1)S(1)}, u32[]{:S(2)}, u32[]{:S(2)}) collective-permute-start(bf16[192,768]{1,0:T(8,128)(2,1)S(1)} %get-tuple-element.222), channel_id=1, source_target_pairs={{0,4},{4,0},{8,12},{12,8},{16,20},{20,16},{24,28},{28,24},{1,5},{5... | collective-permute-start | bytes 884744 | tf_op jit(solution)/shard_map/ppermute | solution.py:29
  159.0 3.6 %collective-permute-done.54.arrived_ref = bf16[192,1536]{1,0:T(8,128)(2,1)S(1)} collective-permute-done((bf16[192,1536]{1,0:T(8,128)(2,1)S(1)}, bf16[192,1536]{1,0:T(8,128)(2,1)S(1)}, u32[]{:S(2)}, u32[]{:S(2)}) %collective-permute-start.54) | collective-permute-done | bytes 589856 | tf_op jit(solution)/shard_map/ppermute | solution.py:29
  166.6 2.7 %collective-permute-done.56 = f32[24,768]{1,0:T(8,128)S(1)} collective-permute-done((f32[24,768]{1,0:T(8,128)S(1)}, f32[24,768]{1,0:T(8,128)S(1)}, u32[]{:S(2)}, u32[]{:S(2)}) %collective-permute-start.56) | collective-permute-done | bytes 73760 | tf_op jit(solution)/shard_map/ppermute | solution.py:29
  171.5 9.2 %collective-permute-done.58.refs_1_ = bf16[96,1536]{1,0:T(8,128)(2,1)S(1)} collective-permute-done((bf16[96,1536]{1,0:T(8,128)(2,1)S(1)}, bf16[96,1536]{1,0:T(8,128)(2,1)S(1)}, u32[]{:S(2)}, u32[]{:S(2)}) %collective-permute-start.58) | collective-permute-done | bytes 294944 | tf_op jit(solution)/shard_map/ppermute | solution.py:29
  (163 shorter events, 83.5 us)
Async XLA Ops:
  8.9 12.0 %collective-permute-start.5 = (bf16[128,384]{1,0:T(8,128)(2,1)S(1)}, bf16[128,384]{1,0:T(8,128)(2,1)S(1)}, u32[]{:S(2)}, u32[]{:S(2)}) collective-permute-start(bf16[128,384]{1,0:T(8,128)(2,1)S(1)} %get-tuple-element.130.refs_3_), channel_id=1, source_target_pairs={{0,4},{4,8},{8,12},{12,16},{16,20},{20,24},{24,28},{1,5},{5,9},{9,... | collective-permute-start | bytes 294920 | tf_op jit(solution)/shard_map/ppermute | solution.py:24
  37.0 19.0 %collective-permute-start.15 = (bf16[128,1152]{1,0:T(8,128)(2,1)S(1)}, bf16[128,1152]{1,0:T(8,128)(2,1)S(1)}, u32[]{:S(2)}, u32[]{:S(2)}) collective-permute-start(bf16[128,1152]{1,0:T(8,128)(2,1)S(1)} %get-tuple-element.144.refs_0_), channel_id=1, source_target_pairs={{0,8},{4,12},{8,0},{12,4},{16,24},{20,28},{24,16},{28,20},{1,9},{5... | collective-permute-start | bytes 884744 | tf_op jit(solution)/shard_map/ppermute | solution.py:29
  40.4 15.6 %collective-permute-start.14 = (bf16[128,640]{1,0:T(8,128)(2,1)S(1)}, bf16[128,640]{1,0:T(8,128)(2,1)S(1)}, u32[]{:S(2)}, u32[]{:S(2)}) collective-permute-start(bf16[128,640]{1,0:T(8,128)(2,1)S(1)} %get-tuple-element.142.refs_0_), channel_id=1, source_target_pairs={{0,8},{4,12},{8,0},{12,4},{16,24},{20,28},{24,16},{28,20},{1,9},{5... | collective-permute-start | bytes 491528 | tf_op jit(solution)/shard_map/ppermute | solution.py:29
  42.7 13.3 %collective-permute-start.18 = (bf16[128,384]{1,0:T(8,128)(2,1)S(1)}, bf16[128,384]{1,0:T(8,128)(2,1)S(1)}, u32[]{:S(2)}, u32[]{:S(2)}) collective-permute-start(bf16[128,384]{1,0:T(8,128)(2,1)S(1)} %get-tuple-element.146.refs_3_), channel_id=1, source_target_pairs={{0,4},{4,8},{8,12},{12,16},{16,20},{20,24},{24,28},{1,5},{5,9},{9,... | collective-permute-start | bytes 294920 | tf_op jit(solution)/shard_map/ppermute | solution.py:24
  72.7 11.6 %collective-permute-start.27 = (bf16[128,1152]{1,0:T(8,128)(2,1)S(1)}, bf16[128,1152]{1,0:T(8,128)(2,1)S(1)}, u32[]{:S(2)}, u32[]{:S(2)}) collective-permute-start(bf16[128,1152]{1,0:T(8,128)(2,1)S(1)} %get-tuple-element.164.refs_0_), channel_id=1, source_target_pairs={{0,8},{4,12},{8,0},{12,4},{16,24},{20,28},{24,16},{28,20},{1,9},{5... | collective-permute-start | bytes 884744 | tf_op jit(solution)/shard_map/ppermute | solution.py:29
  93.1 11.4 %collective-permute-start.38 = (bf16[128,1152]{1,0:T(8,128)(2,1)S(1)}, bf16[128,1152]{1,0:T(8,128)(2,1)S(1)}, u32[]{:S(2)}, u32[]{:S(2)}) collective-permute-start(bf16[128,1152]{1,0:T(8,128)(2,1)S(1)} %get-tuple-element.187.refs_3_), channel_id=1, source_target_pairs={{0,8},{4,12},{8,0},{12,4},{16,24},{20,28},{24,16},{28,20},{1,9},{5... | collective-permute-start | bytes 884744 | tf_op jit(solution)/shard_map/ppermute | solution.py:29
  105.4 22.1 %collective-permute-start.39 = (bf16[192,1536]{1,0:T(8,128)(2,1)S(1)}, bf16[192,1536]{1,0:T(8,128)(2,1)S(1)}, u32[]{:S(2)}, u32[]{:S(2)}) collective-permute-start(bf16[192,1536]{1,0:T(8,128)(2,1)S(1)} %get-tuple-element.190), channel_id=1, source_target_pairs={{0,4},{4,0},{8,12},{12,8},{16,20},{20,16},{24,28},{28,24},{1,5},{5... | collective-permute-start | bytes 1769480 | tf_op jit(solution)/shard_map/ppermute | solution.py:29
  109.8 9.2 %collective-permute-start.40 = (bf16[128,1024]{1,0:T(8,128)(2,1)S(1)}, bf16[128,1024]{1,0:T(8,128)(2,1)S(1)}, u32[]{:S(2)}, u32[]{:S(2)}) collective-permute-start(bf16[128,1024]{1,0:T(8,128)(2,1)S(1)} %get-tuple-element.193.refs_3_), channel_id=1, source_target_pairs={{0,8},{4,12},{8,0},{12,4},{16,24},{20,28},{24,16},{28,20},{1,9},{5... | collective-permute-start | bytes 786440 | tf_op jit(solution)/shard_map/ppermute | solution.py:29
  111.6 15.3 %collective-permute-start.37 = (bf16[128,1152]{1,0:T(8,128)(2,1)S(1)}, bf16[128,1152]{1,0:T(8,128)(2,1)S(1)}, u32[]{:S(2)}, u32[]{:S(2)}) collective-permute-start(bf16[128,1152]{1,0:T(8,128)(2,1)S(1)} %get-tuple-element.182.refs_3_), channel_id=1, source_target_pairs={{0,8},{4,12},{8,0},{12,4},{16,24},{20,28},{24,16},{28,20},{1,9},{5... | collective-permute-start | bytes 884744 | tf_op jit(solution)/shard_map/ppermute | solution.py:29
  116.3 11.4 %collective-permute-start.41 = (bf16[128,384]{1,0:T(8,128)(2,1)S(1)}, bf16[128,384]{1,0:T(8,128)(2,1)S(1)}, u32[]{:S(2)}, u32[]{:S(2)}) collective-permute-start(bf16[128,384]{1,0:T(8,128)(2,1)S(1)} %get-tuple-element.196), channel_id=1, source_target_pairs={{12,0},{16,4},{20,8},{24,12},{28,16},{13,1},{17,5},{21,9},{25,13},... | collective-permute-start | bytes 294920 | tf_op jit(solution)/shard_map/ppermute | solution.py:24
  117.6 10.7 %collective-permute-start.42 = (bf16[128,384]{1,0:T(8,128)(2,1)S(1)}, bf16[128,384]{1,0:T(8,128)(2,1)S(1)}, u32[]{:S(2)}, u32[]{:S(2)}) collective-permute-start(bf16[128,384]{1,0:T(8,128)(2,1)S(1)} %get-tuple-element.197), channel_id=1, source_target_pairs={{8,0},{12,4},{16,8},{20,12},{24,16},{28,20},{9,1},{13,5},{17,9},{2... | collective-permute-start | bytes 294920 | tf_op jit(solution)/shard_map/ppermute | solution.py:24
  119.1 9.3 %collective-permute-start.43 = (bf16[128,384]{1,0:T(8,128)(2,1)S(1)}, bf16[128,384]{1,0:T(8,128)(2,1)S(1)}, u32[]{:S(2)}, u32[]{:S(2)}) collective-permute-start(bf16[128,384]{1,0:T(8,128)(2,1)S(1)} %get-tuple-element.198), channel_id=1, source_target_pairs={{4,0},{8,4},{12,8},{16,12},{20,16},{24,20},{28,24},{5,1},{9,5},{13... | collective-permute-start | bytes 294920 | tf_op jit(solution)/shard_map/ppermute | solution.py:24
  130.6 8.8 %collective-permute-start.46 = (bf16[128,768]{1,0:T(8,128)(2,1)S(1)}, bf16[128,768]{1,0:T(8,128)(2,1)S(1)}, u32[]{:S(2)}, u32[]{:S(2)}) collective-permute-start(bf16[128,768]{1,0:T(8,128)(2,1)S(1)} %convert_add_fusion.1), channel_id=1, source_target_pairs={{0,2},{1,3},{2,0},{3,1},{4,6},{5,7},{6,4},{7,5},{8,10},{9,11},{10,... | collective-permute-start | bytes 589832 | tf_op jit(solution)/shard_map/ppermute | solution.py:29
  130.8 8.6 %collective-permute-start.47 = (f32[24,768]{1,0:T(8,128)S(1)}, f32[24,768]{1,0:T(8,128)S(1)}, u32[]{:S(2)}, u32[]{:S(2)}) collective-permute-start(f32[24,768]{1,0:T(8,128)S(1)} %add.67), channel_id=1, source_target_pairs={{0,2},{1,3},{2,0},{3,1},{4,6},{5,7},{6,4},{7,5},{8,10},{9,11},{10,... | collective-permute-start | bytes 221192 | tf_op jit(solution)/shard_map/ppermute | solution.py:29
  132.7 19.2 %collective-permute-start.49 = (bf16[96,1536]{1,0:T(8,128)(2,1)S(1)}, bf16[96,1536]{1,0:T(8,128)(2,1)S(1)}, u32[]{:S(2)}, u32[]{:S(2)}) collective-permute-start(bf16[96,1536]{1,0:T(8,128)(2,1)S(1)} %get-tuple-element.191), channel_id=1, source_target_pairs={{0,16},{4,20},{8,24},{12,28},{16,0},{20,4},{24,8},{28,12},{1,17},{... | collective-permute-start | bytes 884744 | tf_op jit(solution)/shard_map/ppermute | solution.py:29
  139.5 12.4 %collective-permute-start.50 = (bf16[192,768]{1,0:T(8,128)(2,1)S(1)}, bf16[192,768]{1,0:T(8,128)(2,1)S(1)}, u32[]{:S(2)}, u32[]{:S(2)}) collective-permute-start(bf16[192,768]{1,0:T(8,128)(2,1)S(1)} %get-tuple-element.214), channel_id=1, source_target_pairs={{0,4},{4,0},{8,12},{12,8},{16,20},{20,16},{24,28},{28,24},{1,5},{5... | collective-permute-start | bytes 884744 | tf_op jit(solution)/shard_map/ppermute | solution.py:29
  142.1 20.5 %collective-permute-start.54 = (bf16[192,1536]{1,0:T(8,128)(2,1)S(1)}, bf16[192,1536]{1,0:T(8,128)(2,1)S(1)}, u32[]{:S(2)}, u32[]{:S(2)}) collective-permute-start(bf16[192,1536]{1,0:T(8,128)(2,1)S(1)} %get-tuple-element.184), channel_id=1, source_target_pairs={{0,4},{4,0},{8,12},{12,8},{16,20},{20,16},{24,28},{28,24},{1,5},{5... | collective-permute-start | bytes 1769480 | tf_op jit(solution)/shard_map/ppermute | solution.py:29
  142.1 9.7 %collective-permute-start.48 = (f32[24,768]{1,0:T(8,128)S(1)}, f32[24,768]{1,0:T(8,128)S(1)}, u32[]{:S(2)}, u32[]{:S(2)}) collective-permute-start(f32[24,768]{1,0:T(8,128)S(1)} %add.69), channel_id=1, source_target_pairs={{0,16},{4,20},{8,24},{12,28},{16,0},{20,4},{24,8},{28,12},{1,17},{... | collective-permute-start | bytes 221192 | tf_op jit(solution)/shard_map/ppermute | solution.py:29
  143.8 12.0 %collective-permute-start.52 = (bf16[128,1024]{1,0:T(8,128)(2,1)S(1)}, bf16[128,1024]{1,0:T(8,128)(2,1)S(1)}, u32[]{:S(2)}, u32[]{:S(2)}) collective-permute-start(bf16[128,1024]{1,0:T(8,128)(2,1)S(1)} %get-tuple-element.219.refs_3_), channel_id=1, source_target_pairs={{0,8},{4,12},{8,0},{12,4},{16,24},{20,28},{24,16},{28,20},{1,9},{5... | collective-permute-start | bytes 786440 | tf_op jit(solution)/shard_map/ppermute | solution.py:29
  152.1 10.5 %collective-permute-start.55 = (bf16[96,768]{1,0:T(8,128)(2,1)S(1)}, bf16[96,768]{1,0:T(8,128)(2,1)S(1)}, u32[]{:S(2)}, u32[]{:S(2)}) collective-permute-start(bf16[96,768]{1,0:T(8,128)(2,1)S(1)} %get-tuple-element.225), channel_id=1, source_target_pairs={{0,16},{4,20},{8,24},{12,28},{16,0},{20,4},{24,8},{28,12},{1,17},{... | collective-permute-start | bytes 442376 | tf_op jit(solution)/shard_map/ppermute | solution.py:29
  156.4 13.0 %collective-permute-start.53 = (bf16[192,768]{1,0:T(8,128)(2,1)S(1)}, bf16[192,768]{1,0:T(8,128)(2,1)S(1)}, u32[]{:S(2)}, u32[]{:S(2)}) collective-permute-start(bf16[192,768]{1,0:T(8,128)(2,1)S(1)} %get-tuple-element.222), channel_id=1, source_target_pairs={{0,4},{4,0},{8,12},{12,8},{16,20},{20,16},{24,28},{28,24},{1,5},{5... | collective-permute-start | bytes 884744 | tf_op jit(solution)/shard_map/ppermute | solution.py:29
  162.8 17.9 %collective-permute-start.58 = (bf16[96,1536]{1,0:T(8,128)(2,1)S(1)}, bf16[96,1536]{1,0:T(8,128)(2,1)S(1)}, u32[]{:S(2)}, u32[]{:S(2)}) collective-permute-start(bf16[96,1536]{1,0:T(8,128)(2,1)S(1)} %get-tuple-element.227), channel_id=1, source_target_pairs={{0,16},{4,20},{8,24},{12,28},{16,0},{20,4},{24,8},{28,12},{1,17},{... | collective-permute-start | bytes 884744 | tf_op jit(solution)/shard_map/ppermute | solution.py:29
  169.5 14.3 %collective-permute-start.57 = (bf16[96,768]{1,0:T(8,128)(2,1)S(1)}, bf16[96,768]{1,0:T(8,128)(2,1)S(1)}, u32[]{:S(2)}, u32[]{:S(2)}) collective-permute-start(bf16[96,768]{1,0:T(8,128)(2,1)S(1)} %get-tuple-element.231), channel_id=1, source_target_pairs={{0,16},{4,20},{8,24},{12,28},{16,0},{20,4},{24,8},{28,12},{1,17},{... | collective-permute-start | bytes 442376 | tf_op jit(solution)/shard_map/ppermute | solution.py:29
  171.2 10.7 %collective-permute-start.59 = (f32[24,768]{1,0:T(8,128)S(1)}, f32[24,768]{1,0:T(8,128)S(1)}, u32[]{:S(2)}, u32[]{:S(2)}) collective-permute-start(f32[24,768]{1,0:T(8,128)S(1)} %add.71.total_ref), channel_id=1, source_target_pairs={{0,8},{4,12},{8,0},{12,4},{16,24},{20,28},{24,16},{28,20},{1,9},{5... | collective-permute-start | bytes 221192 | tf_op jit(solution)/shard_map/ppermute | solution.py:29
  (47 other events, 247.7 us)

commit v7 on v6

--- a/solution.py
+++ b/solution.py
@@ -815,7 +815,7 @@
         gmid, picked, dq, dkv, att_small[layer], *away = attend_grad(
             grad, pair, mid, q, kv_parts, mask, att, lse, layer, params
         )
-        arrived = [shifted(away[by - 1], "dp", -by) for by in range(SPAN - 1, 0, -1)]
+        arrived = [shifted(away[by - 1], "dp", -by) for by in (SPAN - 1, *range(1, SPAN - 1))]
         due = []
         if last:
             due.append(rows_b[layer][1])

time: 185 us -> 185 us (level)
  waiting for transfers between devices: 86.5 us -> 90.9 us
  starting transfers between devices: 73.2 us -> 68.9 us
    ppermute x12, waiting for transfers between devices: 11.5 us -> 19.2 us  [shifted(): return lax.ppermute(array, axis, pairs)]
    ppermute x48, starting transfers between devices: 40.1 us -> 35.9 us  [swapped(): return lax.ppermute(array, axis, [(i, i ^ bit) for i in range(length)])]
    ppermute x48, waiting for transfers between devices: 75 us -> 71.7 us  [swapped(): return lax.ppermute(array, axis, [(i, i ^ bit) for i in range(length)])]
  transfers between devices with their start and end apart: 60 -> 60, of which waited for: 37 -> 39; matrix products, arithmetic and copies ran while one was open for 0% -> 0% of each run, Pallas kernels for 8% -> 8%
where the time goes in v7:
time: 185 us
  waiting for transfers between devices  90.9 us (49%)
  starting transfers between devices  68.9 us (37%)
  Pallas kernels  21.6 us (12%)
    ppermute x48, waiting for transfers between devices, swapped(): return lax.ppermute(array, axis, [(i, i ^ bit) for i in range(length)])  71.7 us
    ppermute x48, starting transfers between devices, swapped(): return lax.ppermute(array, axis, [(i, i ^ bit) for i in range(length)])  35.9 us
    ppermute x12, starting transfers between devices, shifted(): return lax.ppermute(array, axis, pairs)  33 us
    pallas_call x26, Pallas kernels, call(): pl.pallas_call(kernel, out_shape=shapes, in_specs=[spec] * len(args), out...  21 us
    ppermute x12, waiting for transfers between devices, shifted(): return lax.ppermute(array, axis, pairs)  19.2 us
  transfers between devices with their start and end apart: 60, of which 39 were waited for; matrix products, arithmetic and copies ran while one was open for 0% of the time, Pallas kernels for 8%

profile of v7, /device:TPU:0, one launch (start us, length us, event | category | flops | bytes accessed | tf_op | source)
XLA Modules:
  0.0 185.0 jit_solution(8821056553620054434)
XLA Ops:
  0.6 3.0 %collective-permute-start.1 = (bf16[32,768]{1,0:T(8,128)(2,1)}, bf16[32,768]{1,0:T(8,128)(2,1)S(1)}, u32[]{:S(2)}, u32[]{:S(2)}) collective-permute-start(bf16[32,768]{1,0:T(8,128)(2,1)} %refs_3_.2), channel_id=1, source_target_pairs={{0,2},{1,3},{2,0},{3,1},{4,6},{5,7},{6,4},{7,5},{8,10},{9,11},{10,... | collective-permute-start | bytes 147464 | tf_op jit(solution)/shard_map/ppermute | solution.py:29
  3.7 2.3 %collective-permute-done.1.refs_1_ = bf16[32,768]{1,0:T(8,128)(2,1)S(1)} collective-permute-done((bf16[32,768]{1,0:T(8,128)(2,1)}, bf16[32,768]{1,0:T(8,128)(2,1)S(1)}, u32[]{:S(2)}, u32[]{:S(2)}) %collective-permute-start.1) | collective-permute-done | bytes 49184 | tf_op jit(solution)/shard_map/ppermute | solution.py:29
  8.9 4.1 %collective-permute-start.5 = (bf16[128,384]{1,0:T(8,128)(2,1)S(1)}, bf16[128,384]{1,0:T(8,128)(2,1)S(1)}, u32[]{:S(2)}, u32[]{:S(2)}) collective-permute-start(bf16[128,384]{1,0:T(8,128)(2,1)S(1)} %get-tuple-element.130.refs_3_), channel_id=1, source_target_pairs={{0,4},{4,8},{8,12},{12,16},{16,20},{20,24},{24,28},{1,5},{5,9},{9,... | collective-permute-start | bytes 294920 | tf_op jit(solution)/shard_map/ppermute | solution.py:24
  13.0 3.5 %collective-permute-start.4 = (bf16[128,384]{1,0:T(8,128)(2,1)S(1)}, bf16[128,384]{1,0:T(8,128)(2,1)S(1)}, u32[]{:S(2)}, u32[]{:S(2)}) collective-permute-start(bf16[128,384]{1,0:T(8,128)(2,1)S(1)} %get-tuple-element.130.refs_3_), channel_id=1, source_target_pairs={{0,8},{4,12},{8,16},{12,20},{16,24},{20,28},{1,9},{5,13},{9,17},{1... | collective-permute-start | bytes 294920 | tf_op jit(solution)/shard_map/ppermute | solution.py:24
  16.5 4.4 %collective-permute-start.3 = (bf16[128,384]{1,0:T(8,128)(2,1)S(1)}, bf16[128,384]{1,0:T(8,128)(2,1)S(1)}, u32[]{:S(2)}, u32[]{:S(2)}) collective-permute-start(bf16[128,384]{1,0:T(8,128)(2,1)S(1)} %get-tuple-element.130.refs_3_), channel_id=1, source_target_pairs={{0,12},{4,16},{8,20},{12,24},{16,28},{1,13},{5,17},{9,21},{13,25},... | collective-permute-start | bytes 294920 | tf_op jit(solution)/shard_map/ppermute | solution.py:24
  27.7 3.4 %collective-permute-done.7 = bf16[64,768]{1,0:T(8,128)(2,1)S(1)} collective-permute-done((bf16[64,768]{1,0:T(8,128)(2,1)S(1)}, bf16[64,768]{1,0:T(8,128)(2,1)S(1)}, u32[]{:S(2)}, u32[]{:S(2)}) %collective-permute-start.7) | collective-permute-done | bytes 98336 | tf_op jit(solution)/shard_map/ppermute | solution.py:29
  37.2 3.1 %collective-permute-done.10 = bf16[64,768]{1,0:T(8,128)(2,1)S(1)} collective-permute-done((bf16[64,768]{1,0:T(8,128)(2,1)S(1)}, bf16[64,768]{1,0:T(8,128)(2,1)S(1)}, u32[]{:S(2)}, u32[]{:S(2)}) %collective-permute-start.10) | collective-permute-done | bytes 98336 | tf_op jit(solution)/shard_map/ppermute | solution.py:29
  42.7 5.5 %collective-permute-start.18 = (bf16[128,384]{1,0:T(8,128)(2,1)S(1)}, bf16[128,384]{1,0:T(8,128)(2,1)S(1)}, u32[]{:S(2)}, u32[]{:S(2)}) collective-permute-start(bf16[128,384]{1,0:T(8,128)(2,1)S(1)} %get-tuple-element.146.refs_3_), channel_id=1, source_target_pairs={{0,4},{4,8},{8,12},{12,16},{16,20},{20,24},{24,28},{1,5},{5,9},{9,... | collective-permute-start | bytes 294920 | tf_op jit(solution)/shard_map/ppermute | solution.py:24
  48.2 2.3 %collective-permute-start.17 = (bf16[128,384]{1,0:T(8,128)(2,1)S(1)}, bf16[128,384]{1,0:T(8,128)(2,1)S(1)}, u32[]{:S(2)}, u32[]{:S(2)}) collective-permute-start(bf16[128,384]{1,0:T(8,128)(2,1)S(1)} %get-tuple-element.146.refs_3_), channel_id=1, source_target_pairs={{0,8},{4,12},{8,16},{12,20},{16,24},{20,28},{1,9},{5,13},{9,17},{1... | collective-permute-start | bytes 294920 | tf_op jit(solution)/shard_map/ppermute | solution.py:24
  50.4 5.5 %collective-permute-start.16 = (bf16[128,384]{1,0:T(8,128)(2,1)S(1)}, bf16[128,384]{1,0:T(8,128)(2,1)S(1)}, u32[]{:S(2)}, u32[]{:S(2)}) collective-permute-start(bf16[128,384]{1,0:T(8,128)(2,1)S(1)} %get-tuple-element.146.refs_3_), channel_id=1, source_target_pairs={{0,12},{4,16},{8,20},{12,24},{16,28},{1,13},{5,17},{9,21},{13,25},... | collective-permute-start | bytes 294920 | tf_op jit(solution)/shard_map/ppermute | solution.py:24
  62.8 3.4 %collective-permute-done.20 = bf16[64,768]{1,0:T(8,128)(2,1)S(1)} collective-permute-done((bf16[64,768]{1,0:T(8,128)(2,1)S(1)}, bf16[64,768]{1,0:T(8,128)(2,1)S(1)}, u32[]{:S(2)}, u32[]{:S(2)}) %collective-permute-start.20) | collective-permute-done | bytes 98336 | tf_op jit(solution)/shard_map/ppermute | solution.py:29
  73.0 4.0 %collective-permute-done.25 = bf16[64,768]{1,0:T(8,128)(2,1)S(1)} collective-permute-done((bf16[64,768]{1,0:T(8,128)(2,1)S(1)}, bf16[64,768]{1,0:T(8,128)(2,1)S(1)}, u32[]{:S(2)}, u32[]{:S(2)}) %collective-permute-start.25) | collective-permute-done | bytes 98336 | tf_op jit(solution)/shard_map/ppermute | solution.py:29
  84.3 4.5 %collective-permute-done.28.refs_0_ = bf16[128,384]{1,0:T(8,128)(2,1)S(1)} collective-permute-done((bf16[128,384]{1,0:T(8,128)(2,1)S(1)}, bf16[128,384]{1,0:T(8,128)(2,1)S(1)}, u32[]{:S(2)}, u32[]{:S(2)}) %collective-permute-start.28) | collective-permute-done | bytes 98336 | tf_op jit(solution)/shard_map/ppermute | solution.py:24
  90.8 3.0 %collective-permute-done.30.refs_2_ = bf16[128,384]{1,0:T(8,128)(2,1)S(1)} collective-permute-done((bf16[128,384]{1,0:T(8,128)(2,1)S(1)}, bf16[128,384]{1,0:T(8,128)(2,1)S(1)}, u32[]{:S(2)}, u32[]{:S(2)}) %collective-permute-start.30) | collective-permute-done | bytes 98336 | tf_op jit(solution)/shard_map/ppermute | solution.py:24
  96.1 2.7 %collective-permute-start.38 = (bf16[128,1152]{1,0:T(8,128)(2,1)S(1)}, bf16[128,1152]{1,0:T(8,128)(2,1)S(1)}, u32[]{:S(2)}, u32[]{:S(2)}) collective-permute-start(bf16[128,1152]{1,0:T(8,128)(2,1)S(1)} %get-tuple-element.187.refs_3_), channel_id=1, source_target_pairs={{0,8},{4,12},{8,0},{12,4},{16,24},{20,28},{24,16},{28,20},{1,9},{5... | collective-permute-start | bytes 884744 | tf_op jit(solution)/shard_map/ppermute | solution.py:29
  103.3 2.5 %collective-permute-done.38.refs_4_ = bf16[128,1152]{1,0:T(8,128)(2,1)S(1)} collective-permute-done((bf16[128,1152]{1,0:T(8,128)(2,1)S(1)}, bf16[128,1152]{1,0:T(8,128)(2,1)S(1)}, u32[]{:S(2)}, u32[]{:S(2)}) %collective-permute-start.38) | collective-permute-done | bytes 294944 | tf_op jit(solution)/shard_map/ppermute | solution.py:29
  119.6 2.4 %collective-permute-done.37.refs_4_ = bf16[128,1152]{1,0:T(8,128)(2,1)S(1)} collective-permute-done((bf16[128,1152]{1,0:T(8,128)(2,1)S(1)}, bf16[128,1152]{1,0:T(8,128)(2,1)S(1)}, u32[]{:S(2)}, u32[]{:S(2)}) %collective-permute-start.37) | collective-permute-done | bytes 294944 | tf_op jit(solution)/shard_map/ppermute | solution.py:29
  122.8 2.7 %collective-permute-done.41.refs_0_ = bf16[128,384]{1,0:T(8,128)(2,1)S(1)} collective-permute-done((bf16[128,384]{1,0:T(8,128)(2,1)S(1)}, bf16[128,384]{1,0:T(8,128)(2,1)S(1)}, u32[]{:S(2)}, u32[]{:S(2)}) %collective-permute-start.41) | collective-permute-done | bytes 98336 | tf_op jit(solution)/shard_map/ppermute | solution.py:24
  125.5 2.7 %collective-permute-done.43.refs_2_ = bf16[128,384]{1,0:T(8,128)(2,1)S(1)} collective-permute-done((bf16[128,384]{1,0:T(8,128)(2,1)S(1)}, bf16[128,384]{1,0:T(8,128)(2,1)S(1)}, u32[]{:S(2)}, u32[]{:S(2)}) %collective-permute-start.43) | collective-permute-done | bytes 98336 | tf_op jit(solution)/shard_map/ppermute | solution.py:24
  134.5 4.8 %collective-permute-done.47 = f32[24,768]{1,0:T(8,128)S(1)} collective-permute-done((f32[24,768]{1,0:T(8,128)S(1)}, f32[24,768]{1,0:T(8,128)S(1)}, u32[]{:S(2)}, u32[]{:S(2)}) %collective-permute-start.47) | collective-permute-done | bytes 73760 | tf_op jit(solution)/shard_map/ppermute | solution.py:29
  144.0 7.7 %collective-permute-done.48 = f32[24,768]{1,0:T(8,128)S(1)} collective-permute-done((f32[24,768]{1,0:T(8,128)S(1)}, f32[24,768]{1,0:T(8,128)S(1)}, u32[]{:S(2)}, u32[]{:S(2)}) %collective-permute-start.48) | collective-permute-done | bytes 73760 | tf_op jit(solution)/shard_map/ppermute | solution.py:29
  157.0 5.0 %collective-permute-done.54.arrived_ref = bf16[192,1536]{1,0:T(8,128)(2,1)S(1)} collective-permute-done((bf16[192,1536]{1,0:T(8,128)(2,1)S(1)}, bf16[192,1536]{1,0:T(8,128)(2,1)S(1)}, u32[]{:S(2)}, u32[]{:S(2)}) %collective-permute-start.54) | collective-permute-done | bytes 589856 | tf_op jit(solution)/shard_map/ppermute | solution.py:29
  165.6 2.9 %collective-permute-done.56 = f32[24,768]{1,0:T(8,128)S(1)} collective-permute-done((f32[24,768]{1,0:T(8,128)S(1)}, f32[24,768]{1,0:T(8,128)S(1)}, u32[]{:S(2)}, u32[]{:S(2)}) %collective-permute-start.56) | collective-permute-done | bytes 73760 | tf_op jit(solution)/shard_map/ppermute | solution.py:29
  172.4 8.5 %collective-permute-done.58.refs_1_ = bf16[96,1536]{1,0:T(8,128)(2,1)S(1)} collective-permute-done((bf16[96,1536]{1,0:T(8,128)(2,1)S(1)}, bf16[96,1536]{1,0:T(8,128)(2,1)S(1)}, u32[]{:S(2)}, u32[]{:S(2)}) %collective-permute-start.58) | collective-permute-done | bytes 294944 | tf_op jit(solution)/shard_map/ppermute | solution.py:29
  (163 shorter events, 90.0 us)
Async XLA Ops:
  8.9 12.0 %collective-permute-start.5 = (bf16[128,384]{1,0:T(8,128)(2,1)S(1)}, bf16[128,384]{1,0:T(8,128)(2,1)S(1)}, u32[]{:S(2)}, u32[]{:S(2)}) collective-permute-start(bf16[128,384]{1,0:T(8,128)(2,1)S(1)} %get-tuple-element.130.refs_3_), channel_id=1, source_target_pairs={{0,4},{4,8},{8,12},{12,16},{16,20},{20,24},{24,28},{1,5},{5,9},{9,... | collective-permute-start | bytes 294920 | tf_op jit(solution)/shard_map/ppermute | solution.py:24
  37.0 19.0 %collective-permute-start.15 = (bf16[128,1152]{1,0:T(8,128)(2,1)S(1)}, bf16[128,1152]{1,0:T(8,128)(2,1)S(1)}, u32[]{:S(2)}, u32[]{:S(2)}) collective-permute-start(bf16[128,1152]{1,0:T(8,128)(2,1)S(1)} %get-tuple-element.144.refs_0_), channel_id=1, source_target_pairs={{0,8},{4,12},{8,0},{12,4},{16,24},{20,28},{24,16},{28,20},{1,9},{5... | collective-permute-start | bytes 884744 | tf_op jit(solution)/shard_map/ppermute | solution.py:29
  40.4 15.6 %collective-permute-start.14 = (bf16[128,640]{1,0:T(8,128)(2,1)S(1)}, bf16[128,640]{1,0:T(8,128)(2,1)S(1)}, u32[]{:S(2)}, u32[]{:S(2)}) collective-permute-start(bf16[128,640]{1,0:T(8,128)(2,1)S(1)} %get-tuple-element.142.refs_0_), channel_id=1, source_target_pairs={{0,8},{4,12},{8,0},{12,4},{16,24},{20,28},{24,16},{28,20},{1,9},{5... | collective-permute-start | bytes 491528 | tf_op jit(solution)/shard_map/ppermute | solution.py:29
  42.7 13.3 %collective-permute-start.18 = (bf16[128,384]{1,0:T(8,128)(2,1)S(1)}, bf16[128,384]{1,0:T(8,128)(2,1)S(1)}, u32[]{:S(2)}, u32[]{:S(2)}) collective-permute-start(bf16[128,384]{1,0:T(8,128)(2,1)S(1)} %get-tuple-element.146.refs_3_), channel_id=1, source_target_pairs={{0,4},{4,8},{8,12},{12,16},{16,20},{20,24},{24,28},{1,5},{5,9},{9,... | collective-permute-start | bytes 294920 | tf_op jit(solution)/shard_map/ppermute | solution.py:24
  72.7 11.6 %collective-permute-start.27 = (bf16[128,1152]{1,0:T(8,128)(2,1)S(1)}, bf16[128,1152]{1,0:T(8,128)(2,1)S(1)}, u32[]{:S(2)}, u32[]{:S(2)}) collective-permute-start(bf16[128,1152]{1,0:T(8,128)(2,1)S(1)} %get-tuple-element.164.refs_0_), channel_id=1, source_target_pairs={{0,8},{4,12},{8,0},{12,4},{16,24},{20,28},{24,16},{28,20},{1,9},{5... | collective-permute-start | bytes 884744 | tf_op jit(solution)/shard_map/ppermute | solution.py:29
  81.7 9.1 %collective-permute-start.29 = (bf16[128,384]{1,0:T(8,128)(2,1)S(1)}, bf16[128,384]{1,0:T(8,128)(2,1)S(1)}, u32[]{:S(2)}, u32[]{:S(2)}) collective-permute-start(bf16[128,384]{1,0:T(8,128)(2,1)S(1)} %get-tuple-element.167), channel_id=1, source_target_pairs={{4,0},{8,4},{12,8},{16,12},{20,16},{24,20},{28,24},{5,1},{9,5},{13... | collective-permute-start | bytes 294920 | tf_op jit(solution)/shard_map/ppermute | solution.py:24
  83.0 10.8 %collective-permute-start.30 = (bf16[128,384]{1,0:T(8,128)(2,1)S(1)}, bf16[128,384]{1,0:T(8,128)(2,1)S(1)}, u32[]{:S(2)}, u32[]{:S(2)}) collective-permute-start(bf16[128,384]{1,0:T(8,128)(2,1)S(1)} %get-tuple-element.168), channel_id=1, source_target_pairs={{8,0},{12,4},{16,8},{20,12},{24,16},{28,20},{9,1},{13,5},{17,9},{2... | collective-permute-start | bytes 294920 | tf_op jit(solution)/shard_map/ppermute | solution.py:24
  96.1 9.7 %collective-permute-start.38 = (bf16[128,1152]{1,0:T(8,128)(2,1)S(1)}, bf16[128,1152]{1,0:T(8,128)(2,1)S(1)}, u32[]{:S(2)}, u32[]{:S(2)}) collective-permute-start(bf16[128,1152]{1,0:T(8,128)(2,1)S(1)} %get-tuple-element.187.refs_3_), channel_id=1, source_target_pairs={{0,8},{4,12},{8,0},{12,4},{16,24},{20,28},{24,16},{28,20},{1,9},{5... | collective-permute-start | bytes 884744 | tf_op jit(solution)/shard_map/ppermute | solution.py:29
  106.7 15.9 %collective-permute-start.39 = (bf16[192,1536]{1,0:T(8,128)(2,1)S(1)}, bf16[192,1536]{1,0:T(8,128)(2,1)S(1)}, u32[]{:S(2)}, u32[]{:S(2)}) collective-permute-start(bf16[192,1536]{1,0:T(8,128)(2,1)S(1)} %get-tuple-element.190), channel_id=1, source_target_pairs={{0,4},{4,0},{8,12},{12,8},{16,20},{20,16},{24,28},{28,24},{1,5},{5... | collective-permute-start | bytes 1769480 | tf_op jit(solution)/shard_map/ppermute | solution.py:29
  108.5 9.2 %collective-permute-start.40 = (bf16[128,1024]{1,0:T(8,128)(2,1)S(1)}, bf16[128,1024]{1,0:T(8,128)(2,1)S(1)}, u32[]{:S(2)}, u32[]{:S(2)}) collective-permute-start(bf16[128,1024]{1,0:T(8,128)(2,1)S(1)} %get-tuple-element.193.refs_3_), channel_id=1, source_target_pairs={{0,8},{4,12},{8,0},{12,4},{16,24},{20,28},{24,16},{28,20},{1,9},{5... | collective-permute-start | bytes 786440 | tf_op jit(solution)/shard_map/ppermute | solution.py:29
  110.2 11.7 %collective-permute-start.37 = (bf16[128,1152]{1,0:T(8,128)(2,1)S(1)}, bf16[128,1152]{1,0:T(8,128)(2,1)S(1)}, u32[]{:S(2)}, u32[]{:S(2)}) collective-permute-start(bf16[128,1152]{1,0:T(8,128)(2,1)S(1)} %get-tuple-element.182.refs_3_), channel_id=1, source_target_pairs={{0,8},{4,12},{8,0},{12,4},{16,24},{20,28},{24,16},{28,20},{1,9},{5... | collective-permute-start | bytes 884744 | tf_op jit(solution)/shard_map/ppermute | solution.py:29
  115.0 10.5 %collective-permute-start.41 = (bf16[128,384]{1,0:T(8,128)(2,1)S(1)}, bf16[128,384]{1,0:T(8,128)(2,1)S(1)}, u32[]{:S(2)}, u32[]{:S(2)}) collective-permute-start(bf16[128,384]{1,0:T(8,128)(2,1)S(1)} %get-tuple-element.196), channel_id=1, source_target_pairs={{12,0},{16,4},{20,8},{24,12},{28,16},{13,1},{17,5},{21,9},{25,13},... | collective-permute-start | bytes 294920 | tf_op jit(solution)/shard_map/ppermute | solution.py:24
  116.3 9.2 %collective-permute-start.42 = (bf16[128,384]{1,0:T(8,128)(2,1)S(1)}, bf16[128,384]{1,0:T(8,128)(2,1)S(1)}, u32[]{:S(2)}, u32[]{:S(2)}) collective-permute-start(bf16[128,384]{1,0:T(8,128)(2,1)S(1)} %get-tuple-element.197), channel_id=1, source_target_pairs={{4,0},{8,4},{12,8},{16,12},{20,16},{24,20},{28,24},{5,1},{9,5},{13... | collective-permute-start | bytes 294920 | tf_op jit(solution)/shard_map/ppermute | solution.py:24
  117.7 10.5 %collective-permute-start.43 = (bf16[128,384]{1,0:T(8,128)(2,1)S(1)}, bf16[128,384]{1,0:T(8,128)(2,1)S(1)}, u32[]{:S(2)}, u32[]{:S(2)}) collective-permute-start(bf16[128,384]{1,0:T(8,128)(2,1)S(1)} %get-tuple-element.198), channel_id=1, source_target_pairs={{8,0},{12,4},{16,8},{20,12},{24,16},{28,20},{9,1},{13,5},{17,9},{2... | collective-permute-start | bytes 294920 | tf_op jit(solution)/shard_map/ppermute | solution.py:24
  132.5 19.2 %collective-permute-start.49 = (bf16[96,1536]{1,0:T(8,128)(2,1)S(1)}, bf16[96,1536]{1,0:T(8,128)(2,1)S(1)}, u32[]{:S(2)}, u32[]{:S(2)}) collective-permute-start(bf16[96,1536]{1,0:T(8,128)(2,1)S(1)} %get-tuple-element.191), channel_id=1, source_target_pairs={{0,16},{4,20},{8,24},{12,28},{16,0},{20,4},{24,8},{28,12},{1,17},{... | collective-permute-start | bytes 884744 | tf_op jit(solution)/shard_map/ppermute | solution.py:29
  139.3 12.4 %collective-permute-start.50 = (bf16[192,768]{1,0:T(8,128)(2,1)S(1)}, bf16[192,768]{1,0:T(8,128)(2,1)S(1)}, u32[]{:S(2)}, u32[]{:S(2)}) collective-permute-start(bf16[192,768]{1,0:T(8,128)(2,1)S(1)} %get-tuple-element.214), channel_id=1, source_target_pairs={{0,4},{4,0},{8,12},{12,8},{16,20},{20,16},{24,28},{28,24},{1,5},{5... | collective-permute-start | bytes 884744 | tf_op jit(solution)/shard_map/ppermute | solution.py:29
  139.4 22.6 %collective-permute-start.54 = (bf16[192,1536]{1,0:T(8,128)(2,1)S(1)}, bf16[192,1536]{1,0:T(8,128)(2,1)S(1)}, u32[]{:S(2)}, u32[]{:S(2)}) collective-permute-start(bf16[192,1536]{1,0:T(8,128)(2,1)S(1)} %get-tuple-element.184), channel_id=1, source_target_pairs={{0,4},{4,0},{8,12},{12,8},{16,20},{20,16},{24,28},{28,24},{1,5},{5... | collective-permute-start | bytes 1769480 | tf_op jit(solution)/shard_map/ppermute | solution.py:29
  141.4 10.3 %collective-permute-start.48 = (f32[24,768]{1,0:T(8,128)S(1)}, f32[24,768]{1,0:T(8,128)S(1)}, u32[]{:S(2)}, u32[]{:S(2)}) collective-permute-start(f32[24,768]{1,0:T(8,128)S(1)} %add.69), channel_id=1, source_target_pairs={{0,16},{4,20},{8,24},{12,28},{16,0},{20,4},{24,8},{28,12},{1,17},{... | collective-permute-start | bytes 221192 | tf_op jit(solution)/shard_map/ppermute | solution.py:29
  143.3 12.3 %collective-permute-start.52 = (bf16[128,1024]{1,0:T(8,128)(2,1)S(1)}, bf16[128,1024]{1,0:T(8,128)(2,1)S(1)}, u32[]{:S(2)}, u32[]{:S(2)}) collective-permute-start(bf16[128,1024]{1,0:T(8,128)(2,1)S(1)} %get-tuple-element.219.refs_3_), channel_id=1, source_target_pairs={{0,8},{4,12},{8,0},{12,4},{16,24},{20,28},{24,16},{28,20},{1,9},{5... | collective-permute-start | bytes 786440 | tf_op jit(solution)/shard_map/ppermute | solution.py:29
  151.9 10.0 %collective-permute-start.55 = (bf16[96,768]{1,0:T(8,128)(2,1)S(1)}, bf16[96,768]{1,0:T(8,128)(2,1)S(1)}, u32[]{:S(2)}, u32[]{:S(2)}) collective-permute-start(bf16[96,768]{1,0:T(8,128)(2,1)S(1)} %get-tuple-element.225), channel_id=1, source_target_pairs={{0,16},{4,20},{8,24},{12,28},{16,0},{20,4},{24,8},{28,12},{1,17},{... | collective-permute-start | bytes 442376 | tf_op jit(solution)/shard_map/ppermute | solution.py:29
  156.2 12.3 %collective-permute-start.53 = (bf16[192,768]{1,0:T(8,128)(2,1)S(1)}, bf16[192,768]{1,0:T(8,128)(2,1)S(1)}, u32[]{:S(2)}, u32[]{:S(2)}) collective-permute-start(bf16[192,768]{1,0:T(8,128)(2,1)S(1)} %get-tuple-element.222), channel_id=1, source_target_pairs={{0,4},{4,0},{8,12},{12,8},{16,20},{20,16},{24,28},{28,24},{1,5},{5... | collective-permute-start | bytes 884744 | tf_op jit(solution)/shard_map/ppermute | solution.py:29
  162.2 18.7 %collective-permute-start.58 = (bf16[96,1536]{1,0:T(8,128)(2,1)S(1)}, bf16[96,1536]{1,0:T(8,128)(2,1)S(1)}, u32[]{:S(2)}, u32[]{:S(2)}) collective-permute-start(bf16[96,1536]{1,0:T(8,128)(2,1)S(1)} %get-tuple-element.227), channel_id=1, source_target_pairs={{0,16},{4,20},{8,24},{12,28},{16,0},{20,4},{24,8},{28,12},{1,17},{... | collective-permute-start | bytes 884744 | tf_op jit(solution)/shard_map/ppermute | solution.py:29
  168.7 15.3 %collective-permute-start.57 = (bf16[96,768]{1,0:T(8,128)(2,1)S(1)}, bf16[96,768]{1,0:T(8,128)(2,1)S(1)}, u32[]{:S(2)}, u32[]{:S(2)}) collective-permute-start(bf16[96,768]{1,0:T(8,128)(2,1)S(1)} %get-tuple-element.231), channel_id=1, source_target_pairs={{0,16},{4,20},{8,24},{12,28},{16,0},{20,4},{24,8},{28,12},{1,17},{... | collective-permute-start | bytes 442376 | tf_op jit(solution)/shard_map/ppermute | solution.py:29
  170.5 11.5 %collective-permute-start.59 = (f32[24,768]{1,0:T(8,128)S(1)}, f32[24,768]{1,0:T(8,128)S(1)}, u32[]{:S(2)}, u32[]{:S(2)}) collective-permute-start(f32[24,768]{1,0:T(8,128)S(1)} %add.71.total_ref), channel_id=1, source_target_pairs={{0,8},{4,12},{8,0},{12,4},{16,24},{20,28},{24,16},{28,20},{1,9},{5... | collective-permute-start | bytes 221192 | tf_op jit(solution)/shard_map/ppermute | solution.py:29
  (47 other events, 242.7 us)
